TPU v7x, 32 devices: a whole 2x2x4 slice. The times are simulated.
32 devices in a mesh: group: 4 (over z), expert: 8 (over y, x, core).
Axes of the slice: x: 2, y: 2, z: 4, core: 2. Of those that a mesh axis runs over, the one named last changes fastest.
Arguments:
- tokens: bfloat16 [16384, 768], P(('group', 'expert')), may hold values from -6 to 6
- gain_first: float32 [768], replicated, may hold values from 0.5 to 1.5
- w_qkv: bfloat16 [768, 2304], replicated, may hold values from -0.21875 to 0.21875
- w_proj: bfloat16 [768, 768], replicated, may hold values from -1.25 to 1.25
- bias_table: float32 [32, 12], replicated, may hold values from -4 to 4
- gain_second: float32 [768], replicated, may hold values from 0.5 to 1.5
- w_router: bfloat16 [768, 8], replicated, may hold values from -0.109375 to 0.109375
- w_in: bfloat16 [8, 768, 3072], P('expert'), may hold values from -0.21875 to 0.21875
- w_out: bfloat16 [8, 3072, 768], P('expert'), may hold values from -0.21875 to 0.21875
- routes: int32 [16384, 2], P(('group', 'expert')), may hold values from 0 to 7, all different within a row; in each aligned block of 512 rows (0 to 511, 512 to 1023, ...) at most 256 rows name the same one
- priority: int32 [32, 512], P(('group', 'expert')), may hold values from 0 to 511, each once within a row
- span_start: int32 [32], P(('group', 'expert')), may hold values from 0 to 256
- cotangent: bfloat16 [16384, 768], P(('group', 'expert')), may hold values from -6 to 6
Outputs:
- block_out: bfloat16 [16384, 768], P(('group', 'expert'))
- grad_tokens: bfloat16 [16384, 768], P(('group', 'expert'))
- grad_gain_first: float32 [768], P('expert')
- grad_qkv: float32 [768, 2304], P('expert')
- grad_proj: float32 [768, 768], P('expert')
- grad_table: float32 [32, 12], P('expert')
- grad_gain_second: float32 [768], P('expert')
- grad_router: float32 [768, 8], P('expert')
- grad_in: float32 [8, 768, 3072], P('expert', 'group')
- grad_out: float32 [8, 3072, 768], P('expert', 'group')
Inputs may be any that keep to these rules, and one draw needn't show every extreme that they name: `routes`: each token names two different experts; among the 512 rows of one device no expert is named by more than 256 rows. `priority`: each row is a permutation of the ranks of one sequence's tokens.
All inputs are finite; a program needn't handle non-finite values.
Results may differ from a plain program's by a relative error of at most 0.02.
Values may be sent and summed in bfloat16 or wider, within the bound.
A program may use at most 192 MiB of HBM per device.

v0:
```python
import math

import jax
import jax.numpy as jnp
import numpy as np
from jax import lax
from jax.sharding import PartitionSpec as P

PIC = 256


def bucket_table(seq_len, buckets):
    half_count = buckets // 2
    exact_count = half_count // 2
    offsets = np.arange(-(seq_len - 1), seq_len)
    upper_half = (offsets > 0).astype(np.int64) * half_count
    distance = np.abs(offsets)
    scaled = (
        np.log(np.maximum(distance, 1) / float(exact_count))
        / np.log(128.0 / exact_count)
        * (half_count - exact_count)
    )
    larger = np.minimum(
        exact_count + np.floor(np.maximum(scaled, 0.0)).astype(np.int64), half_count - 1
    )
    bucket = upper_half + np.where(distance < exact_count, distance, larger)
    places = np.arange(seq_len)
    return bucket[places[None, :] - places[:, None] + seq_len - 1].astype(np.int32)


def allowed_pairs(seq_len, span_begin, span_len):
    places = jnp.arange(seq_len, dtype=jnp.int32)
    causal = places[None, :] <= places[:, None]
    inside = (places >= span_begin) & (places < span_begin + span_len)
    return causal | inside[:, None] & inside[None, :]


def rms_norm(values, norm_gain):
    return values * lax.rsqrt(jnp.mean(values * values, axis=-1, keepdims=True) + 1e-06) * norm_gain


def gate_values(logits, routes, experts):
    probabilities = jax.nn.softmax(logits, axis=-1)
    chosen = (routes[..., None] == jnp.arange(experts, dtype=jnp.int32)).astype(jnp.float32)
    picked = jnp.sum(probabilities[:, None, :] * chosen, axis=-1)
    return picked / jnp.sum(picked, axis=1, keepdims=True)


def local_ranks(choice_hits, priority):
    token_count = priority.shape[0]
    token_order = (
        jnp.zeros((token_count,), jnp.int32)
        .at[priority]
        .set(jnp.arange(token_count, dtype=jnp.int32))
    )
    ordered = choice_hits[token_order]
    running = jnp.cumsum(ordered, axis=0) - ordered
    return jnp.sum(running[priority] * choice_hits, axis=-1)


def contract_rows(left, right):
    return lax.dot_general(
        left, right, (((0,), (0,)), ((), ())), preferred_element_type=jnp.float32
    )


def on_device(
    tokens,
    gain_first,
    w_qkv,
    w_proj,
    bias_table,
    gain_second,
    w_router,
    w_in,
    w_out,
    routes,
    priority,
    span_start,
    cotangent,
):
    seq_len, model_width = tokens.shape
    buckets, head_count = bias_table.shape
    head_dim = model_width // head_count
    experts = w_router.shape[1]
    slot_count = 4 * seq_len // experts
    capacity = 5 * seq_len // 2
    score_scale = 1.0 / math.sqrt(head_dim)
    highest = lax.Precision.HIGHEST
    lowtype = jnp.bfloat16
    fulltype = jnp.float32
    tokens_f = tokens.astype(fulltype)
    normed_one = rms_norm(tokens_f, gain_first).astype(lowtype)
    qkv_rows = jnp.dot(normed_one, w_qkv, preferred_element_type=fulltype).astype(lowtype)
    qkv_rows = qkv_rows.reshape(seq_len, 3, head_count, head_dim)
    queries, key_rows, value_rows = (qkv_rows[:, 0], qkv_rows[:, 1], qkv_rows[:, 2])
    bucket_index = jnp.asarray(bucket_table(seq_len, buckets))
    onehot_table = (bucket_index[:, :, None] == jnp.arange(buckets, dtype=jnp.int32)).astype(
        fulltype
    )
    rel_bias = jnp.einsum("qkb,bh->hqk", onehot_table, bias_table, precision=highest)
    allowed = allowed_pairs(seq_len, span_start[0], PIC)

    def masked_scores():
        raw_scores = (
            jnp.einsum("qhc,khc->hqk", queries, key_rows, preferred_element_type=fulltype)
            * score_scale
            + rel_bias
        )
        return jnp.where(allowed[None], raw_scores, -1e30)

    scores = masked_scores()
    log_total = jax.nn.logsumexp(scores, axis=-1)
    attn_probs = jnp.exp(scores - log_total[..., None]).astype(lowtype)
    mixed_heads = jnp.einsum(
        "hqk,khc->qhc", attn_probs, value_rows, preferred_element_type=fulltype
    )
    mixed_heads = mixed_heads.astype(lowtype).reshape(seq_len, model_width)
    hidden = tokens_f + jnp.dot(mixed_heads, w_proj, preferred_element_type=fulltype)
    normed_two = rms_norm(hidden, gain_second).astype(lowtype)
    logits = jnp.dot(normed_two, w_router, preferred_element_type=fulltype)
    gate_weights = gate_values(logits, routes, experts)
    choice_hits = (routes[..., None] == jnp.arange(experts, dtype=jnp.int32)).astype(jnp.int32)
    counts = jnp.sum(choice_hits, axis=0)
    every_count = lax.all_gather(counts[None], "expert", axis=0, tiled=True)
    pair_ranks = local_ranks(choice_hits, priority[0])
    second_shift = jnp.sum(choice_hits[:, 1] * counts[0], axis=-1)
    slot_index = pair_ranks + jnp.stack([jnp.zeros_like(second_shift), second_shift], axis=-1)
    flat_slot = (routes * slot_count + slot_index).reshape(-1)
    own_expert = (jnp.arange(experts, dtype=jnp.int32) == lax.axis_index("expert")).astype(
        jnp.int32
    )
    own_counts = jnp.sum(every_count * own_expert, axis=-1)
    first_rows, second_rows = (own_counts[:, 0], own_counts[:, 1])
    first_before = jnp.cumsum(first_rows) - first_rows
    second_before = jnp.cumsum(second_rows) - second_rows
    first_total = jnp.sum(first_rows)
    column = jnp.arange(slot_count, dtype=jnp.int32)[None, :]
    position = jnp.where(
        column < first_rows[:, None],
        first_before[:, None] + column,
        first_total + second_before[:, None] + column - first_rows[:, None],
    )
    usable = (column < (first_rows + second_rows)[:, None]) & (position < capacity)
    destination = jnp.where(usable, position, capacity).reshape(-1)

    def pack_pairs(pair_rows):
        packed = jnp.zeros((experts * slot_count, model_width), lowtype)
        packed = packed.at[flat_slot].set(pair_rows.reshape(-1, model_width))
        return packed.reshape(experts, slot_count, model_width)

    def compact_rows(arrived):
        gathered_rows = jnp.zeros((capacity + 1, model_width), lowtype)
        return gathered_rows.at[destination].add(arrived.reshape(-1, model_width))[:capacity]

    def spread_rows(expert_out):
        padded = jnp.concatenate([expert_out, jnp.zeros((1, model_width), lowtype)], axis=0)
        return padded[destination].reshape(-1, slot_count, model_width)

    def unpack_pairs(received):
        return (
            received.reshape(-1, model_width)[flat_slot]
            .reshape(seq_len, 2, model_width)
            .astype(fulltype)
        )

    pair_rows = jnp.broadcast_to(normed_two[:, None, :], (seq_len, 2, model_width))
    arrived = lax.all_to_all(
        pack_pairs(pair_rows), "expert", split_axis=0, concat_axis=0, tiled=True
    )
    expert_rows = compact_rows(arrived)
    inner_pre = jnp.dot(expert_rows, w_in[0], preferred_element_type=fulltype)
    active = jax.nn.gelu(inner_pre).astype(lowtype)
    result = jnp.dot(active, w_out[0], preferred_element_type=fulltype).astype(lowtype)
    returned = unpack_pairs(
        lax.all_to_all(spread_rows(result), "expert", split_axis=0, concat_axis=0, tiled=True)
    )
    block_out = hidden + jnp.sum(gate_weights[..., None] * returned, axis=1)
    upstream = cotangent.astype(fulltype)
    gate_grad = jnp.sum(upstream[:, None, :] * returned, axis=-1)
    result_grad = (gate_weights[..., None] * upstream[:, None, :]).astype(lowtype)
    result_rows = compact_rows(
        lax.all_to_all(pack_pairs(result_grad), "expert", split_axis=0, concat_axis=0, tiled=True)
    )
    grad_outer = contract_rows(active, result_rows)
    hidden_pre_grad = jnp.dot(result_rows, w_out[0].T, preferred_element_type=fulltype)
    inner_grad = jax.vjp(jax.nn.gelu, inner_pre)[1](hidden_pre_grad)[0].astype(lowtype)
    grad_inner = contract_rows(expert_rows, inner_grad)
    rows_grad = jnp.dot(inner_grad, w_in[0].T, preferred_element_type=fulltype).astype(lowtype)
    pair_grad = unpack_pairs(
        lax.all_to_all(spread_rows(rows_grad), "expert", split_axis=0, concat_axis=0, tiled=True)
    )
    logit_grad = jax.vjp(lambda values: gate_values(values, routes, experts), logits)[1](gate_grad)[
        0
    ].astype(lowtype)
    grad_router = contract_rows(normed_two, logit_grad)
    normed_grad = jnp.sum(pair_grad, axis=1) + jnp.dot(
        logit_grad, w_router.T, preferred_element_type=fulltype
    )
    second_back = jax.vjp(rms_norm, hidden, gain_second)[1](normed_grad)
    hidden_grad = upstream + second_back[0]
    branch_grad = hidden_grad.astype(lowtype)
    grad_proj = contract_rows(mixed_heads, branch_grad)
    mixed_grad = jnp.dot(branch_grad, w_proj.T, preferred_element_type=fulltype).astype(lowtype)
    mixed_grad = mixed_grad.reshape(seq_len, head_count, head_dim)
    scores = masked_scores()
    probs_full = jnp.exp(scores - log_total[..., None])
    probs_low = probs_full.astype(lowtype)
    prob_grad = jnp.einsum("qhc,khc->hqk", mixed_grad, value_rows, preferred_element_type=fulltype)
    value_grad = jnp.einsum("hqk,qhc->khc", probs_low, mixed_grad, preferred_element_type=fulltype)
    row_dot = jnp.sum(probs_full * prob_grad, axis=-1, keepdims=True)
    score_grad = (probs_full * (prob_grad - row_dot)).astype(lowtype)
    query_grad = (
        jnp.einsum("hqk,khc->qhc", score_grad, key_rows, preferred_element_type=fulltype)
        * score_scale
    )
    key_grad = (
        jnp.einsum("hqk,qhc->khc", score_grad, queries, preferred_element_type=fulltype)
        * score_scale
    )
    grad_table = jnp.einsum(
        "hqk,qkb->bh", score_grad.astype(fulltype), onehot_table, precision=highest
    )
    qkv_grad = (
        jnp.stack([query_grad, key_grad, value_grad], axis=1)
        .astype(lowtype)
        .reshape(seq_len, 3 * model_width)
    )
    grad_qkv = contract_rows(normed_one, qkv_grad)
    normed_one_grad = jnp.dot(qkv_grad, w_qkv.T, preferred_element_type=fulltype)
    first_back = jax.vjp(rms_norm, tokens_f, gain_first)[1](normed_one_grad)
    grad_tokens = (hidden_grad + first_back[0]).astype(lowtype)
    dense_grads = (first_back[1], grad_qkv, grad_proj, grad_table, second_back[1], grad_router)
    shares = (
        lax.psum_scatter(
            dense_grads[0].astype(jnp.bfloat16), "expert", scatter_dimension=0, tiled=True
        ).astype(jnp.float32),
        lax.psum_scatter(
            dense_grads[1].astype(jnp.bfloat16), "expert", scatter_dimension=0, tiled=True
        ).astype(jnp.float32),
        lax.psum_scatter(
            dense_grads[2].astype(jnp.bfloat16), "expert", scatter_dimension=0, tiled=True
        ).astype(jnp.float32),
        lax.psum_scatter(
            dense_grads[3].astype(jnp.bfloat16), "expert", scatter_dimension=0, tiled=True
        ).astype(jnp.float32),
        lax.psum_scatter(
            dense_grads[4].astype(jnp.bfloat16), "expert", scatter_dimension=0, tiled=True
        ).astype(jnp.float32),
        lax.psum_scatter(
            dense_grads[5].astype(jnp.bfloat16), "expert", scatter_dimension=0, tiled=True
        ).astype(jnp.float32),
    )
    totals = (
        lax.psum(shares[0].astype(jnp.bfloat16), "group").astype(jnp.float32),
        lax.psum(shares[1].astype(jnp.bfloat16), "group").astype(jnp.float32),
        lax.psum(shares[2].astype(jnp.bfloat16), "group").astype(jnp.float32),
        lax.psum(shares[3].astype(jnp.bfloat16), "group").astype(jnp.float32),
        lax.psum(shares[4].astype(jnp.bfloat16), "group").astype(jnp.float32),
        lax.psum(shares[5].astype(jnp.bfloat16), "group").astype(jnp.float32),
    )
    grad_in, grad_out = (
        lax.psum_scatter(
            grad_inner[None].astype(jnp.bfloat16), "group", scatter_dimension=1, tiled=True
        ).astype(jnp.float32),
        lax.psum_scatter(
            grad_outer[None].astype(jnp.bfloat16), "group", scatter_dimension=1, tiled=True
        ).astype(jnp.float32),
    )
    return (
        block_out.astype(lowtype),
        grad_tokens,
        totals[0],
        totals[1],
        totals[2],
        totals[3],
        totals[4],
        totals[5],
        grad_in,
        grad_out,
    )


def solution(mesh):
    return jax.shard_map(
        on_device,
        mesh=mesh,
        in_specs=(
            P(("group", "expert"), None),
            P(),
            P(),
            P(),
            P(),
            P(),
            P(),
            P("expert", None, None),
            P("expert", None, None),
            P(("group", "expert"), None),
            P(("group", "expert"), None),
            P(("group", "expert")),
            P(("group", "expert"), None),
        ),
        out_specs=(
            P(("group", "expert"), None),
            P(("group", "expert"), None),
            P("expert"),
            P("expert", None),
            P("expert", None),
            P("expert", None),
            P("expert"),
            P("expert", None),
            P("expert", "group", None),
            P("expert", "group", None),
        ),
        check_vma=False,
    )
```

profile of v0, /device:TPU:8, one launch (start us, length us, event | category | flops | bytes accessed | tf_op | source)
XLA Modules:
  0.0 789.1 jit_solution(4465253492348536120)
XLA Ops:
  12.0 2.4 scatter_custom_fusion
  16.9 2.5 fusion.74
  21.2 3.3 gather_fusion
  26.3 5.1 reduce-window.16
  36.9 2.3 bitcast_subtract_fusion
  39.2 3.4 gather_fusion.1
  42.6 11.5 %select_reduce_fusion.3 = (s32[512,2]{1,0:T(8,128)}, s32[2,8]{1,0:T(2,128)S(1)}) fusion(s32[512,2,8]{2,1,0:T(2,128)} %gather_fusion.1, s32[512,2]{1,0:T(8,128)} %copy.116), kind=kLoop, calls=%fused_computation.112 | loop fusion | flops 39920 | bytes 41024 | tf_op jit(solution)/shard_map/reduce_sum | solution.py:58
  58.9 4.6 convolution_convert_fusion.3
  63.5 4.3 copy.113
  67.8 3.6 mul.330
  71.4 5.3 mul.331
  76.7 15.2 %fusion.1 = f32[512,512,12]{0,2,1:T(8,128)} fusion(s32[512,512]{0,1:T(8,128)} %constant.21.clone, f32[32,12]{0,1:T(8,128)S(1)} %copy-done.40), kind=kOutput, calls=%fused_computation.13 | convolution fusion | flops 1216348160 | bytes 13633024 | tf_op jit(solution)/shard_map/qkb,bh->hqk/dot_general | solution.py:101
  91.9 15.1 %fusion.88 = (f32[12,512]{1,0:T(8,128)S(1)}, f32[12,512,512]{1,2,0:T(8,128)S(1)}) fusion(f32[512,512,12]{0,2,1:T(8,128)} %fusion.1, bf16[512,3,12,64]{0,3,2,1:T(8,128)(2,1)S(1)} %bitcast.149, pred[512,512]{0,1:T(8,128)(4,1)S(1)} %copy-done.22), kind=kOutput, calls=%fused_computation.169 | convolution fusion | flops 415229952 | bytes 27025408 | tf_op jit(solution)/shard_map/qhc,khc->hqk/dot_general | solution.py:106
  108.9 2.7 copy-done.1
  111.7 3.4 fusion.51
  122.0 8.9 %select_reduce_fusion = (f32[512]{0:T(512)S(1)}, f32[512,2]{1,0:T(8,128)S(1)}) fusion(f32[512,8]{1,0:T(8,128)} %copy.117, s32[512,2]{1,0:T(8,128)} %copy.116), kind=kLoop, calls=%fused_computation.108 | loop fusion | flops 31232 | bytes 26624 | tf_op jit(solution)/shard_map/reduce_sum | solution.py:46
  134.2 8.3 %scatter_custom_fusion.3 = bf16[2048,768]{1,0:T(8,128)(2,1)} fusion(s32[1024]{0:T(1024)} %bitcast.174, f32[1024,768]{1,0:T(8,128)} %mul.331, f32[1024]{0:T(1024)} %div.88, bf16[]{:T(256)} %constant.29.clone.1), kind=kCustom, calls=%fused_computation.75 | custom fusion | flops 1572864 | bytes 6296064 | tf_op jit(solution)/shard_map/scatter | solution.py:149
  142.5 4.8 all-to-all-start.2
  147.4 3.1 broadcast_in_dim.41
  150.4 4.7 reshape.505
  155.1 7.9 %scatter_custom_fusion.1 = bf16[2048,768]{1,0:T(8,128)(2,1)} fusion(s32[1024]{0:T(1024)} %bitcast.175, bf16[1024,768]{1,0:T(8,128)(2,1)} %reshape.505, bf16[]{:T(256)} %constant.29.clone.1), kind=kCustom, calls=%fused_computation.83 | custom fusion | bytes 3146240 | tf_op jit(solution)/shard_map/scatter | solution.py:149
  163.1 22.2 %all-to-all-done.2 = bf16[8,256,768]{2,1,0:T(8,128)(2,1)} async-done(((bf16[8,256,768]{2,1,0:T(8,128)(2,1)}), bf16[8,256,768]{2,1,0:T(8,128)(2,1)}, u32[]{:S(2)}, u32[]{:S(2)}) %all-to-all-start.2) | async-done | bytes 3145760 | tf_op jit(solution)/shard_map/all_to_all | solution.py:183
  185.3 4.5 all-to-all-start
  190.4 40.2 %all-gather.1 = s32[8,2,8]{2,1,0:T(2,128)S(1)} all-gather(s32[1,2,8]{2,1,0:T(2,128)} %bitcast.180), channel_id=2, replica_groups=mesh['group'=4,'expert'=8] {'expert'}, dimensions={0}, use_global_device_ids=true | all-gather | bytes 576 | tf_op jit(solution)/shard_map/all_gather | solution.py:125
  232.7 2.1 add_reduce_fusion.1
  241.2 16.9 %scatter_custom_fusion.4 = bf16[1281,768]{1,0:T(8,128)(2,1)} fusion(s32[2048]{0:T(1024)} %bitcast.169, bf16[2048,768]{1,0:T(8,128)(2,1)} %bitcast.29, bf16[]{:T(256)} %constant.29.clone.1), kind=kCustom, calls=%fused_computation.100 | custom fusion | flops 1572864 | bytes 1968128 | tf_op jit(solution)/shard_map/scatter-add | solution.py:154
  258.1 17.1 %scatter_custom_fusion.2 = bf16[1281,768]{1,0:T(8,128)(2,1)} fusion(s32[2048]{0:T(1024)} %bitcast.170, bf16[2048,768]{1,0:T(8,128)(2,1)} %bitcast.23, bf16[]{:T(256)} %constant.29.clone.1), kind=kCustom, calls=%fused_computation.102 | custom fusion | flops 1572864 | bytes 1968128 | tf_op jit(solution)/shard_map/scatter-add | solution.py:154
  275.3 8.7 %fusion.19 = f32[1280,3072]{1,0:T(8,128)S(1)} fusion(bf16[1,768,3072]{2,1,0:T(8,128)(2,1)} %param.21, bf16[1281,768]{1,0:T(8,128)(2,1)} %scatter_custom_fusion.2), kind=kOutput, calls=%fused_computation.42 | convolution fusion | flops 6039797760 | bytes 22413312 | tf_op jit(solution)/shard_map/dot_general | solution.py:172
  284.0 15.2 %fusion.26 = bf16[1280,768]{1,0:T(8,128)(2,1)S(1)} fusion(bf16[1,3072,768]{2,1,0:T(8,128)(2,1)} %param.22, f32[1280,3072]{1,0:T(8,128)S(1)} %fusion.19), kind=kOutput, calls=%fused_computation.48 | convolution fusion | flops 6076170240 | bytes 22413312 | tf_op jit(solution)/shard_map/dot_general | solution.py:174
  300.6 12.5 %gather_fusion.2 = bf16[2048,768]{1,0:T(8,128)(2,1)} fusion(bf16[1281,768]{1,0:T(8,128)(2,1)} %concatenate.6, s32[2048]{0:T(1024)} %broadcast_clamp_fusion), kind=kCustom, calls=%fused_computation.2 | custom fusion | bytes 6299648 | tf_op jit(solution)/shard_map/gather | solution.py:158
  313.0 4.7 all-to-all-start.1
  317.7 18.4 %fusion.10 = bf16[1280,3072]{1,0:T(8,128)(2,1)S(1)} fusion(f32[1280,3072]{1,0:T(8,128)} %copy-done.51, bf16[1,3072,768]{2,1,0:T(8,128)(2,1)} %param.22, bf16[1281,768]{1,0:T(8,128)(2,1)} %scatter_custom_fusion.4), kind=kOutput, calls=%fused_computation.24 | convolution fusion | flops 6118440960 | bytes 30277632 | tf_op jit(solution)/shard_map/dot_general | solution.py:186
  336.2 11.5 %fusion.23 = bf16[1280,768]{1,0:T(8,128)(2,1)S(1)} fusion(bf16[1280,3072]{1,0:T(8,128)(2,1)S(1)} %fusion.10, bf16[1,768,3072]{2,1,0:T(8,128)(2,1)} %param.21), kind=kOutput, calls=%fused_computation.47 | convolution fusion | flops 6040780800 | bytes 14548992 | tf_op jit(solution)/shard_map/dot_general | solution.py:189
  349.1 12.5 %gather_fusion.4 = bf16[2048,768]{1,0:T(8,128)(2,1)} fusion(bf16[1281,768]{1,0:T(8,128)(2,1)} %concatenate.7, s32[2048]{0:T(1024)} %broadcast_clamp_fusion), kind=kCustom, calls=%fused_computation.4 | custom fusion | bytes 6299648 | tf_op jit(solution)/shard_map/gather | solution.py:158
  361.6 4.5 all-to-all-start.3
  366.1 2.4 convert_element_type.174
  372.3 8.5 %gather_fusion.3 = bf16[1024,768]{1,0:T(8,128)(2,1)} fusion(bf16[2048,768]{1,0:T(8,128)(2,1)} %bitcast.27, s32[1024]{0:T(1024)} %broadcast_clamp_fusion.1), kind=kCustom, calls=%fused_computation.3 | custom fusion | bytes 3149824 | tf_op jit(solution)/shard_map/gather | solution.py:162
  380.8 4.9 reshape.443
  385.7 9.6 %multiply_reduce_fusion.1 = (f32[512,2]{1,0:T(8,128)S(1)}, f32[512,768]{1,0:T(8,128)}) fusion(f32[512,2,768]{2,1,0:T(2,128)} %reshape.443, f32[512,768]{1,0:T(8,128)} %convert_element_type.174, f32[512,2]{1,0:T(8,128)} %broadcast_divide_fusion), kind=kLoop, calls=%fused_computation.49 | loop fusion | flops 2751488 | bytes 6299648 | tf_op jit(solution)/shard_map/reduce_sum | solution.py:180
  395.8 3.6 select_reduce_fusion.2
  404.0 8.1 %gather_fusion.5 = bf16[1024,768]{1,0:T(8,128)(2,1)} fusion(bf16[2048,768]{1,0:T(8,128)(2,1)} %bitcast.31, s32[1024]{0:T(1024)} %broadcast_clamp_fusion.1), kind=kCustom, calls=%fused_computation.5 | custom fusion | bytes 3149824 | tf_op jit(solution)/shard_map/gather | solution.py:162
  412.1 5.0 reshape.444
  417.1 6.8 reduce_sum.212
  423.9 3.3 multiply_reduce_fusion.3
  431.6 3.4 convolution_convert_fusion.5
  435.1 2.3 copy.128
  437.4 12.5 %multiply_reduce_fusion = (f32[12,512]{1,0:T(8,128)S(1)}, f32[12,512,512]{1,2,0:T(8,128)}) fusion(f32[12,512,512]{1,2,0:T(8,128)} %copy-done.1, f32[12,512]{1,0:T(8,128)} %copy-done.23, bf16[512,12,64]{0,2,1:T(8,128)(2,1)} %bitcast.156, bf16[512,3,12,64]{0,3,2,1:T(8,128)(2,1)} %bitcast.148), kind=kOutput, calls=%fused_computation.29 | convolution fusion | flops 412084224 | bytes 26796032 | tf_op jit(solution)/shard_map/qhc,khc->hqk/dot_general | solution.py:209
  450.0 7.2 multiply_convert_fusion.1
  457.2 2.0 fusion.61
  461.0 2.0 fusion.57
  464.7 4.1 convolution_convert_fusion.2
  472.7 52.0 %reduce-scatter.8.cloned.1.call-done = bf16[96,2304]{1,0:T(8,128)(2,1)} async-done(((bf16[768,2304]{1,0:T(8,128)(2,1)}), bf16[96,2304]{1,0:T(8,128)(2,1)}) %reduce-scatter.8.cloned.1.call-update) | async-done | bytes 442384 | tf_op jit(solution)/shard_map/reduce_scatter | solution.py:238
  524.8 13.8 %fusion.22 = bf16[1,3072,768]{2,1,0:T(8,128)(2,1)} fusion(bf16[1281,768]{1,0:T(8,128)(2,1)} %scatter_custom_fusion.4, f32[1280,3072]{1,0:T(8,128)} %copy-done.51), kind=kOutput, calls=%fused_computation.45 | convolution fusion | flops 6077546496 | bytes 22413312 | tf_op jit(solution)/shard_map/dot_general | solution.py:62
  538.6 11.0 %fusion.21 = bf16[1,768,3072]{2,1,0:T(8,128)(2,1)} fusion(bf16[1280,3072]{1,0:T(8,128)(2,1)} %copy-done.50, bf16[1281,768]{1,0:T(8,128)(2,1)} %scatter_custom_fusion.2), kind=kOutput, calls=%fused_computation.44 | convolution fusion | flops 6042157056 | bytes 14548992 | tf_op jit(solution)/shard_map/dot_general | solution.py:62
  552.2 5.9 fusion.40
  558.1 9.1 %fusion.65 = bf16[32,12]{1,0:T(8,128)(2,1)} fusion(bf16[12,512,512]{1,2,0:T(8,128)(2,1)} %copy-done.2, s32[512,512]{0,1:T(8,128)S(1)} %copy-done.21), kind=kOutput, calls=%fused_computation.97 | convolution fusion | flops 209715584 | bytes 7340800 | tf_op jit(solution)/shard_map/hqk,qkb->bh/dot_general | solution.py:221
  567.2 23.3 %all-reduce.6 = (bf16[768]{0:T(1024)(128)(2,1)}, bf16[32,12]{1,0:T(8,128)(2,1)}, bf16[768]{0:T(1024)(128)(2,1)}) all-reduce(bf16[768]{0:T(1024)(128)(2,1)} %get-tuple-element.14, bf16[32,12]{1,0:T(8,128)(2,1)} %fusion.65, bf16[768]{0:T(1024)(128)(2,1)S(1)} %copy-done.39), channel_id=3, replica_groups=mesh['group'=4,'expert'=8] {'expert'}, use_global_device_ids=true, to_apply=%region_32.33.clone | all-reduce | flops 1920 | bytes 7680
  594.5 3.5 fusion.43
  598.7 10.1 %all-reduce.7 = (bf16[96]{0:T(256)(128)(2,1)}, bf16[4,12]{1,0:T(4,128)(2,1)S(1)}, bf16[96]{0:T(256)(128)(2,1)}, bf16[96,8]{0,1:T(8,128)(2,1)S(1)}) all-reduce(bf16[96]{0:T(256)(128)(2,1)} %dynamic-slice.1, bf16[4,12]{1,0:T(4,128)(2,1)S(1)} %constant_dynamic-slice_fusion, ...), channel_id=1, replica_groups=mesh['group'=4,'expert'=8] {'group'}, use_global_device_ids=true, to_apply=%region_33.34 | all-reduce | flops 1008 | bytes 4032 | tf_op jit(solution)/shard_map/psum | solution.py:255
  614.0 2.0 convert_element_type.189
  616.0 74.9 %reduce-scatter.14.cloned.1.call-done = bf16[1,768,768]{2,1,0:T(8,128)(2,1)} async-done(((bf16[1,3072,768]{2,1,0:T(8,128)(2,1)}), bf16[1,768,768]{2,1,0:T(8,128)(2,1)}) %reduce-scatter.14.cloned.1.call-update) | async-done | bytes 1179664 | tf_op jit(solution)/shard_map/reduce_scatter | solution.py:266
  690.9 2.8 convert_element_type.203
  693.8 85.1 %reduce-scatter.12.cloned.1.call-done = bf16[1,192,3072]{2,1,0:T(8,128)(2,1)} async-done(((bf16[1,768,3072]{2,1,0:T(8,128)(2,1)}), bf16[1,192,3072]{2,1,0:T(8,128)(2,1)}) %reduce-scatter.12.cloned.1.call-update) | async-done | bytes 1179664 | tf_op jit(solution)/shard_map/reduce_scatter | solution.py:263
  778.9 2.9 convert_element_type.200
  (212 shorter events, 76.0 us)
Async XLA Ops:
  7.2 51.7 %copy-start = (bf16[768,2304]{1,0:T(8,128)(2,1)S(1)}, bf16[768,2304]{1,0:T(8,128)(2,1)}, u32[]{:S(2)}) copy-start(bf16[768,2304]{1,0:T(8,128)(2,1)} %param.16) | copy-start | bytes 10616836
  9.5 0.6 copy-start.36
  19.4 0.8 copy-start.13
  21.2 35.1 %copy-start.38 = (s32[512,2]{0,1:T(2,128)S(1)}, s32[512,2]{0,1:T(2,128)}, u32[]{:S(2)}) copy-start(s32[512,2]{0,1:T(2,128)} %param.23) | copy-start | bytes 12292
  33.7 25.2 %copy-start.41 = (f32[512]{0:T(512)S(1)}, f32[512]{0:T(512)}, u32[]{:S(2)}) copy-start(f32[512]{0:T(512)} %fusion.83) | copy-start | bytes 6148
  54.1 2.2 copy-start.47
  71.4 5.3 copy-start.40
  76.7 15.2 %copy-start.3 = (bf16[512,2304]{0,1:T(8,128)(2,1)S(1)}, bf16[512,2304]{0,1:T(8,128)(2,1)}, u32[]{:S(2)}) copy-start(bf16[512,2304]{0,1:T(8,128)(2,1)} %copy.113) | copy-start | bytes 7077892
  76.7 15.2 %copy-start.22 = (pred[512,512]{0,1:T(8,128)(4,1)S(1)}, pred[512,512]{0,1:T(8,128)(4,1)}, u32[]{:S(2)}) copy-start(pred[512,512]{0,1:T(8,128)(4,1)} %fusion.68) | copy-start | bytes 786436
  107.0 4.7 copy-start.1
  111.7 3.4 copy-start.23
  111.7 3.4 copy-start.16
  111.7 3.4 copy-start.48
  115.1 2.3 copy-start.14
  115.1 2.1 copy-start.28
  115.1 3.2 copy-start.27
  116.0 0.6 copy-start.44
  116.0 1.1 copy-start.5
  116.6 2.0 copy-start.30
  117.4 0.9 copy-start.8
  118.6 0.6 copy-start.26
  130.9 0.7 copy-start.18
  130.9 0.7 copy-start.32
  142.5 42.7 %all-to-all-start.2 = ((bf16[8,256,768]{2,1,0:T(8,128)(2,1)}), bf16[8,256,768]{2,1,0:T(8,128)(2,1)}, u32[]{:S(2)}, u32[]{:S(2)}) async-start(bf16[8,256,768]{2,1,0:T(8,128)(2,1)} %bitcast.153), calls=%async_computation.2 | async-start | bytes 6291456 | tf_op jit(solution)/shard_map/all_to_all | solution.py:183
  185.3 72.9 %all-to-all-start = ((bf16[8,256,768]{2,1,0:T(8,128)(2,1)}), bf16[8,256,768]{2,1,0:T(8,128)(2,1)}, u32[]{:S(2)}, u32[]{:S(2)}) async-start(bf16[8,256,768]{2,1,0:T(8,128)(2,1)} %bitcast.152), calls=%async_computation | async-start | bytes 6291456 | tf_op jit(solution)/shard_map/all_to_all | solution.py:168
  240.0 0.6 copy-start.35
  284.0 15.2 %copy-start.51 = (f32[1280,3072]{1,0:T(8,128)}, f32[1280,3072]{1,0:T(8,128)S(1)}, u32[]{:S(2)}) copy-start(f32[1280,3072]{1,0:T(8,128)S(1)} %fusion.19) | copy-start | bytes 47185924
  313.0 48.5 %all-to-all-start.1 = ((bf16[8,256,768]{2,1,0:T(8,128)(2,1)}), bf16[8,256,768]{2,1,0:T(8,128)(2,1)}, u32[]{:S(2)}, u32[]{:S(2)}) async-start(bf16[8,256,768]{2,1,0:T(8,128)(2,1)} %bitcast.155), calls=%async_computation.1 | async-start | bytes 6291456 | tf_op jit(solution)/shard_map/all_to_all | solution.py:176
  336.2 11.5 %copy-start.50 = (bf16[1280,3072]{1,0:T(8,128)(2,1)}, bf16[1280,3072]{1,0:T(8,128)(2,1)S(1)}, u32[]{:S(2)}) copy-start(bf16[1280,3072]{1,0:T(8,128)(2,1)S(1)} %fusion.10) | copy-start | bytes 23592964
  361.6 42.4 %all-to-all-start.3 = ((bf16[8,256,768]{2,1,0:T(8,128)(2,1)}), bf16[8,256,768]{2,1,0:T(8,128)(2,1)}, u32[]{:S(2)}, u32[]{:S(2)}) async-start(bf16[8,256,768]{2,1,0:T(8,128)(2,1)} %bitcast.154), calls=%async_computation.3 | async-start | bytes 6291456 | tf_op jit(solution)/shard_map/all_to_all | solution.py:191
  366.1 106.6 %reduce-scatter.10.cloned.1.call-start = ((), (), s32[]{:S(2)}) async-start(), calls=%async_computation.10 | async-start | bytes 1327104 | tf_op jit(solution)/shard_map/reduce_scatter | solution.py:241
  385.7 9.6 %copy-start.19 = (f32[512,2]{1,0:T(8,128)S(1)}, f32[512,2]{1,0:T(8,128)}, u32[]{:S(2)}) copy-start(f32[512,2]{1,0:T(8,128)} %copy-done.18) | copy-start | bytes 12292
  385.7 9.6 %copy-start.43 = (f32[512]{0:T(512)S(1)}, f32[512]{0:T(512)}, u32[]{:S(2)}) copy-start(f32[512]{0:T(512)} %multiply_divide_fusion.1) | copy-start | bytes 6148
  385.7 9.8 %copy-start.33 = (f32[512]{0:T(512)S(1)}, f32[512]{0:T(512)}, u32[]{:S(2)}) copy-start(f32[512]{0:T(512)} %copy-done.32) | copy-start | bytes 6148
  385.7 10.0 %copy-start.11 = (s32[512,2]{1,0:T(8,128)S(1)}, s32[512,2]{1,0:T(8,128)}, u32[]{:S(2)}) copy-start(s32[512,2]{1,0:T(8,128)} %copy.116) | copy-start | bytes 12292
  417.1 6.8 copy-start.25
  417.1 6.8 copy-start.29
  417.1 6.8 copy-start.31
  423.9 3.3 copy-start.45
  423.9 3.4 copy-start.6
  423.9 3.4 copy-start.10
  423.9 3.3 copy-start.12
  427.3 2.6 copy-start.15
  428.6 1.2 copy-start.7
  435.1 89.6 %reduce-scatter.8.cloned.1.call-start = ((), (), s32[]{:S(2)}) async-start(), calls=%async_computation.9 | async-start | bytes 3981312 | tf_op jit(solution)/shard_map/reduce_scatter | solution.py:238
  437.4 12.5 %slice-start = ((s8[12582912]{0:T(1024)(128)(4,1)}), s8[4194304]{0:T(1024)(128)(4,1)S(1)}, s32[]{:S(2)}) async-start(s8[12582912]{0:T(1024)(128)(4,1)} %bitcast.145), calls=%async_computation.15 | async-start | bytes 8388608
  437.4 12.5 %slice-start.1 = ((s8[12582912]{0:T(1024)(128)(4,1)}), s8[4194304]{0:T(1024)(128)(4,1)S(1)}, s32[]{:S(2)}) async-start(s8[12582912]{0:T(1024)(128)(4,1)} %bitcast.145), calls=%async_computation.16 | async-start | bytes 8388608
  437.4 12.5 %slice-start.2 = ((s8[12582912]{0:T(1024)(128)(4,1)}), s8[4194304]{0:T(1024)(128)(4,1)S(1)}, s32[]{:S(2)}) async-start(s8[12582912]{0:T(1024)(128)(4,1)} %bitcast.145), calls=%async_computation.17 | async-start | bytes 8388608
  437.4 12.5 %copy-start.24 = (f32[12,512]{1,0:T(8,128)S(1)}, f32[12,512]{1,0:T(8,128)}, u32[]{:S(2)}) copy-start(f32[12,512]{1,0:T(8,128)} %copy-done.23) | copy-start | bytes 73732
  450.0 7.2 copy-start.4
  457.2 2.6 copy-start.2
  459.8 1.1 copy-start.9
  463.0 1.7 copy-start.17
  463.0 1.7 copy-start.42
  463.0 1.7 copy-start.46
  463.3 1.4 copy-start.20
  468.8 129.1 %reduce-scatter.16.cloned.1.call-start = ((), (), s32[]{:S(2)}) async-start(), calls=%async_computation.13 | async-start | bytes 221184
  472.4 139.9 %all-reduce.11.cloned.1.call-start = ((), (), s32[]{:S(2)}) async-start(), calls=%async_computation.14 | async-start | bytes 1179648 | tf_op jit(solution)/shard_map/psum | solution.py:256
  524.7 166.2 %reduce-scatter.14.cloned.1.call-start = ((), (), s32[]{:S(2)}) async-start(), calls=%async_computation.12 | async-start | bytes 5898240 | tf_op jit(solution)/shard_map/reduce_scatter | solution.py:266
  538.6 240.3 %reduce-scatter.12.cloned.1.call-start = ((), (), s32[]{:S(2)}) async-start(), calls=%async_computation.11 | async-start | bytes 5898240 | tf_op jit(solution)/shard_map/reduce_scatter | solution.py:263
  549.7 0.7 copy-start.49
  552.2 5.9 copy-start.21
  558.1 9.1 %copy-start.39 = (bf16[768]{0:T(1024)(128)(2,1)S(1)}, bf16[768]{0:T(1024)(128)(2,1)}, u32[]{:S(2)}) copy-start(bf16[768]{0:T(1024)(128)(2,1)} %get-tuple-element.10) | copy-start | bytes 4612
  558.1 35.7 %copy-start.37 = (f32[512]{0:T(512)S(1)}, f32[512]{0:T(512)}, u32[]{:S(2)}) copy-start(f32[512]{0:T(512)} %copy-done.36) | copy-start | bytes 6148
  (1 other events, 0.6 us)
Sparse Core Ops, SparseCore 0:
  435.2 37.4 reduce-scatter.9
  476.6 48.0 reduce-scatter.7
  528.6 33.4 reduce-scatter.15
  564.4 39.0 all-reduce.10
  605.7 85.2 reduce-scatter.13
  693.1 85.7 reduce-scatter.11
where the time goes:
time: 803 us; the launch traced here: 789 us
  waiting for transfers between devices  236 us (29%)
  matrix products  165 us (21%)
  other arithmetic  147 us (18%)
  local copies, waits for them, and re-layouts  132 us (16%)
  blocking collectives  73.6 us (9%)
  starting transfers between devices  18.7 us (2%)
  between operations  17.4 us (2%)
    reduce_scatter x1, waiting for transfers between devices, on_device(): lax.psum_scatter(grad_inner[None].astype(jnp.bfloat16), 'group', scatter_...  85.1 us
    reduce_scatter x1, waiting for transfers between devices, on_device(): lax.psum_scatter(grad_outer[None].astype(jnp.bfloat16), 'group', scatter_...  74.9 us
    reduce_scatter x1, waiting for transfers between devices, on_device(): lax.psum_scatter(dense_grads[1].astype(jnp.bfloat16), 'expert', scatter_d...  52 us
    all_gather x1, blocking collectives, on_device(): every_count = lax.all_gather(counts[None], 'expert', axis=0, tiled=True)  40.2 us
    scatter-add x2, other arithmetic, compact_rows(): gathered_rows.at[destination].add(arrived.reshape(-1, model_width))  34.1 us
    dot_general x5, matrix products, contract_rows(): lax.dot_general(left, right, (((0,), (0,)), ((), ())), preferred_element_...  32.6 us
    gather x2, local copies, waits for them, and re-layouts, spread_rows(): return padded[destination].reshape(-1, slot_count, model_width)  24.9 us
    unnamed x1, blocking collectives  23.3 us
  transfers between devices with their start and end apart: 10, of which 6 were waited for; matrix products, arithmetic and copies ran while one was open for 28% of the time, Pallas kernels for 0%

commit v1 on v0

--- a/solution.py
+++ b/solution.py
@@ -1,12 +1,1057 @@
+import functools
 import math
 
 import jax
 import jax.numpy as jnp
 import numpy as np
 from jax import lax
+from jax.experimental import pallas as pl
+from jax.experimental.pallas import tpu as pltpu
 from jax.sharding import PartitionSpec as P
 
 PIC = 256
+EPS = 1e-6
+LOW = jnp.bfloat16
+FULL = jnp.float32
+VM = pl.BlockSpec(memory_space=pltpu.VMEM)
+SM = pl.BlockSpec(memory_space=pltpu.SMEM)
+HBM = pl.BlockSpec(memory_space=pl.ANY)
+MIB = 1 << 20
+ATT_ROWS = 256
+ATT_UNROLL = 2
+MESH = pl.DeviceIdType.MESH
+SECOND = 512.0
+SLOTS = 256
+ROW_TILE = 256
+FF_TILE = 512
+
+
+def offset_bucket(offsets, buckets):
+    half_count = buckets // 2
+    exact_count = half_count // 2
+    upper_half = (offsets > 0).astype(np.int64) * half_count
+    distance = np.abs(offsets)
+    scaled = (
+        np.log(np.maximum(distance, 1) / float(exact_count))
+        / np.log(128.0 / exact_count)
+        * (half_count - exact_count)
+    )
+    larger = np.minimum(
+        exact_count + np.floor(np.maximum(scaled, 0.0)).astype(np.int64), half_count - 1
+    )
+    return upper_half + np.where(distance < exact_count, distance, larger)
+
+
+def near_onehot(buckets):
+    bucket = offset_bucket(np.arange(512) - 256, buckets)
+    return (np.arange(buckets)[:, None] == bucket[None, :]).astype(np.float32)
+
+
+def dot_nn(a, b):
+    return lax.dot_general(a, b, (((1,), (0,)), ((), ())), preferred_element_type=FULL)
+
+
+def dot_nt(a, b):
+    return lax.dot_general(a, b, (((1,), (1,)), ((), ())), preferred_element_type=FULL)
+
+
+def dot_tn(a, b):
+    return lax.dot_general(a, b, (((0,), (0,)), ((), ())), preferred_element_type=FULL)
+
+
+def exact_nn(a, b):
+    return lax.dot_general(
+        a, b, (((1,), (0,)), ((), ())), precision=lax.Precision.HIGHEST, preferred_element_type=FULL
+    )
+
+
+def exact_nt(a, b):
+    return lax.dot_general(
+        a, b, (((1,), (1,)), ((), ())), precision=lax.Precision.HIGHEST, preferred_element_type=FULL
+    )
+
+
+def split3(x):
+    hi = x.astype(LOW)
+    rest = x - hi.astype(FULL)
+    mid = rest.astype(LOW)
+    low = (rest - mid.astype(FULL)).astype(LOW)
+    return hi, mid, low
+
+
+def half_mask(sub, value, shape=(1, 128)):
+    lane = lax.broadcasted_iota(jnp.int32, shape, 1)
+    keep = (lane < 64) if sub == 0 else (lane >= 64)
+    return jnp.where(keep, value, 0.0).astype(FULL)
+
+
+def attn_setup(span_ref, table_ref, onehot_ref, near_ref, mask_ref):
+    seq_len = mask_ref.shape[0]
+    heads = near_ref.shape[0]
+    start = span_ref[0]
+    qi = lax.broadcasted_iota(jnp.int32, (seq_len, seq_len), 0)
+    kj = lax.broadcasted_iota(jnp.int32, (seq_len, seq_len), 1)
+    q_in = (qi >= start) & (qi < start + PIC)
+    k_in = (kj >= start) & (kj < start + PIC)
+    mask_ref[...] = jnp.where((kj <= qi) | (q_in & k_in), 0.0, -1e30).astype(FULL)
+    vecs = exact_nn(table_ref[...], onehot_ref[...])
+    for h in range(heads):
+        rows = jnp.broadcast_to(vecs[h : h + 1, :], (128, 512))
+        rolled = pltpu.roll(rows, 0, 1, stride=1, stride_axis=0)
+        near_ref[h] = rolled[:, 128:]
+
+
+def bias_rows(block, blocks, near):
+    far_neg = jnp.broadcast_to(near[127:128, 0:1], (128, 128))
+    far_pos = jnp.broadcast_to(near[0:1, 383:384], (128, 128))
+    pieces = []
+    for other in range(blocks):
+        d = other - block
+        if d <= -2:
+            pieces.append(far_neg)
+        elif d >= 2:
+            pieces.append(far_pos)
+        else:
+            pieces.append(near[:, (d + 1) * 128 : (d + 2) * 128])
+    return jnp.concatenate(pieces, axis=1)
+
+
+def attn_block(row0, count, qkv_ref, near_ref, mask_ref, prob_ref, mixed_ref):
+    seq_len, width3 = qkv_ref.shape
+    width = width3 // 3
+    blocks = seq_len // 128
+    rows = slice(row0, row0 + count)
+
+    @pl.loop(0, width // 128, unroll=ATT_UNROLL)
+    def _(pair):
+        col = pl.multiple_of(pair * 128, 128)
+        qp = qkv_ref[rows, pl.ds(col, 128)].astype(FULL)
+        kp = qkv_ref[:, pl.ds(width + col, 128)]
+        vp = qkv_ref[:, pl.ds(2 * width + col, 128)]
+        qs = jnp.concatenate([qp * half_mask(sub, 0.125) for sub in range(2)], axis=0)
+        scores = dot_nt(qs.astype(LOW), kp)
+        probs = []
+        for sub in range(2):
+            h = 2 * pair + sub
+            for part in range(count // 128):
+                first = sub * count + part * 128
+                here = slice(row0 + part * 128, row0 + part * 128 + 128)
+                s = scores[first : first + 128]
+                bias = bias_rows(row0 // 128 + part, blocks, near_ref[h])
+                s = s + bias + mask_ref[here, :]
+                top = jnp.max(s, axis=1, keepdims=True)
+                e = jnp.exp(s - top)
+                total = jnp.sum(e, axis=1, keepdims=True)
+                p = (e * (1.0 / total)).astype(LOW)
+                prob_ref[h, here, :] = p
+                probs.append(p)
+        outs = dot_nn(jnp.concatenate(probs, axis=0), vp)
+        lane = lax.broadcasted_iota(jnp.int32, (count, 128), 1)
+        mixed_ref[rows, pl.ds(col, 128)] = jnp.where(
+            lane < 64, outs[:count], outs[count:]
+        ).astype(LOW)
+
+
+def choice_hits(routes, experts):
+    who = lax.broadcasted_iota(jnp.int32, (experts, routes.shape[1]), 0)
+    return [who == routes[k : k + 1, :] for k in range(2)]
+
+
+def to_column(row, width):
+    return jnp.transpose(jnp.broadcast_to(row, (8, width)))[:, 0:1]
+
+
+def ranks_by_priority(hits, priority):
+    tokens = priority.shape[1]
+    prio = priority.astype(FULL)
+    less = jnp.where(to_column(prio, tokens) < prio, 1.0, 0.0).astype(LOW)
+    return [dot_nn(jnp.where(hit, 1.0, 0.0).astype(LOW), less) for hit in hits]
+
+
+def attn_dispatch_kernel(
+    tokens_ref,
+    cot_ref,
+    gain1_ref,
+    wqkv_ref,
+    wproj_ref,
+    table_ref,
+    onehot_ref,
+    gain2_ref,
+    wrouter_ref,
+    routes_ref,
+    prio_ref,
+    span_ref,
+    qkv_out,
+    prob_out,
+    mixed_out,
+    hidden_out,
+    normed2_out,
+    rows_ref,
+    cotrows_ref,
+    resg_ref,
+    gatecol_ref,
+    token_ref,
+    info_ref,
+    qkv_ref,
+    prob_ref,
+    mixed_ref,
+    hidden_ref,
+    normed2_ref,
+    near_ref,
+    mask_ref,
+    meta_ref,
+    gate_ref,
+    meta_all,
+    gate_all,
+    gat_c,
+    gat_n,
+    acc_c,
+    acc_n,
+    acc_g,
+    pos_ref,
+    send_sem,
+    recv_sem,
+    small_send,
+    small_recv,
+    out_sem,
+):
+    g = lax.axis_index("group")
+    me = lax.axis_index("expert")
+    experts = wrouter_ref.shape[0]
+    seq_len, width = tokens_ref.shape
+    half = seq_len // 2
+
+    def device(mask):
+        return (g, lax.bitwise_xor(me, mask))
+
+    barrier = pltpu.get_barrier_semaphore()
+    for mask in range(1, experts):
+        pl.semaphore_signal(barrier, inc=1, device_id=device(mask), device_id_type=MESH)
+    pl.semaphore_wait(barrier, experts - 1)
+
+    gats = (gat_c, gat_n)
+    owns = (cot_ref, normed2_ref)
+
+    def send(which, kind, chunk, held, target):
+        rows = pl.ds(chunk * half, half)
+        slot = lax.bitwise_xor(me, held)
+        src = owns[which].at[rows, :] if held == 0 else gats[which].at[slot, rows, :]
+        return pltpu.make_async_remote_copy(
+            src_ref=src,
+            dst_ref=gats[which].at[slot, rows, :],
+            send_sem=send_sem.at[which, kind, chunk],
+            recv_sem=recv_sem.at[which, held ^ target, chunk],
+            device_id=device(target),
+            device_id_type=MESH,
+        )
+
+    started = []
+
+    def go(*args):
+        copy = send(*args)
+        copy.start()
+        started.append(copy)
+
+    def arrived(which, mask, chunk):
+        rows = pl.ds(chunk * half, half)
+        here = gats[which].at[lax.bitwise_xor(me, mask), rows, :]
+        pltpu.make_async_remote_copy(
+            src_ref=here,
+            dst_ref=here,
+            send_sem=send_sem.at[which, 0, chunk],
+            recv_sem=recv_sem.at[which, mask, chunk],
+            device_id=device(1),
+            device_id_type=MESH,
+        ).wait_recv()
+
+    def own_out(which, chunk):
+        go(which, 0, chunk, 0, 2)
+        go(which, 1, chunk, 0, 4)
+        go(which, 2, chunk, 0, 1)
+
+    def relay(which):
+        arrived(which, 2, 0)
+        go(which, 3, 0, 2, 4)
+        arrived(which, 4, 1)
+        go(which, 3, 1, 4, 2)
+
+    def small(src, dst, index):
+        for mask in range(1, experts):
+            copy = pltpu.make_async_remote_copy(
+                src_ref=src,
+                dst_ref=dst.at[me],
+                send_sem=small_send.at[index, mask],
+                recv_sem=small_recv.at[index, mask],
+                device_id=device(mask),
+                device_id_type=MESH,
+            )
+            copy.start()
+            started.append(copy)
+
+    def small_arrived(dst, index):
+        for mask in range(1, experts):
+            here = dst.at[lax.bitwise_xor(me, mask)]
+            pltpu.make_async_remote_copy(
+                src_ref=here,
+                dst_ref=here,
+                send_sem=small_send.at[index, mask],
+                recv_sem=small_recv.at[index, mask],
+                device_id=device(1),
+                device_id_type=MESH,
+            ).wait_recv()
+
+    own_out(0, 0)
+    own_out(0, 1)
+
+    hits = choice_hits(routes_ref[...], experts)
+    ranks = ranks_by_priority(hits, prio_ref[...])
+    meta = jnp.where(hits[0], ranks[0], jnp.where(hits[1], ranks[1] + SECOND, -1.0))
+    meta_ref[...] = meta
+    meta_all[me] = meta
+    small(meta_ref, meta_all, 0)
+
+    attn_setup(span_ref, table_ref, onehot_ref, near_ref, mask_ref)
+    for row0 in range(0, seq_len, 128):
+        rows = slice(row0, row0 + 128)
+        x = tokens_ref[rows, :].astype(FULL)
+        inv = lax.rsqrt(jnp.mean(x * x, axis=1, keepdims=True) + EPS)
+        n1 = (x * inv * gain1_ref[...][None, :]).astype(LOW)
+        qkv_ref[rows, :] = dot_nn(n1, wqkv_ref[...]).astype(LOW)
+    outs = [pltpu.make_async_copy(qkv_ref, qkv_out, out_sem.at[0])]
+    outs[0].start()
+
+    logits = []
+    for chunk in range(2):
+        row0 = chunk * half
+        rows = slice(row0, row0 + half)
+        attn_block(row0, half, qkv_ref, near_ref, mask_ref, prob_ref, mixed_ref)
+        hidden = tokens_ref[rows, :].astype(FULL) + dot_nn(mixed_ref[rows, :], wproj_ref[...])
+        hidden_ref[rows, :] = hidden
+        inv = lax.rsqrt(jnp.mean(hidden * hidden, axis=1, keepdims=True) + EPS)
+        n2 = (hidden * inv * gain2_ref[...][None, :]).astype(LOW)
+        normed2_ref[rows, :] = n2
+        own_out(1, chunk)
+        logits.append(dot_nt(wrouter_ref[...], n2))
+        if chunk == 0:
+            relay(0)
+    for index, (src, dst) in enumerate(
+        ((prob_ref, prob_out), (mixed_ref, mixed_out), (hidden_ref, hidden_out), (normed2_ref, normed2_out))
+    ):
+        copy = pltpu.make_async_copy(src, dst, out_sem.at[index + 1])
+        copy.start()
+        outs.append(copy)
+
+    logits = jnp.concatenate(logits, axis=1)
+    unnormed = jnp.exp(logits - jnp.max(logits, axis=0, keepdims=True))
+    probabilities = unnormed / jnp.sum(unnormed, axis=0, keepdims=True)
+    picked = [jnp.sum(jnp.where(hit, probabilities, 0.0), axis=0, keepdims=True) for hit in hits]
+    both = picked[0] + picked[1]
+    gates = [p / both for p in picked]
+    gate = jnp.where(hits[0], gates[0], jnp.where(hits[1], gates[1], 0.0))
+    gate_ref[...] = gate
+    gate_all[me] = gate
+    small(gate_ref, gate_all, 1)
+
+    first_count = jnp.sum(jnp.where(hits[0], 1.0, 0.0), axis=1, keepdims=True)
+    who = lax.broadcasted_iota(jnp.int32, hits[0].shape, 0).astype(FULL)
+    slots = [
+        jnp.sum(jnp.where(hits[0], ranks[0] + who * SLOTS, 0.0), axis=0, keepdims=True),
+        jnp.sum(
+            jnp.where(hits[1], ranks[1] + first_count + who * SLOTS, 0.0), axis=0, keepdims=True
+        ),
+    ]
+    routes_f = routes_ref[...].astype(FULL)
+    token_rows = jnp.concatenate(slots + gates + [routes_f[0:1], routes_f[1:2]] + slots, axis=0)
+    token_ref[...] = jnp.transpose(token_rows)
+
+    small_arrived(meta_all, 0)
+    value = meta_all[:, me, :]
+    is_first = (value >= 0.0) & (value < SECOND)
+    is_second = value >= SECOND
+    counts = [
+        jnp.sum(jnp.where(hit, 1.0, 0.0), axis=1, keepdims=True) for hit in (is_first, is_second)
+    ]
+    row = lax.broadcasted_iota(jnp.int32, (experts, 128), 0)
+    lane = lax.broadcasted_iota(jnp.int32, (experts, 128), 1)
+    count_mat = jnp.where(lane == 0, counts[0], jnp.where(lane == 1, counts[1], 0.0))
+    before = jnp.zeros((experts, 128), FULL)
+    for s in range(experts):
+        before = before + jnp.where(row > s, count_mat[s : s + 1, :], 0.0)
+    first_total = jnp.sum(counts[0], axis=0, keepdims=True)
+    base = [before[:, 0:1], before[:, 1:2] + first_total]
+    pos_ref[...] = jnp.where(
+        is_first, value + base[0], jnp.where(is_second, value - SECOND + base[1], -1.0)
+    )
+    info_ref[...] = jnp.where(
+        lane == 0,
+        counts[0],
+        jnp.where(lane == 1, counts[1], jnp.where(lane == 2, base[0], base[1])),
+    )
+
+    acc_c[...] = jnp.zeros_like(acc_c)
+    acc_n[...] = jnp.zeros_like(acc_n)
+    acc_g[...] = jnp.zeros_like(acc_g)
+
+    def compact(which, mask, chunk):
+        slot = lax.bitwise_xor(me, mask)
+        cols = slice(chunk * half, chunk * half + half)
+        acc = (acc_c, acc_n)[which]
+
+        @pl.loop(0, acc.shape[0] // ROW_TILE)
+        def _(tile):
+            row0 = pl.multiple_of(tile * ROW_TILE, ROW_TILE)
+            place = pos_ref[pl.ds(slot, 1), :][:, cols] - row0.astype(FULL)
+            at = lax.broadcasted_iota(jnp.int32, (ROW_TILE, half), 0).astype(FULL)
+            pick = jnp.where(at == place, 1.0, 0.0).astype(LOW)
+            if mask == 0:
+                data = owns[which][cols, :]
+            else:
+                data = gats[which][slot, cols, :]
+            acc[pl.ds(row0, ROW_TILE), :] += dot_nn(pick, data)
+            if which == 1:
+                g_row = gate_all[slot, pl.ds(me, 1), :][:, cols]
+                terms = [jnp.broadcast_to(t.astype(FULL), (8, half)) for t in split3(g_row)]
+                third = lax.broadcasted_iota(jnp.int32, (8, half), 0)
+                mat = jnp.where(
+                    third == 0, terms[0], jnp.where(third == 1, terms[1], jnp.where(third == 2, terms[2], 0.0))
+                ).astype(LOW)
+                acc_g[pl.ds(row0, ROW_TILE), :] += dot_nt(pick, mat)
+
+    def take(which, mask):
+        for chunk in range(2):
+            if mask:
+                arrived(which, mask, chunk)
+        if mask in (2, 4, 6):
+            for chunk in range(2):
+                go(which, 2 + mask // 2 + 0 * chunk + 1, chunk, mask, 1)
+        for chunk in range(2):
+            compact(which, mask, chunk)
+
+    def take_relayed(which, mask, chunk_done):
+        arrived(which, mask, 1 - chunk_done)
+        for chunk in range(2):
+            go(which, 3 + mask // 2, chunk, mask, 1)
+        for chunk in range(2):
+            compact(which, mask, chunk)
+
+    take(0, 0)
+    take(0, 1)
+    take_relayed(0, 2, 0)
+    take_relayed(0, 4, 1)
+    take(0, 6)
+    take(0, 3)
+    take(0, 5)
+    relay(1)
+    take(0, 7)
+    small_arrived(gate_all, 1)
+    take(1, 0)
+    take(1, 1)
+    take_relayed(1, 2, 0)
+    take_relayed(1, 4, 1)
+    take(1, 3)
+    take(1, 5)
+    take(1, 6)
+    take(1, 7)
+
+    @pl.loop(0, acc_n.shape[0] // ROW_TILE)
+    def _(tile):
+        rows = pl.ds(pl.multiple_of(tile * ROW_TILE, ROW_TILE), ROW_TILE)
+        cot_rows = acc_c[rows, :]
+        gate_col = jnp.sum(acc_g[rows, :], axis=1, keepdims=True)
+        rows_ref[rows, :] = acc_n[rows, :].astype(LOW)
+        cotrows_ref[rows, :] = cot_rows.astype(LOW)
+        resg_ref[rows, :] = (gate_col * cot_rows).astype(LOW)
+        gatecol_ref[rows, :] = jnp.broadcast_to(gate_col, (ROW_TILE, 128))
+
+    for copy in outs:
+        copy.wait()
+    for copy in started:
+        copy.wait_send()
+
+
+def attn_dispatch(
+    tokens, cot, gain1, wqkv, wproj, table, gain2, wrouter, routes, priority, span
+):
+    seq_len, width = tokens.shape
+    buckets, heads = table.shape
+    experts = wrouter.shape[1]
+    capacity = 5 * seq_len // 2
+    sds = jax.ShapeDtypeStruct
+    dma = pltpu.SemaphoreType.DMA
+    return pl.pallas_call(
+        attn_dispatch_kernel,
+        out_shape=(
+            sds((seq_len, 3 * width), LOW),
+            sds((heads, seq_len, seq_len), LOW),
+            sds((seq_len, width), LOW),
+            sds((seq_len, width), FULL),
+            sds((seq_len, width), LOW),
+            sds((capacity, width), LOW),
+            sds((capacity, width), LOW),
+            sds((capacity, width), LOW),
+            sds((capacity, 128), FULL),
+            sds((seq_len, 8), FULL),
+            sds((experts, 128), FULL),
+        ),
+        in_specs=[VM] * 11 + [SM],
+        out_specs=[HBM] * 5 + [VM] * 6,
+        scratch_shapes=[
+            pltpu.VMEM((seq_len, 3 * width), LOW),
+            pltpu.VMEM((heads, seq_len, seq_len), LOW),
+            pltpu.VMEM((seq_len, width), LOW),
+            pltpu.VMEM((seq_len, width), FULL),
+            pltpu.VMEM((seq_len, width), LOW),
+            pltpu.VMEM((heads, 128, 384), FULL),
+            pltpu.VMEM((seq_len, seq_len), FULL),
+            pltpu.VMEM((experts, seq_len), FULL),
+            pltpu.VMEM((experts, seq_len), FULL),
+            pltpu.VMEM((experts, experts, seq_len), FULL),
+            pltpu.VMEM((experts, experts, seq_len), FULL),
+            pltpu.VMEM((experts, seq_len, width), LOW),
+            pltpu.VMEM((experts, seq_len, width), LOW),
+            pltpu.VMEM((capacity, width), FULL),
+            pltpu.VMEM((capacity, width), FULL),
+            pltpu.VMEM((capacity, 8), FULL),
+            pltpu.VMEM((experts, seq_len), FULL),
+            dma((2, 7, 2)),
+            dma((2, 8, 2)),
+            dma((2, 8)),
+            dma((2, 8)),
+            dma((5,)),
+        ],
+        compiler_params=pltpu.CompilerParams(
+            vmem_limit_bytes=60 * MIB, collective_id=0, has_side_effects=True
+        ),
+    )(
+        tokens,
+        cot,
+        gain1,
+        wqkv,
+        wproj,
+        table.T,
+        jnp.asarray(near_onehot(buckets)),
+        gain2,
+        wrouter.T,
+        routes.T,
+        priority,
+        span,
+    )
+
+
+def expert_first_kernel(rows_ref, resg_ref, win_ref, act_ref, slope_ref, gout_ref):
+    pre = dot_nn(rows_ref[...], win_ref[...])
+    act, slope = gelu_and_slope(pre)
+    act_ref[...] = act.astype(LOW)
+    slope_ref[...] = slope.astype(LOW)
+    gout_ref[...] = dot_tn(act_ref[...], resg_ref[...]).astype(LOW)
+
+
+def gelu_and_slope(x):
+    c = math.sqrt(2.0 / math.pi)
+    square = x * x
+    t = jnp.tanh(x * (c + (c * 0.044715) * square))
+    cdf = 0.5 + 0.5 * t
+    slope = cdf + (0.5 * x) * (1.0 - t * t) * (c + (3.0 * c * 0.044715) * square)
+    return x * cdf, slope
+
+
+def expert_first(rows, resg, w_in):
+    capacity, width = rows.shape
+    ff = w_in.shape[1]
+    sds = jax.ShapeDtypeStruct
+    return pl.pallas_call(
+        expert_first_kernel,
+        grid=(ff // FF_TILE,),
+        out_shape=(
+            sds((capacity, ff), LOW),
+            sds((capacity, ff), LOW),
+            sds((ff, width), LOW),
+        ),
+        in_specs=[
+            pl.BlockSpec((capacity, width), lambda f: (0, 0)),
+            pl.BlockSpec((capacity, width), lambda f: (0, 0)),
+            pl.BlockSpec((width, FF_TILE), lambda f: (0, f)),
+        ],
+        out_specs=[
+            pl.BlockSpec((capacity, FF_TILE), lambda f: (0, f)),
+            pl.BlockSpec((capacity, FF_TILE), lambda f: (0, f)),
+            pl.BlockSpec((FF_TILE, width), lambda f: (f, 0)),
+        ],
+        compiler_params=pltpu.CompilerParams(vmem_limit_bytes=56 * MIB),
+        cost_estimate=pl.CostEstimate(
+            flops=4 * capacity * width * ff, bytes_accessed=40 * MIB, transcendentals=capacity * ff
+        ),
+    )(rows, resg, w_in)
+
+
+def pack_rows(source, info_ref, data, out_ref, slots):
+    info = info_ref[source : source + 1, :]
+    slot = lax.broadcasted_iota(jnp.int32, (slots, 1), 0).astype(FULL)
+    n0, n1, b0, b1 = [info[:, i : i + 1] for i in range(4)]
+    place = jnp.where(slot < n0, b0 + slot, jnp.where(slot < n0 + n1, b1 + slot - n0, -1.0))
+    at = lax.broadcasted_iota(jnp.int32, (slots, data.shape[0]), 1).astype(FULL)
+    pick = jnp.where(at == place, 1.0, 0.0).astype(LOW)
+    out_ref[source] = dot_nn(pick, data[...]).astype(LOW)
+
+
+def expert_second_kernel(
+    cot_ref, gate_ref, act_ref, slope_ref, wout_ref, win_ref, info_ref, ig_ref, packed_ref, acc_ref, gg_ref, data_ref
+):
+    step = pl.program_id(0)
+    width = cot_ref.shape[1]
+
+    @pl.when(step == 0)
+    def _():
+        acc_ref[...] = jnp.zeros_like(acc_ref)
+        gg_ref[...] = jnp.zeros_like(gg_ref)
+
+    back = dot_nt(cot_ref[...], wout_ref[...])
+    part = act_ref[...].astype(FULL) * back
+    total = part[:, 0:128]
+    for i in range(1, part.shape[1] // 128):
+        total = total + part[:, i * 128 : i * 128 + 128]
+    gg_ref[...] += total
+    ig = (slope_ref[...].astype(FULL) * (gate_ref[:, 0:1] * back)).astype(LOW)
+    ig_ref[...] = ig
+    acc_ref[...] += dot_nt(ig, win_ref[...])
+
+    @pl.when(step == pl.num_programs(0) - 1)
+    def _():
+        data_ref[:, :width] = acc_ref[...].astype(LOW)
+        gg = jnp.sum(gg_ref[...], axis=1, keepdims=True)
+        hi, mid, low = [t.astype(FULL) for t in split3(gg)]
+        lane = lax.broadcasted_iota(jnp.int32, (gg.shape[0], 128), 1)
+        data_ref[:, width:] = jnp.where(
+            lane == 0, hi, jnp.where(lane == 1, mid, jnp.where(lane == 2, low, 0.0))
+        ).astype(LOW)
+        for source in range(packed_ref.shape[0]):
+            pack_rows(source, info_ref, data_ref, packed_ref, packed_ref.shape[1])
+
+
+def expert_second(cot_rows, gate_col, act, slope, w_out, w_in, info):
+    capacity, width = cot_rows.shape
+    ff = w_in.shape[1]
+    experts = info.shape[0]
+    sds = jax.ShapeDtypeStruct
+    return pl.pallas_call(
+        expert_second_kernel,
+        grid=(ff // FF_TILE,),
+        out_shape=(
+            sds((capacity, ff), LOW),
+            sds((experts, SLOTS, width + 128), LOW),
+        ),
+        in_specs=[
+            pl.BlockSpec((capacity, width), lambda f: (0, 0)),
+            pl.BlockSpec((capacity, 128), lambda f: (0, 0)),
+            pl.BlockSpec((capacity, FF_TILE), lambda f: (0, f)),
+            pl.BlockSpec((capacity, FF_TILE), lambda f: (0, f)),
+            pl.BlockSpec((FF_TILE, width), lambda f: (f, 0)),
+            pl.BlockSpec((width, FF_TILE), lambda f: (0, f)),
+            pl.BlockSpec((experts, 128), lambda f: (0, 0)),
+        ],
+        out_specs=[
+            pl.BlockSpec((capacity, FF_TILE), lambda f: (0, f)),
+            pl.BlockSpec((experts, SLOTS, width + 128), lambda f: (0, 0, 0)),
+        ],
+        scratch_shapes=[
+            pltpu.VMEM((capacity, width), FULL),
+            pltpu.VMEM((capacity, 128), FULL),
+            pltpu.VMEM((capacity, width + 128), LOW),
+        ],
+        compiler_params=pltpu.CompilerParams(vmem_limit_bytes=56 * MIB),
+        cost_estimate=pl.CostEstimate(
+            flops=4 * capacity * width * ff, bytes_accessed=50 * MIB, transcendentals=0
+        ),
+    )(cot_rows, gate_col, act, slope, w_out, w_in, info)
+
+
+def expert_inner_kernel(rows_ref, ig_ref, gin_ref, rows_t):
+    @pl.when(pl.program_id(0) == 0)
+    def _():
+        rows_t[...] = jnp.transpose(rows_ref[...])
+
+    gin_ref[...] = dot_nn(rows_t[...], ig_ref[...]).astype(LOW)
+
+
+def expert_inner(rows, ig):
+    capacity, width = rows.shape
+    ff = ig.shape[1]
+    return pl.pallas_call(
+        expert_inner_kernel,
+        grid=(ff // FF_TILE,),
+        out_shape=jax.ShapeDtypeStruct((width, ff), LOW),
+        in_specs=[
+            pl.BlockSpec((capacity, width), lambda f: (0, 0)),
+            pl.BlockSpec((capacity, FF_TILE), lambda f: (0, f)),
+        ],
+        out_specs=pl.BlockSpec((width, FF_TILE), lambda f: (0, f)),
+        scratch_shapes=[pltpu.VMEM((width, capacity), LOW)],
+        compiler_params=pltpu.CompilerParams(vmem_limit_bytes=56 * MIB),
+        cost_estimate=pl.CostEstimate(
+            flops=2 * capacity * width * ff, bytes_accessed=15 * MIB, transcendentals=0
+        ),
+    )(rows, ig)
+
+
+def expert_result_kernel(act_ref, wout_ref, info_ref, packed_ref, acc_ref, data_ref):
+    step = pl.program_id(0)
+
+    @pl.when(step == 0)
+    def _():
+        acc_ref[...] = jnp.zeros_like(acc_ref)
+
+    acc_ref[...] += dot_nn(act_ref[...], wout_ref[...])
+
+    @pl.when(step == pl.num_programs(0) - 1)
+    def _():
+        data_ref[...] = acc_ref[...].astype(LOW)
+        for source in range(packed_ref.shape[0]):
+            pack_rows(source, info_ref, data_ref, packed_ref, packed_ref.shape[1])
+
+
+def expert_result(act, w_out, info):
+    capacity, ff = act.shape
+    width = w_out.shape[1]
+    experts = info.shape[0]
+    return pl.pallas_call(
+        expert_result_kernel,
+        grid=(ff // FF_TILE,),
+        out_shape=jax.ShapeDtypeStruct((experts, SLOTS, width), LOW),
+        in_specs=[
+            pl.BlockSpec((capacity, FF_TILE), lambda f: (0, f)),
+            pl.BlockSpec((FF_TILE, width), lambda f: (f, 0)),
+            pl.BlockSpec((experts, 128), lambda f: (0, 0)),
+        ],
+        out_specs=pl.BlockSpec((experts, SLOTS, width), lambda f: (0, 0, 0)),
+        scratch_shapes=[pltpu.VMEM((capacity, width), FULL), pltpu.VMEM((capacity, width), LOW)],
+        compiler_params=pltpu.CompilerParams(vmem_limit_bytes=56 * MIB),
+        cost_estimate=pl.CostEstimate(
+            flops=2 * capacity * width * ff, bytes_accessed=20 * MIB, transcendentals=0
+        ),
+    )(act, w_out, info)
+
+
+def slot_picks(token_ref, slots):
+    at = lax.broadcasted_iota(jnp.int32, (token_ref.shape[0], slots), 1).astype(FULL)
+    return [jnp.where(at == token_ref[:, k : k + 1], 1.0, 0.0) for k in range(2)]
+
+
+def combine_kernel(hidden_ref, token_ref, back_ref, out_ref):
+    rows = 128
+    width = hidden_ref.shape[1]
+    for row0 in range(0, hidden_ref.shape[0], rows):
+        here = slice(row0, row0 + rows)
+        token = token_ref[here, :]
+        at = lax.broadcasted_iota(jnp.int32, (rows, back_ref.shape[0]), 1).astype(FULL)
+        picks = [jnp.where(at == token[:, k : k + 1], 1.0, 0.0).astype(LOW) for k in range(2)]
+        got = dot_nn(jnp.concatenate(picks, axis=0), back_ref[...])
+        out = hidden_ref[here, :] + token[:, 2:3] * got[:rows] + token[:, 3:4] * got[rows:]
+        out_ref[here, :] = out.astype(LOW)
+
+
+def combine(hidden, token, back):
+    return pl.pallas_call(
+        combine_kernel,
+        out_shape=jax.ShapeDtypeStruct(hidden.shape, LOW),
+        in_specs=[VM] * 3,
+        out_specs=VM,
+        compiler_params=pltpu.CompilerParams(vmem_limit_bytes=56 * MIB),
+        cost_estimate=pl.CostEstimate(
+            flops=4 * hidden.shape[0] * hidden.shape[1] * back.shape[0],
+            bytes_accessed=6 * MIB,
+            transcendentals=0,
+        ),
+    )(hidden, token, back)
+
+
+def attn_back_kernel(
+    tokens_ref,
+    cot_ref,
+    hidden_ref,
+    normed2_ref,
+    mixed_ref,
+    qkv_ref,
+    prob_ref,
+    recv_ref,
+    token_ref,
+    gain1_ref,
+    gain2_ref,
+    wqkv_ref,
+    wproj_ref,
+    wrouter_ref,
+    onehot_ref,
+    gtok_ref,
+    ggain1_ref,
+    gqkv_ref,
+    gproj_ref,
+    gtable_ref,
+    ggain2_ref,
+    grouter_ref,
+    hgrad_ref,
+    mgrad_ref,
+    mgrad_t,
+    q_t,
+    ds_ref,
+    diag_ref,
+    dk_t,
+    dv_t,
+    dqkv_ref,
+):
+    seq_len, width = tokens_ref.shape
+    experts = wrouter_ref.shape[0]
+    heads = prob_ref.shape[0]
+    tile = 128
+    ggain2 = jnp.zeros((8, width), FULL)
+    lg_t = []
+    for row0 in range(0, seq_len, tile):
+        rows = slice(row0, row0 + tile)
+        token = token_ref[rows, :]
+        at = lax.broadcasted_iota(jnp.int32, (tile, recv_ref.shape[0]), 1).astype(FULL)
+        picks = [jnp.where(at == token[:, k : k + 1], 1.0, 0.0).astype(LOW) for k in range(2)]
+        got = dot_nn(jnp.concatenate(picks, axis=0), recv_ref[...])
+        gg = [
+            jnp.sum(got[k * tile : k * tile + tile, width:], axis=1, keepdims=True) for k in range(2)
+        ]
+        pull = token[:, 2:3] * token[:, 3:4] * (gg[0] - gg[1])
+        expert = lax.broadcasted_iota(jnp.int32, (tile, 128), 1).astype(FULL)
+        lg = jnp.where(expert == token[:, 4:5], pull, jnp.where(expert == token[:, 5:6], -pull, 0.0))
+        lg_t.append(jnp.transpose(lg)[:experts])
+        ngrad = (
+            got[:tile, :width]
+            + got[tile:, :width]
+            + dot_nn(lg[:, :experts].astype(LOW), wrouter_ref[...])
+        )
+        hidden = hidden_ref[rows, :]
+        inv = lax.rsqrt(jnp.mean(hidden * hidden, axis=1, keepdims=True) + EPS)
+        unit = hidden * inv
+        ng = ngrad * unit
+        for i in range(tile // 8):
+            ggain2 = ggain2 + ng[i * 8 : i * 8 + 8]
+        scaled = ngrad * gain2_ref[...][None, :]
+        proj = jnp.mean(scaled * unit, axis=1, keepdims=True)
+        hgrad_ref[rows, :] = cot_ref[rows, :].astype(FULL) + inv * (scaled - unit * proj)
+        mgrad_ref[rows, :] = dot_nt(hgrad_ref[rows, :].astype(LOW), wproj_ref[...]).astype(LOW)
+    ggain2_ref[...] = jnp.sum(ggain2, axis=0, keepdims=True)
+    logit_grad_t = jnp.concatenate(lg_t, axis=1).astype(LOW)
+    grouter_ref[...] = dot_nn(logit_grad_t, normed2_ref[...])
+    gproj_ref[...] = dot_nn(
+        jnp.transpose(mixed_ref[...]), hgrad_ref[...].astype(LOW)
+    ).astype(LOW)
+    mgrad_t[...] = jnp.transpose(mgrad_ref[...])
+    q_t[...] = jnp.transpose(qkv_ref[:, :width])
+    up = lax.broadcasted_iota(jnp.int32, (128, 128), 0)
+    across = lax.broadcasted_iota(jnp.int32, (128, 128), 1)
+    flip = jnp.where(up + across == 127, 1.0, 0.0).astype(FULL)
+
+    @pl.loop(0, width // 128)
+    def _(pair):
+        col = pl.multiple_of(pair * 128, 128)
+        kp = qkv_ref[:, pl.ds(width + col, 128)]
+        vp = qkv_ref[:, pl.ds(2 * width + col, 128)]
+        op = mgrad_ref[:, pl.ds(col, 128)].astype(FULL)
+        os = jnp.concatenate([(op * half_mask(sub, 1.0)).astype(LOW) for sub in range(2)], axis=0)
+        dp = dot_nt(os, vp)
+        for sub in range(2):
+            h = 2 * pair + sub
+            near = jnp.zeros((128, 384), FULL)
+            far_neg = jnp.zeros((128, 128), FULL)
+            far_pos = jnp.zeros((128, 128), FULL)
+            blocks = seq_len // 128
+            for block in range(blocks):
+                first = sub * seq_len + block * 128
+                here = slice(block * 128, block * 128 + 128)
+                p = prob_ref[h, here, :].astype(FULL)
+                weighted = p * dp[first : first + 128]
+                ds = weighted - p * jnp.sum(weighted, axis=1, keepdims=True)
+                low = ds.astype(LOW)
+                ds_ref[sub, here, :] = low
+                ds = low.astype(FULL)
+                strip = []
+                for d in range(-1, 2):
+                    other = block + d
+                    if 0 <= other < blocks:
+                        strip.append(ds[:, other * 128 : other * 128 + 128])
+                    else:
+                        strip.append(jnp.zeros((128, 128), FULL))
+                near = near + jnp.concatenate(strip, axis=1)
+                for other in range(blocks):
+                    piece = ds[:, other * 128 : other * 128 + 128]
+                    if other - block <= -2:
+                        far_neg = far_neg + piece
+                    elif other - block >= 2:
+                        far_pos = far_pos + piece
+            low_sum = jnp.sum(far_neg)
+            high_sum = jnp.sum(far_pos)
+            padded = jnp.concatenate([exact_nn(flip, near), jnp.zeros((128, 128), FULL)], axis=1)
+            turned = pltpu.roll(padded, 1, 1, stride=1, stride_axis=0)
+            sums = jnp.sum(turned, axis=0, keepdims=True)
+            lane = lax.broadcasted_iota(jnp.int32, (1, 512), 1)
+            sums = sums + jnp.where(lane == 1, low_sum, jnp.where(lane == 511, high_sum, 0.0))
+            diag_ref[pl.ds(h, 1), :] = sums
+        lane = lax.broadcasted_iota(jnp.int32, (seq_len, 128), 1)
+        dq = dot_nn(jnp.concatenate([ds_ref[0], ds_ref[1]], axis=0), kp)
+        dqkv_ref[:, pl.ds(col, 128)] = (
+            jnp.where(lane < 64, dq[:seq_len], dq[seq_len:]) * 0.125
+        ).astype(LOW)
+        for sub in range(2):
+            part = pl.ds(pl.multiple_of(col + sub * 64, 64), 64)
+            dk_t[part, :] = (dot_nn(q_t[part, :], ds_ref[sub]) * 0.125).astype(LOW)
+            dv_t[part, :] = dot_nn(mgrad_t[part, :], prob_ref[2 * pair + sub]).astype(LOW)
+
+    gtable_ref[...] = exact_nt(onehot_ref[...], diag_ref[...])
+    dqkv_ref[:, width : 2 * width] = jnp.transpose(dk_t[...])
+    dqkv_ref[:, 2 * width :] = jnp.transpose(dv_t[...])
+
+    ggain1 = jnp.zeros((8, width), FULL)
+    for row0 in range(0, seq_len, tile):
+        rows = slice(row0, row0 + tile)
+        x = tokens_ref[rows, :].astype(FULL)
+        inv = lax.rsqrt(jnp.mean(x * x, axis=1, keepdims=True) + EPS)
+        unit = x * inv
+        mgrad_ref[rows, :] = (unit * gain1_ref[...][None, :]).astype(LOW)
+        ngrad = dot_nt(dqkv_ref[rows, :], wqkv_ref[...])
+        ng = ngrad * unit
+        for i in range(tile // 8):
+            ggain1 = ggain1 + ng[i * 8 : i * 8 + 8]
+        scaled = ngrad * gain1_ref[...][None, :]
+        proj = jnp.mean(scaled * unit, axis=1, keepdims=True)
+        gtok_ref[rows, :] = (hgrad_ref[rows, :] + inv * (scaled - unit * proj)).astype(LOW)
+    ggain1_ref[...] = jnp.sum(ggain1, axis=0, keepdims=True)
+    mgrad_t[...] = jnp.transpose(mgrad_ref[...])
+    gqkv_ref[...] = dot_nn(mgrad_t[...], dqkv_ref[...]).astype(LOW)
+
+
+def attn_back(
+    tokens, cot, hidden, normed2, mixed, qkv, prob, recv, token, gain1, gain2, wqkv, wproj, wrouter, table
+):
+    seq_len, width = tokens.shape
+    buckets, heads = table.shape
+    experts = wrouter.shape[1]
+    sds = jax.ShapeDtypeStruct
+    return pl.pallas_call(
+        attn_back_kernel,
+        out_shape=(
+            sds((seq_len, width), LOW),
+            sds((1, width), FULL),
+            sds((width, 3 * width), LOW),
+            sds((width, width), LOW),
+            sds((buckets, heads), FULL),
+            sds((1, width), FULL),
+            sds((experts, width), FULL),
+        ),
+        in_specs=[VM] * 15,
+        out_specs=[VM] * 7,
+        scratch_shapes=[
+            pltpu.VMEM((seq_len, width), FULL),
+            pltpu.VMEM((seq_len, width), LOW),
+            pltpu.VMEM((width, seq_len), LOW),
+            pltpu.VMEM((width, seq_len), LOW),
+            pltpu.VMEM((2, seq_len, seq_len), LOW),
+            pltpu.VMEM((heads, 512), FULL),
+            pltpu.VMEM((width, seq_len), LOW),
+            pltpu.VMEM((width, seq_len), LOW),
+            pltpu.VMEM((seq_len, 3 * width), LOW),
+        ],
+        compiler_params=pltpu.CompilerParams(vmem_limit_bytes=56 * MIB),
+        cost_estimate=pl.CostEstimate(
+            flops=20_000_000_000, bytes_accessed=30 * MIB, transcendentals=0
+        ),
+    )(
+        tokens,
+        cot,
+        hidden,
+        normed2,
+        mixed,
+        qkv,
+        prob,
+        recv,
+        token,
+        gain1,
+        gain2,
+        wqkv,
+        wproj,
+        wrouter.T,
+        jnp.asarray(near_onehot(buckets)),
+    )
+
+
+def on_device_fast(
+    tokens,
+    gain_first,
+    w_qkv,
+    w_proj,
+    bias_table,
+    gain_second,
+    w_router,
+    w_in,
+    w_out,
+    routes,
+    priority,
+    span_start,
+    cotangent,
+):
+    experts = w_router.shape[1]
+    width = tokens.shape[1]
+    qkv, prob, mixed, hidden, normed2, rows, cot_rows, resg, gate_col, token, info = attn_dispatch(
+        tokens,
+        cotangent,
+        gain_first,
+        w_qkv,
+        w_proj,
+        bias_table,
+        gain_second,
+        w_router,
+        routes,
+        priority,
+        span_start,
+    )
+    act, slope, grad_outer = expert_first(rows, resg, w_in[0])
+    grad_out = lax.psum_scatter(
+        grad_outer[None], "group", scatter_dimension=1, tiled=True
+    ).astype(FULL)
+    ig, packed = expert_second(cot_rows, gate_col, act, slope, w_out[0], w_in[0], info)
+    recv = lax.all_to_all(packed, "expert", split_axis=0, concat_axis=0, tiled=True)
+    grad_inner = expert_inner(rows, ig)
+    grad_in = lax.psum_scatter(
+        grad_inner[None], "group", scatter_dimension=1, tiled=True
+    ).astype(FULL)
+    packed_out = expert_result(act, w_out[0], info)
+    back = lax.all_to_all(packed_out, "expert", split_axis=0, concat_axis=0, tiled=True)
+    gtok, ggain1, gqkv, gproj, gtable, ggain2, grouter = attn_back(
+        tokens,
+        cotangent,
+        hidden,
+        normed2,
+        mixed,
+        qkv,
+        prob,
+        recv.reshape(-1, width + 128),
+        token,
+        gain_first,
+        gain_second,
+        w_qkv,
+        w_proj,
+        w_router,
+        bias_table,
+    )
+    block_out = combine(hidden, token, back.reshape(-1, width))
+
+    def reduce(x):
+        share = lax.psum_scatter(x.astype(LOW), "expert", scatter_dimension=0, tiled=True)
+        return lax.psum(share, "group").astype(FULL)
+
+    return (
+        block_out,
+        gtok,
+        reduce(ggain1[0]),
+        reduce(gqkv),
+        reduce(gproj),
+        reduce(gtable),
+        reduce(ggain2[0]),
+        reduce(grouter.T),
+        grad_in,
+        grad_out,
+    )
 
 
 def bucket_table(seq_len, buckets):
@@ -282,8 +1327,9 @@
 
 
 def solution(mesh):
+    step = on_device_fast if mesh.shape["expert"] == 8 else on_device
     return jax.shard_map(
-        on_device,
+        step,
         mesh=mesh,
         in_specs=(
             P(("group", "expert"), None),

time: 803 us -> 591 us (0.74); the launches traced: 789 us -> 586 us
  Pallas kernels: 0 us -> 204 us
  matrix products: 165 us -> 0 us
  other arithmetic: 147 us -> 11.6 us
  local copies, waits for them, and re-layouts: 132 us -> 4.06 us
  waiting for transfers between devices: 236 us -> 266 us
  starting transfers between devices: 18.7 us -> 4.23 us
    pallas_call x0 -> x7, Pallas kernels: none -> 204 us  [the longest x1 82.4 us: attn_dispatch(): pl.pallas_call(attn_dispatch_kernel, out_shape=(sds((seq_len, 3 * width),...]
    dot_general x23 -> x0, matrix products: 165 us -> none  [the longest x5 32.6 us: contract_rows(): lax.dot_general(left, right, (((0,), (0,)), ((), ())), preferred_element_...]
    all_to_all x0 -> x1, blocking collectives: none -> 48.4 us  [on_device_fast(): lax.all_to_all(packed, 'expert', split_axis=0, concat_axis=0, tiled=True)]
    gather x6 -> x0, local copies, waits for them, and re-layouts: 48.2 us -> none  [the longest x2 24.9 us: spread_rows(): return padded[destination].reshape(-1, slot_count, model_width)]
    reduce_sum x12 -> x0, other arithmetic: 46.7 us -> none  [the longest x1 11.5 us: local_ranks(): return jnp.sum(running[priority] * choice_hits, axis=-1)]
    all_gather x1 -> x0, blocking collectives: 40.2 us -> none  [on_device(): every_count = lax.all_gather(counts[None], 'expert', axis=0, tiled=True)]
    scatter-add x2 -> x0, other arithmetic: 34.1 us -> none  [compact_rows(): gathered_rows.at[destination].add(arrived.reshape(-1, model_width))]
    convert_element_type x15 -> x11, other arithmetic: 30.1 us -> 11.6 us  [the longest x6 5.83 us: reduce(): return lax.psum(share, 'group').astype(FULL)]
  transfers between devices with their start and end apart: 10 -> 7, of which waited for: 6 -> 5; matrix products, arithmetic and copies ran while one was open for 28% -> 2% of each run, Pallas kernels for 0% -> 6%
where the time goes in v1:
time: 591 us; the launch traced here: 586 us
  waiting for transfers between devices  266 us (45%)
  Pallas kernels  204 us (35%)
  blocking collectives  80.2 us (14%)
  between operations  16.4 us (3%)
  other arithmetic  11.6 us (2%)
    reduce_scatter x2, waiting for transfers between devices, reduce(): lax.psum_scatter(x.astype(LOW), 'expert', scatter_dimension=0, tiled=True)  86.5 us
    reduce_scatter x1, waiting for transfers between devices, on_device_fast(): lax.psum_scatter(grad_inner[None], 'group', scatter_dimension=1, tiled=True)  85 us
    pallas_call x1, Pallas kernels, attn_dispatch(): pl.pallas_call(attn_dispatch_kernel, out_shape=(sds((seq_len, 3 * width),...  82.4 us
    reduce_scatter x1, waiting for transfers between devices, on_device_fast(): lax.psum_scatter(grad_outer[None], 'group', scatter_dimension=1, tiled=True)  56.7 us
    all_to_all x1, blocking collectives, on_device_fast(): lax.all_to_all(packed, 'expert', split_axis=0, concat_axis=0, tiled=True)  48.4 us
    all_to_all x1, waiting for transfers between devices, on_device_fast(): lax.all_to_all(packed_out, 'expert', split_axis=0, concat_axis=0, tiled=T...  36 us
    pallas_call x1, Pallas kernels, attn_back(): pl.pallas_call(attn_back_kernel, out_shape=(sds((seq_len, width), LOW), s...  35.1 us
    pallas_call x1, Pallas kernels, expert_second(): pl.pallas_call(expert_second_kernel, grid=(ff // FF_TILE,), out_shape=(sd...  27.2 us
  transfers between devices with their start and end apart: 7, of which 5 were waited for; matrix products, arithmetic and copies ran while one was open for 2% of the time, Pallas kernels for 6%

profile of v1, /device:TPU:8, one launch (start us, length us, event | category | flops | bytes accessed | tf_op | source)
XLA Modules:
  0.0 585.9 jit_solution(5091477992196106048)
XLA Ops:
  7.2 0.0 reduce-scatter.10.cloned.1.call-start
  7.9 82.4 %shard_map.222 = (bf16[512,2304]{1,0:T(8,128)(2,1)}, bf16[12,512,512]{2,1,0:T(8,128)(2,1)}, bf16[512,768]{1,0:T(8,128)(2,1)}, f32[512,768]{1,0:T(8,128)}, bf16[5...) custom-call(bf16[512,768]{1,0:T(8,128)(2,1)} %tokens_ref.3, ...), custom_call_target="tpu_custom_call" | custom-call | tf_op jit(solution)/shard_map/pallas_call | solution.py:481
  90.3 24.5 %shard_map.223 = (bf16[1280,3072]{1,0:T(8,128)(2,1)}, bf16[1280,3072]{1,0:T(8,128)(2,1)}, bf16[3072,768]{1,0:T(8,128)(2,1)}) custom-call(bf16[1280,768]{1,0:T(8,128)(2,1)} %get-tuple-element.35.rows_ref, bf16[1280,768]{1,0:T(8,128)(2,1)} %get-tuple-element.36.resg_ref, bf16[768,3072]{1,0:T(8,128)(2,1)} %bitcast.21), custom_call_target="tpu_custom_call" | custom-call | flops 12079595520 | bytes 41943040 | tf_op jit(solution)/shard_map/pallas_call | solution.py:562
  114.7 27.2 %shard_map.226 = (bf16[1280,3072]{1,0:T(8,128)(2,1)}, bf16[8,256,896]{2,1,0:T(8,128)(2,1)}) custom-call(bf16[1280,768]{1,0:T(8,128)(2,1)} %get-tuple-element.43.cot_ref, f32[1280,128]{1,0:T(8,128)} %get-tuple-element.44.gate_ref, bf16[1280,3072]{1,0:T(8,128)(2,1)} %get-tuple-element.37.act_ref, bf16[1280,3072]{1,0:T(8,128)(2,1)} %get-tuple-element.45.slope_ref, ...), custom_call_target="tpu_custom_call" | custom-call | flops 12079595520 | bytes 52428800 | tf_op jit(solution)/shard_map/pallas_call | solution.py:636
  142.0 48.4 %all_to_all.10 = bf16[8,256,896]{2,1,0:T(8,128)(2,1)} all-to-all(bf16[8,256,896]{2,1,0:T(8,128)(2,1)} %get-tuple-element.46), channel_id=1, replica_groups=mesh['group'=4,'expert'=8] {'expert'}, dimensions={0} | all-to-all | bytes 7340032 | tf_op jit(solution)/shard_map/all_to_all | solution.py:1013
  190.4 35.1 %shard_map.227 = (bf16[512,768]{1,0:T(8,128)(2,1)}, f32[1,768]{1,0:T(1,128)}, bf16[768,2304]{1,0:T(8,128)(2,1)}, bf16[768,768]{1,0:T(8,128)(2,1)}, f32[32,12]{1,...) custom-call(bf16[512,768]{1,0:T(8,128)(2,1)} %tokens_ref.3, bf16[512,768]{1,0:T(8,128)(2,1)} %cot_ref.3, ...), custom_call_target="tpu_custom_call" | custom-call | flops 20000000000 | bytes 31457280 | tf_op jit(solution)/shard_map/pallas_call | solution.py:931
  225.5 0.0 copy-start.1
  225.5 0.0 reduce-scatter.10.cloned.1.call-update
  225.5 0.0 reduce-scatter.8.cloned.1.call-start
  225.6 0.7 reduce-scatter.8.cloned.1.call-update
  226.3 0.0 reduce-scatter.16.cloned.1.call-start
  226.3 0.0 copy-done.1
  226.3 0.8 copy.25
  227.1 0.0 reduce-scatter.16.cloned.1.call-update
  227.2 0.0 all-reduce.8.cloned.1.call-start
  227.2 34.5 %reduce-scatter.10.cloned.1.call-done = bf16[96,768]{1,0:T(8,128)(2,1)} async-done(((bf16[768,768]{1,0:T(8,128)(2,1)}), bf16[96,768]{1,0:T(8,128)(2,1)}) %reduce-scatter.10.cloned.1.call-update) | async-done | bytes 147472 | tf_op jit(solution)/shard_map/reduce_scatter | solution.py:1040
  261.7 52.0 %reduce-scatter.8.cloned.1.call-done = bf16[96,2304]{1,0:T(8,128)(2,1)} async-done(((bf16[768,2304]{1,0:T(8,128)(2,1)}), bf16[96,2304]{1,0:T(8,128)(2,1)}) %reduce-scatter.8.cloned.1.call-update) | async-done | bytes 442384 | tf_op jit(solution)/shard_map/reduce_scatter | solution.py:1040
  313.7 0.0 all-reduce.8.cloned.1.call-update
  313.7 0.0 reduce-scatter.14.cloned.1.call-start
  313.8 0.5 reduce-scatter.14.cloned.1.call-update
  314.3 0.0 reduce-scatter.12.cloned.1.call-start
  314.4 11.6 %shard_map.228 = bf16[768,3072]{1,0:T(8,128)(2,1)} custom-call(bf16[1280,768]{1,0:T(8,128)(2,1)} %get-tuple-element.35.rows_ref, bf16[1280,3072]{1,0:T(8,128)(2,1)} %get-tuple-element.54.ig_ref), custom_call_target="tpu_custom_call" | custom-call | flops 6039797760 | bytes 15728640 | tf_op jit(solution)/shard_map/pallas_call | solution.py:679
  326.0 0.0 reduce-scatter.12.cloned.1.call-update
  326.1 16.1 %shard_map.224 = bf16[8,256,768]{2,1,0:T(8,128)(2,1)} custom-call(bf16[1280,3072]{1,0:T(8,128)(2,1)} %get-tuple-element.37.act_ref, bf16[3072,768]{1,0:T(8,128)(2,1)} %bitcast.24, f32[8,128]{1,0:T(8,128)} %get-tuple-element.38.info_ref), custom_call_target="tpu_custom_call" | custom-call | flops 6039797760 | bytes 20971520 | tf_op jit(solution)/shard_map/pallas_call | solution.py:716
  342.1 0.0 copy-start.5
  342.1 4.0 all-to-all-start
  346.1 0.0 copy-done.5
  346.1 0.6 dynamic-slice
  348.0 36.0 %all-to-all-done = bf16[8,256,768]{2,1,0:T(8,128)(2,1)S(1)} async-done(((bf16[8,256,768]{2,1,0:T(8,128)(2,1)}), bf16[8,256,768]{2,1,0:T(8,128)(2,1)S(1)}, u32[]{:S(2)}, u32[]{:S(2)}) %all-to-all-start) | async-done | bytes 3145760 | tf_op jit(solution)/shard_map/all_to_all | solution.py:1019
  384.1 0.0 copy-start
  384.1 1.7 copy-done
  385.8 0.0 copy-start.2
  385.8 0.0 copy-start.3
  385.8 0.0 copy-start.4
  385.8 6.9 %shard_map.225 = bf16[512,768]{1,0:T(8,128)(2,1)} custom-call(f32[512,768]{1,0:T(8,128)} %get-tuple-element.33.hidden_ref, f32[512,8]{1,0:T(8,128)} %get-tuple-element.34.token_ref, bf16[2048,768]{1,0:T(8,128)(2,1)} %bitcast.16), custom_call_target="tpu_custom_call" | custom-call | flops 3221225472 | bytes 6291456 | tf_op jit(solution)/shard_map/pallas_call | solution.py:753
  392.7 0.0 copy-done.2
  392.7 0.0 copy-done.3
  392.7 0.0 copy-done.4
  392.8 22.8 %all-reduce.3 = (bf16[768]{0:T(1024)(128)(2,1)S(1)}, bf16[32,12]{1,0:T(8,128)(2,1)S(1)}, bf16[768]{0:T(1024)(128)(2,1)S(1)}) all-reduce(bf16[768]{0:T(1024)(128)(2,1)S(1)} %get-tuple-element.66, bf16[32,12]{1,0:T(8,128)(2,1)S(1)} %convert_element_type.50, ...), channel_id=2, replica_groups=mesh['group'=4,'expert'=8] {'expert'}, use_global_device_ids=true, to_apply=%region_0.0.clone | all-reduce | flops 1920 | bytes 7680
  415.5 0.1 dynamic-slice.1
  415.6 0.1 dynamic-slice.5
  415.7 0.0 reduce-scatter.16.cloned.1.call-done
  415.7 0.8 copy.26
  416.5 9.0 %all-reduce.4 = (bf16[96]{0:T(256)(128)(2,1)S(1)}, bf16[4,12]{1,0:T(4,128)(2,1)S(1)}, bf16[96]{0:T(256)(128)(2,1)S(1)}, bf16[96,8]{0,1:T(8,128)(2,1)S(1)}) all-reduce(bf16[96]{0:T(256)(128)(2,1)S(1)} %dynamic-slice.1, bf16[4,12]{1,0:T(4,128)(2,1)S(1)} %constant_dynamic-slice_fusion, ...), channel_id=1, replica_groups=mesh['group'=4,'expert'=8] {'group'}, use_global_device_ids=true, to_apply=%region_1.0 | all-reduce | flops 1008 | bytes 4032 | tf_op jit(solution)/shard_map/psum | solution.py:1041
  425.5 0.5 convert_element_type.47
  426.0 0.5 convert_element_type.54
  426.5 0.6 convert_element_type.51
  427.1 0.6 convert_element_type.57
  427.7 0.0 all-reduce.8.cloned.1.call-done
  427.7 1.6 convert_element_type.49
  429.4 2.0 convert_element_type.48
  431.4 56.7 %reduce-scatter.14.cloned.1.call-done = bf16[1,768,768]{2,1,0:T(8,128)(2,1)} async-done(((bf16[1,3072,768]{2,1,0:T(8,128)(2,1)}), bf16[1,768,768]{2,1,0:T(8,128)(2,1)}) %reduce-scatter.14.cloned.1.call-update) | async-done | bytes 1179664 | tf_op jit(solution)/shard_map/reduce_scatter | solution.py:1009
  488.1 2.8 convert_element_type.59
  490.9 85.0 %reduce-scatter.12.cloned.1.call-done = bf16[1,192,3072]{2,1,0:T(8,128)(2,1)} async-done(((bf16[1,768,3072]{2,1,0:T(8,128)(2,1)}), bf16[1,192,3072]{2,1,0:T(8,128)(2,1)}) %reduce-scatter.12.cloned.1.call-update) | async-done | bytes 1179664 | tf_op jit(solution)/shard_map/reduce_scatter | solution.py:1015
  575.9 2.9 convert_element_type.58
  (4 shorter events, 0.0 us)
Async XLA Ops:
  7.2 254.5 %reduce-scatter.10.cloned.1.call-start = ((), (), s32[]{:S(2)}) async-start(), calls=%async_computation.8 | async-start | bytes 1327104 | tf_op jit(solution)/shard_map/reduce_scatter | solution.py:1040
  225.5 0.8 copy-start.1
  225.5 88.2 %reduce-scatter.8.cloned.1.call-start = ((), (), s32[]{:S(2)}) async-start(), calls=%async_computation.7 | async-start | bytes 3981312 | tf_op jit(solution)/shard_map/reduce_scatter | solution.py:1040
  226.3 189.4 %reduce-scatter.16.cloned.1.call-start = ((), (), s32[]{:S(2)}) async-start(), calls=%async_computation.11 | async-start | bytes 221184
  227.2 200.6 %all-reduce.8.cloned.1.call-start = ((), (), s32[]{:S(2)}) async-start(), calls=%async_computation.12 | async-start | bytes 1179648 | tf_op jit(solution)/shard_map/psum | solution.py:1041
  313.7 174.3 %reduce-scatter.14.cloned.1.call-start = ((), (), s32[]{:S(2)}) async-start(), calls=%async_computation.10 | async-start | bytes 5898240 | tf_op jit(solution)/shard_map/reduce_scatter | solution.py:1009
  314.3 261.6 %reduce-scatter.12.cloned.1.call-start = ((), (), s32[]{:S(2)}) async-start(), calls=%async_computation.9 | async-start | bytes 5898240 | tf_op jit(solution)/shard_map/reduce_scatter | solution.py:1015
  342.1 4.0 copy-start.5
  342.1 41.9 %all-to-all-start = ((bf16[8,256,768]{2,1,0:T(8,128)(2,1)}), bf16[8,256,768]{2,1,0:T(8,128)(2,1)S(1)}, u32[]{:S(2)}, u32[]{:S(2)}) async-start(bf16[8,256,768]{2,1,0:T(8,128)(2,1)} %shard_map.224), calls=%async_computation | async-start | bytes 6291456 | tf_op jit(solution)/shard_map/all_to_all | solution.py:1019
  384.1 1.7 copy-start
  385.8 7.0 %copy-start.2 = (f32[32,12]{1,0:T(8,128)S(1)}, f32[32,12]{1,0:T(8,128)}, u32[]{:S(2)}) copy-start(f32[32,12]{1,0:T(8,128)} %get-tuple-element.51) | copy-start | bytes 4612
  385.8 7.0 %copy-start.3 = (f32[1,768]{1,0:T(1,128)S(1)}, f32[1,768]{1,0:T(1,128)}, u32[]{:S(2)}) copy-start(f32[1,768]{1,0:T(1,128)} %get-tuple-element.48) | copy-start | bytes 9220
  385.8 7.0 %copy-start.4 = (f32[1,768]{1,0:T(1,128)S(1)}, f32[1,768]{1,0:T(1,128)}, u32[]{:S(2)}) copy-start(f32[1,768]{1,0:T(1,128)} %get-tuple-element.52) | copy-start | bytes 9220
Sparse Core Ops, SparseCore 0:
  225.6 36.0 reduce-scatter.9
  265.6 48.0 reduce-scatter.7
  317.6 33.5 reduce-scatter.15
  353.4 47.0 all-reduce.7
  402.7 85.3 reduce-scatter.13
  490.2 85.6 reduce-scatter.11

commit v2 on v1

--- a/solution.py
+++ b/solution.py
@@ -781,26 +781,148 @@
     wrouter_ref,
     onehot_ref,
     gtok_ref,
-    ggain1_ref,
-    gqkv_ref,
-    gproj_ref,
-    gtable_ref,
-    ggain2_ref,
-    grouter_ref,
+    dense_out,
+    small_out,
     hgrad_ref,
     mgrad_ref,
     mgrad_t,
+    normed_t,
     q_t,
     ds_ref,
     diag_ref,
     dk_t,
     dv_t,
     dqkv_ref,
+    part_ref,
+    pair_in,
+    chip_ref,
+    plane_in,
+    plane_ref,
+    group_in,
+    small_ref,
+    small_in,
+    small_plane,
+    small_group,
+    pair_sems,
+    plane_sems,
+    group_sems,
+    final_sems,
+    small_sems,
+    smallz_sems,
 ):
     seq_len, width = tokens_ref.shape
     experts = wrouter_ref.shape[0]
-    heads = prob_ref.shape[0]
+    chunks = part_ref.shape[0]
+    groups = group_in.shape[0]
     tile = 128
+    g = lax.axis_index("group")
+    me = lax.axis_index("expert")
+    parity = lax.rem(me, 2)
+    mine = lax.div(me, 2)
+    summer = [(c * (groups - 1)) % groups for c in range(chunks)]
+
+    def device(mask):
+        return (g, lax.bitwise_xor(me, mask))
+
+    barrier = pltpu.get_barrier_semaphore()
+    for mask in range(1, experts):
+        pl.semaphore_signal(barrier, inc=1, device_id=device(mask), device_id_type=MESH)
+    for step in range(1, groups):
+        pl.semaphore_signal(
+            barrier, inc=1, device_id=(lax.rem(g + step, groups), me), device_id_type=MESH
+        )
+    pl.semaphore_wait(barrier, experts - 1 + groups - 1)
+
+    def remote(src, dst, sems, at, where):
+        return pltpu.make_async_remote_copy(
+            src_ref=src,
+            dst_ref=dst,
+            send_sem=sems.at[(0, *at)],
+            recv_sem=sems.at[(1, *at)],
+            device_id=where,
+            device_id_type=MESH,
+        )
+
+    started = []
+
+    def go(copy):
+        copy.start()
+        started.append(copy)
+
+    def pair_send(c):
+        for chip in range(experts // 2):
+            other = 2 * chip + 1 - parity
+            go(remote(part_ref.at[c, other], pair_in.at[c, chip], pair_sems, (c, chip), device(1)))
+
+    def plane_send(c):
+        for chip in range(experts // 2):
+            remote(
+                part_ref.at[c, 0], pair_in.at[c, chip], pair_sems, (c, chip), device(1)
+            ).wait_recv()
+            total = part_ref[c, 2 * chip + parity].astype(FULL) + pair_in[c, chip].astype(FULL)
+            chip_ref[c, chip] = total.astype(LOW)
+        for other in range(1, experts // 2):
+            go(
+                remote(
+                    chip_ref.at[c, lax.bitwise_xor(mine, other)],
+                    plane_in.at[c, other - 1],
+                    plane_sems,
+                    (c, other - 1),
+                    device(2 * other),
+                )
+            )
+
+    def group_send(c):
+        total = chip_ref[c, mine].astype(FULL)
+        for other in range(1, experts // 2):
+            remote(
+                chip_ref.at[c, 0],
+                plane_in.at[c, other - 1],
+                plane_sems,
+                (c, other - 1),
+                device(2 * other),
+            ).wait_recv()
+            total = total + plane_in[c, other - 1].astype(FULL)
+        plane_ref[c] = total.astype(LOW)
+
+        @pl.when(g != summer[c])
+        def _():
+            remote(
+                plane_ref.at[c], group_in.at[g], group_sems, (g,), (jnp.int32(summer[c]), me)
+            ).start()
+
+    def final_send(c):
+        @pl.when(g == summer[c])
+        def _():
+            total = plane_ref[c].astype(FULL)
+            for step in range(1, groups):
+                src = lax.rem(g + step, groups)
+                remote(
+                    plane_ref.at[c], group_in.at[src], group_sems, (src,), (src, me)
+                ).wait_recv()
+                total = total + group_in[src].astype(FULL)
+            dense_out[c] = total.astype(LOW)
+            for step in range(1, groups):
+                where = (lax.rem(g + step, groups), me)
+                remote(dense_out.at[c], dense_out.at[c], final_sems, (c, step - 1), where).start()
+
+    def finish(c):
+        where = (lax.rem(g + 1, groups), me)
+        for step in range(1, groups):
+            copy = remote(dense_out.at[c], dense_out.at[c], final_sems, (c, step - 1), where)
+
+            @pl.when(g == summer[c])
+            def _():
+                copy.wait_send()
+
+            @pl.when(lax.rem(summer[c] + step, groups) == g)
+            def _():
+                copy.wait_recv()
+
+        @pl.when(g != summer[c])
+        def _():
+            remote(plane_ref.at[c], group_in.at[g], group_sems, (g,), where).wait_send()
+
     ggain2 = jnp.zeros((8, width), FULL)
     lg_t = []
     for row0 in range(0, seq_len, tile):
@@ -829,22 +951,29 @@
             ggain2 = ggain2 + ng[i * 8 : i * 8 + 8]
         scaled = ngrad * gain2_ref[...][None, :]
         proj = jnp.mean(scaled * unit, axis=1, keepdims=True)
-        hgrad_ref[rows, :] = cot_ref[rows, :].astype(FULL) + inv * (scaled - unit * proj)
-        mgrad_ref[rows, :] = dot_nt(hgrad_ref[rows, :].astype(LOW), wproj_ref[...]).astype(LOW)
-    ggain2_ref[...] = jnp.sum(ggain2, axis=0, keepdims=True)
+        hgrad = cot_ref[rows, :].astype(FULL) + inv * (scaled - unit * proj)
+        hgrad_ref[rows, :] = hgrad
+        mgrad_ref[rows, :] = dot_nt(hgrad.astype(LOW), wproj_ref[...]).astype(LOW)
+        x = tokens_ref[rows, :].astype(FULL)
+        inv = lax.rsqrt(jnp.mean(x * x, axis=1, keepdims=True) + EPS)
+        dqkv_ref[rows, :width] = (x * inv * gain1_ref[...][None, :]).astype(LOW)
+    ggain2 = jnp.sum(ggain2, axis=0, keepdims=True)
     logit_grad_t = jnp.concatenate(lg_t, axis=1).astype(LOW)
-    grouter_ref[...] = dot_nn(logit_grad_t, normed2_ref[...])
-    gproj_ref[...] = dot_nn(
-        jnp.transpose(mixed_ref[...]), hgrad_ref[...].astype(LOW)
-    ).astype(LOW)
+    grouter = dot_nn(logit_grad_t, normed2_ref[...])
+    normed_t[...] = jnp.transpose(dqkv_ref[:, :width])
+    part_ref[0] = (
+        dot_nn(jnp.transpose(mixed_ref[...]), hgrad_ref[...].astype(LOW))
+        .astype(LOW)
+        .reshape(experts, width // experts, width)
+    )
+    pair_send(0)
     mgrad_t[...] = jnp.transpose(mgrad_ref[...])
     q_t[...] = jnp.transpose(qkv_ref[:, :width])
     up = lax.broadcasted_iota(jnp.int32, (128, 128), 0)
     across = lax.broadcasted_iota(jnp.int32, (128, 128), 1)
     flip = jnp.where(up + across == 127, 1.0, 0.0).astype(FULL)
 
-    @pl.loop(0, width // 128)
-    def _(pair):
+    def heads_back(pair):
         col = pl.multiple_of(pair * 128, 128)
         kp = qkv_ref[:, pl.ds(width + col, 128)]
         vp = qkv_ref[:, pl.ds(2 * width + col, 128)]
@@ -898,9 +1027,32 @@
             dk_t[part, :] = (dot_nn(q_t[part, :], ds_ref[sub]) * 0.125).astype(LOW)
             dv_t[part, :] = dot_nn(mgrad_t[part, :], prob_ref[2 * pair + sub]).astype(LOW)
 
-    gtable_ref[...] = exact_nt(onehot_ref[...], diag_ref[...])
-    dqkv_ref[:, width : 2 * width] = jnp.transpose(dk_t[...])
-    dqkv_ref[:, 2 * width :] = jnp.transpose(dv_t[...])
+    stripe = width // (chunks - 1)
+    for c in range(1, chunks):
+        pairs = stripe // 128
+
+        @pl.loop((c - 1) * pairs, c * pairs)
+        def _(pair):
+            heads_back(pair)
+
+        col = (c - 1) * stripe
+        dqkv_ref[:, width + col : width + col + stripe] = jnp.transpose(dk_t[col : col + stripe, :])
+        dqkv_ref[:, 2 * width + col : 2 * width + col + stripe] = jnp.transpose(
+            dv_t[col : col + stripe, :]
+        )
+        for third in range(3):
+            here = third * width + col
+            part_ref[c, :, :, third * stripe : third * stripe + stripe] = (
+                dot_nn(normed_t[...], dqkv_ref[:, here : here + stripe])
+                .astype(LOW)
+                .reshape(experts, width // experts, stripe)
+            )
+        pair_send(c)
+        plane_send(c - 1)
+        if c >= 2:
+            group_send(c - 2)
+        if c >= 3:
+            final_send(c - 3)
 
     ggain1 = jnp.zeros((8, width), FULL)
     for row0 in range(0, seq_len, tile):
@@ -908,7 +1060,6 @@
         x = tokens_ref[rows, :].astype(FULL)
         inv = lax.rsqrt(jnp.mean(x * x, axis=1, keepdims=True) + EPS)
         unit = x * inv
-        mgrad_ref[rows, :] = (unit * gain1_ref[...][None, :]).astype(LOW)
         ngrad = dot_nt(dqkv_ref[rows, :], wqkv_ref[...])
         ng = ngrad * unit
         for i in range(tile // 8):
@@ -916,34 +1067,77 @@
         scaled = ngrad * gain1_ref[...][None, :]
         proj = jnp.mean(scaled * unit, axis=1, keepdims=True)
         gtok_ref[rows, :] = (hgrad_ref[rows, :] + inv * (scaled - unit * proj)).astype(LOW)
-    ggain1_ref[...] = jnp.sum(ggain1, axis=0, keepdims=True)
-    mgrad_t[...] = jnp.transpose(mgrad_ref[...])
-    gqkv_ref[...] = dot_nn(mgrad_t[...], dqkv_ref[...]).astype(LOW)
+        if row0 == 0:
+            plane_send(chunks - 1)
+        if row0 == tile:
+            group_send(chunks - 2)
+    ggain1 = jnp.sum(ggain1, axis=0, keepdims=True)
+
+    gtable = exact_nt(onehot_ref[...], diag_ref[...])
+    shard = width // experts
+    per = gtable.shape[0] // experts
+    for e in range(experts):
+        cols = slice(e * shard, e * shard + shard)
+        block = jnp.concatenate([ggain1[:, cols], ggain2[:, cols], grouter[:, cols]], axis=0)
+        small_ref[e] = jnp.zeros(small_ref.shape[1:], FULL)
+        small_ref[e, 0 : 2 + experts, 0:shard] = block
+        small_ref[e, 2 + experts : 2 + experts + per, 0 : gtable.shape[1]] = gtable[
+            e * per : e * per + per
+        ]
+    for mask in range(1, experts):
+        other = lax.bitwise_xor(me, mask)
+        go(remote(small_ref.at[other], small_in.at[mask], small_sems, (mask,), device(mask)))
+    group_send(chunks - 1)
+    final_send(chunks - 3)
+    total = small_ref[me]
+    for mask in range(1, experts):
+        remote(
+            small_ref.at[0], small_in.at[mask], small_sems, (mask,), device(mask)
+        ).wait_recv()
+        total = total + small_in[mask]
+    small_plane[...] = total
+    for step in range(1, groups):
+        where = (lax.rem(g + step, groups), me)
+        go(remote(small_plane, small_group.at[step], smallz_sems, (step,), where))
+    final_send(chunks - 2)
+    final_send(chunks - 1)
+    for step in range(1, groups):
+        remote(
+            small_plane, small_group.at[step], smallz_sems, (step,), (lax.rem(g + step, groups), me)
+        ).wait_recv()
+        total = total + small_group[step]
+    small_out[...] = total
+    for c in range(chunks):
+        finish(c)
+    for copy in started:
+        copy.wait_send()
 
 
 def attn_back(
-    tokens, cot, hidden, normed2, mixed, qkv, prob, recv, token, gain1, gain2, wqkv, wproj, wrouter, table
+    tokens, cot, hidden, normed2, mixed, qkv, prob, recv, token, gain1, gain2, wqkv, wproj, wrouter, table, groups
 ):
     seq_len, width = tokens.shape
     buckets, heads = table.shape
     experts = wrouter.shape[1]
+    shard = width // experts
+    chunks = groups
+    chips = experts // 2
+    small = (16, 128)
     sds = jax.ShapeDtypeStruct
+    dma = pltpu.SemaphoreType.DMA
     return pl.pallas_call(
         attn_back_kernel,
         out_shape=(
             sds((seq_len, width), LOW),
-            sds((1, width), FULL),
-            sds((width, 3 * width), LOW),
-            sds((width, width), LOW),
-            sds((buckets, heads), FULL),
-            sds((1, width), FULL),
-            sds((experts, width), FULL),
+            sds((chunks, shard, width), LOW),
+            sds(small, FULL),
         ),
         in_specs=[VM] * 15,
-        out_specs=[VM] * 7,
+        out_specs=[VM] * 3,
         scratch_shapes=[
             pltpu.VMEM((seq_len, width), FULL),
             pltpu.VMEM((seq_len, width), LOW),
+            pltpu.VMEM((width, seq_len), LOW),
             pltpu.VMEM((width, seq_len), LOW),
             pltpu.VMEM((width, seq_len), LOW),
             pltpu.VMEM((2, seq_len, seq_len), LOW),
@@ -951,10 +1145,28 @@
             pltpu.VMEM((width, seq_len), LOW),
             pltpu.VMEM((width, seq_len), LOW),
             pltpu.VMEM((seq_len, 3 * width), LOW),
+            pltpu.VMEM((chunks, experts, shard, width), LOW),
+            pltpu.VMEM((chunks, chips, shard, width), LOW),
+            pltpu.VMEM((chunks, chips, shard, width), LOW),
+            pltpu.VMEM((chunks, chips - 1, shard, width), LOW),
+            pltpu.VMEM((chunks, shard, width), LOW),
+            pltpu.VMEM((groups, shard, width), LOW),
+            pltpu.VMEM((experts, *small), FULL),
+            pltpu.VMEM((experts, *small), FULL),
+            pltpu.VMEM(small, FULL),
+            pltpu.VMEM((groups, *small), FULL),
+            dma((2, chunks, chips)),
+            dma((2, chunks, chips - 1)),
+            dma((2, groups)),
+            dma((2, chunks, groups - 1)),
+            dma((2, experts)),
+            dma((2, groups)),
         ],
-        compiler_params=pltpu.CompilerParams(vmem_limit_bytes=56 * MIB),
+        compiler_params=pltpu.CompilerParams(
+            vmem_limit_bytes=60 * MIB, collective_id=1, has_side_effects=True
+        ),
         cost_estimate=pl.CostEstimate(
-            flops=20_000_000_000, bytes_accessed=30 * MIB, transcendentals=0
+            flops=30_000_000_000, bytes_accessed=30 * MIB, transcendentals=0
         ),
     )(
         tokens,
@@ -1017,7 +1229,7 @@
     ).astype(FULL)
     packed_out = expert_result(act, w_out[0], info)
     back = lax.all_to_all(packed_out, "expert", split_axis=0, concat_axis=0, tiled=True)
-    gtok, ggain1, gqkv, gproj, gtable, ggain2, grouter = attn_back(
+    gtok, dense, small = attn_back(
         tokens,
         cotangent,
         hidden,
@@ -1033,22 +1245,25 @@
         w_proj,
         w_router,
         bias_table,
+        lax.axis_size("group"),
     )
     block_out = combine(hidden, token, back.reshape(-1, width))
-
-    def reduce(x):
-        share = lax.psum_scatter(x.astype(LOW), "expert", scatter_dimension=0, tiled=True)
-        return lax.psum(share, "group").astype(FULL)
-
+    shard = width // experts
+    heads = bias_table.shape[1]
+    per = bias_table.shape[0] // experts
+    stripe = width // (dense.shape[0] - 1)
+    grad_qkv = (
+        dense[1:].reshape(-1, shard, 3, stripe).transpose(1, 2, 0, 3).reshape(shard, 3 * width)
+    )
     return (
         block_out,
         gtok,
-        reduce(ggain1[0]),
-        reduce(gqkv),
-        reduce(gproj),
-        reduce(gtable),
-        reduce(ggain2[0]),
-        reduce(grouter.T),
+        small[0, :shard],
+        grad_qkv.astype(FULL),
+        dense[0].astype(FULL),
+        small[2 + experts : 2 + experts + per, :heads],
+        small[1, :shard],
+        small[2 : 2 + experts, :shard].T,
         grad_in,
         grad_out,
     )
@@ -1327,7 +1542,8 @@
 
 
 def solution(mesh):
-    step = on_device_fast if mesh.shape["expert"] == 8 else on_device
+    fast = (mesh.shape["group"], mesh.shape["expert"]) == (4, 8)
+    step = on_device_fast if fast else on_device
     return jax.shard_map(
         step,
         mesh=mesh,

time: 591 us -> 342 us (0.58)
  waiting for transfers between devices: 266 us -> 36.6 us
  blocking collectives: 80.2 us -> 0 us
  Pallas kernels: 204 us -> 261 us
    reduce_scatter x2 -> x0, waiting for transfers between devices: 86.5 us -> none  [reduce(): lax.psum_scatter(x.astype(LOW), 'expert', scatter_dimension=0, tiled=True)]
    reduce_scatter x1, waiting for transfers between devices: 85 us -> 0.01 us  [on_device_fast(): lax.psum_scatter(grad_inner[None], 'group', scatter_dimension=1, tiled=True)]
    reduce_scatter x1, waiting for transfers between devices: 56.7 us -> 0.01 us  [on_device_fast(): lax.psum_scatter(grad_outer[None], 'group', scatter_dimension=1, tiled=True)]
    pallas_call x1, Pallas kernels: 35.1 us -> 91 us  [attn_back(): pl.pallas_call(attn_back_kernel, out_shape=(sds((seq_len, width), LOW), s...]
    all_to_all x1 -> x0, blocking collectives: 48.4 us -> none  [on_device_fast(): lax.all_to_all(packed, 'expert', split_axis=0, concat_axis=0, tiled=True)]
    all_to_all x0 -> x1, waiting for transfers between devices: none -> 36.6 us  [on_device_fast(): lax.all_to_all(packed, 'expert', split_axis=0, concat_axis=0, tiled=True)]
    all_to_all x1, waiting for transfers between devices: 36 us -> 0.01 us  [on_device_fast(): lax.all_to_all(packed_out, 'expert', split_axis=0, concat_axis=0, tiled=T...]
    unnamed x1 -> x0, blocking collectives: 22.8 us -> none
  transfers between devices with their start and end apart: 7 -> 4, of which waited for: 5 -> 1; matrix products, arithmetic and copies ran while one was open for 2% -> 3% of each run, Pallas kernels for 6% -> 46%
where the time goes in v2:
time: 342 us; the launch traced here: 337 us
  Pallas kernels  261 us (76%)
  waiting for transfers between devices  36.6 us (11%)
  between operations  15 us (4%)
  other arithmetic  8.57 us (3%)
  starting transfers between devices  8.39 us (2%)
  local copies, waits for them, and re-layouts  7.56 us (2%)
    pallas_call x1, Pallas kernels, attn_back(): pl.pallas_call(attn_back_kernel, out_shape=(sds((seq_len, width), LOW), s...  91 us
    pallas_call x1, Pallas kernels, attn_dispatch(): pl.pallas_call(attn_dispatch_kernel, out_shape=(sds((seq_len, 3 * width),...  82.5 us
    all_to_all x1, waiting for transfers between devices, on_device_fast(): lax.all_to_all(packed, 'expert', split_axis=0, concat_axis=0, tiled=True)  36.6 us
    pallas_call x1, Pallas kernels, expert_second(): pl.pallas_call(expert_second_kernel, grid=(ff // FF_TILE,), out_shape=(sd...  27.8 us
    pallas_call x1, Pallas kernels, expert_first(): pl.pallas_call(expert_first_kernel, grid=(ff // FF_TILE,), out_shape=(sds...  24.4 us
    pallas_call x1, Pallas kernels, expert_result(): pl.pallas_call(expert_result_kernel, grid=(ff // FF_TILE,), out_shape=jax...  16.4 us
    pallas_call x1, Pallas kernels, expert_inner(): pl.pallas_call(expert_inner_kernel, grid=(ff // FF_TILE,), out_shape=jax....  11.6 us
    pallas_call x1, Pallas kernels, combine(): pl.pallas_call(combine_kernel, out_shape=jax.ShapeDtypeStruct(hidden.shap...  6.93 us
  transfers between devices with their start and end apart: 4, of which 1 were waited for; matrix products, arithmetic and copies ran while one was open for 3% of the time, Pallas kernels for 46%

profile of v2, /device:TPU:8, one launch (start us, length us, event | category | flops | bytes accessed | tf_op | source)
XLA Modules:
  0.0 336.8 jit_solution(3655290028660757417)
XLA Ops:
  7.2 0.0 reduce-scatter.5.cloned.1.call-start
  7.9 82.5 %shard_map.222 = (bf16[512,2304]{1,0:T(8,128)(2,1)}, bf16[12,512,512]{2,1,0:T(8,128)(2,1)}, bf16[512,768]{1,0:T(8,128)(2,1)}, f32[512,768]{1,0:T(8,128)}, bf16[5...) custom-call(bf16[512,768]{1,0:T(8,128)(2,1)} %tokens_ref.3, ...), custom_call_target="tpu_custom_call" | custom-call | tf_op jit(solution)/shard_map/pallas_call | solution.py:481
  90.4 24.4 %shard_map.223 = (bf16[1280,3072]{1,0:T(8,128)(2,1)}, bf16[1280,3072]{1,0:T(8,128)(2,1)}, bf16[3072,768]{1,0:T(8,128)(2,1)}) custom-call(bf16[1280,768]{1,0:T(8,128)(2,1)} %get-tuple-element.31.rows_ref, bf16[1280,768]{1,0:T(8,128)(2,1)} %get-tuple-element.32.resg_ref, bf16[768,3072]{1,0:T(8,128)(2,1)} %bitcast.27), custom_call_target="tpu_custom_call" | custom-call | flops 12079595520 | bytes 41943040 | tf_op jit(solution)/shard_map/pallas_call | solution.py:562
  114.8 0.0 reduce-scatter.5.cloned.1.call-update
  114.9 16.4 %shard_map.224 = bf16[8,256,768]{2,1,0:T(8,128)(2,1)} custom-call(bf16[1280,3072]{1,0:T(8,128)(2,1)} %get-tuple-element.33.act_ref, bf16[3072,768]{1,0:T(8,128)(2,1)} %bitcast.29, f32[8,128]{1,0:T(8,128)} %get-tuple-element.34.info_ref), custom_call_target="tpu_custom_call" | custom-call | flops 6039797760 | bytes 20971520 | tf_op jit(solution)/shard_map/pallas_call | solution.py:716
  131.3 3.6 %all-to-all-start = ((bf16[8,256,768]{2,1,0:T(8,128)(2,1)}), bf16[8,256,768]{2,1,0:T(8,128)(2,1)S(1)}, u32[]{:S(2)}, u32[]{:S(2)}) async-start(bf16[8,256,768]{2,1,0:T(8,128)(2,1)} %shard_map.224), calls=%async_computation | async-start | bytes 6291456 | tf_op jit(solution)/shard_map/all_to_all | solution.py:1231
  134.9 0.0 reduce-scatter.3.cloned.1.call-start
  135.0 27.8 %shard_map.226 = (bf16[1280,3072]{1,0:T(8,128)(2,1)}, bf16[8,256,896]{2,1,0:T(8,128)(2,1)}) custom-call(bf16[1280,768]{1,0:T(8,128)(2,1)} %get-tuple-element.39.cot_ref, f32[1280,128]{1,0:T(8,128)} %get-tuple-element.40.gate_ref, bf16[1280,3072]{1,0:T(8,128)(2,1)} %get-tuple-element.33.act_ref, bf16[1280,3072]{1,0:T(8,128)(2,1)} %get-tuple-element.41.slope_ref, ...), custom_call_target="tpu_custom_call" | custom-call | flops 12079595520 | bytes 52428800 | tf_op jit(solution)/shard_map/pallas_call | solution.py:636
  162.8 11.6 %shard_map.228 = bf16[768,3072]{1,0:T(8,128)(2,1)} custom-call(bf16[1280,768]{1,0:T(8,128)(2,1)} %get-tuple-element.31.rows_ref, bf16[1280,3072]{1,0:T(8,128)(2,1)} %get-tuple-element.46.ig_ref), custom_call_target="tpu_custom_call" | custom-call | flops 6039797760 | bytes 15728640 | tf_op jit(solution)/shard_map/pallas_call | solution.py:679
  174.4 0.0 reduce-scatter.3.cloned.1.call-update
  174.4 0.0 all-to-all-done
  174.4 0.0 copy-start
  174.4 1.7 copy-done
  176.1 4.7 %all-to-all-start.1 = ((bf16[8,256,896]{2,1,0:T(8,128)(2,1)}), bf16[8,256,896]{2,1,0:T(8,128)(2,1)}, u32[]{:S(2)}, u32[]{:S(2)}) async-start(bf16[8,256,896]{2,1,0:T(8,128)(2,1)} %get-tuple-element.42), calls=%async_computation.1 | async-start | bytes 7340032 | tf_op jit(solution)/shard_map/all_to_all | solution.py:1225
  180.8 6.9 %shard_map.225 = bf16[512,768]{1,0:T(8,128)(2,1)} custom-call(f32[512,768]{1,0:T(8,128)} %get-tuple-element.29.hidden_ref, f32[512,8]{1,0:T(8,128)} %get-tuple-element.30.token_ref, bf16[2048,768]{1,0:T(8,128)(2,1)} %bitcast.22), custom_call_target="tpu_custom_call" | custom-call | flops 3221225472 | bytes 6291456 | tf_op jit(solution)/shard_map/pallas_call | solution.py:753
  187.7 36.6 %all-to-all-done.1 = bf16[8,256,896]{2,1,0:T(8,128)(2,1)} async-done(((bf16[8,256,896]{2,1,0:T(8,128)(2,1)}), bf16[8,256,896]{2,1,0:T(8,128)(2,1)}, u32[]{:S(2)}, u32[]{:S(2)}) %all-to-all-start.1) | async-done | bytes 3670048 | tf_op jit(solution)/shard_map/all_to_all | solution.py:1225
  224.3 91.0 %shard_map.227 = (bf16[512,768]{1,0:T(8,128)(2,1)}, bf16[4,96,768]{2,1,0:T(8,128)(2,1)}, f32[16,128]{1,0:T(8,128)}) custom-call(bf16[512,768]{1,0:T(8,128)(2,1)} %tokens_ref.3, bf16[512,768]{1,0:T(8,128)(2,1)} %cot_ref.3, f32[512,768]{1,0:T(8,128)} %get-tuple-element.29.hidden_ref, bf16[512,768]{1,0:T(8,128)(2,1)} %get-tuple-element.35.normed2_ref, ...), custom_call_target="tpu_custom_call" | custom-call | flops 30000001024 | bytes 31457280 | tf_op jit(solution)/shard_map/pallas_call | solution.py:1128
  315.3 1.3 slice.21
  316.5 1.1 slice_convert_fusion
  317.6 0.0 copy-start.2
  317.6 0.5 reshape.38
  318.1 0.6 copy.26
  318.7 1.5 reshape.36
  320.2 0.0 copy-done.2
  320.2 0.5 slice_bitcast_fusion.1
  320.8 0.6 slice_bitcast_fusion
  321.4 1.6 bitcast_convert_fusion
  323.0 0.0 copy-start.1
  323.0 0.0 reduce-scatter.5.cloned.1.call-done
  323.0 2.9 convert_element_type.31
  325.9 0.0 reduce-scatter.3.cloned.1.call-done
  325.9 2.9 convert_element_type.30
  328.9 0.0 copy-done.1
  328.9 0.9 copy.29
Async XLA Ops:
  7.2 315.8 %reduce-scatter.5.cloned.1.call-start = ((), (), s32[]{:S(2)}) async-start(), calls=%async_computation.5 | async-start | bytes 5898240 | tf_op jit(solution)/shard_map/reduce_scatter | solution.py:1221
  131.3 43.2 %all-to-all-start = ((bf16[8,256,768]{2,1,0:T(8,128)(2,1)}), bf16[8,256,768]{2,1,0:T(8,128)(2,1)S(1)}, u32[]{:S(2)}, u32[]{:S(2)}) async-start(bf16[8,256,768]{2,1,0:T(8,128)(2,1)} %shard_map.224), calls=%async_computation | async-start | bytes 6291456 | tf_op jit(solution)/shard_map/all_to_all | solution.py:1231
  134.9 191.0 %reduce-scatter.3.cloned.1.call-start = ((), (), s32[]{:S(2)}) async-start(), calls=%async_computation.4 | async-start | bytes 5898240 | tf_op jit(solution)/shard_map/reduce_scatter | solution.py:1227
  174.4 1.7 copy-start
  176.1 48.2 %all-to-all-start.1 = ((bf16[8,256,896]{2,1,0:T(8,128)(2,1)}), bf16[8,256,896]{2,1,0:T(8,128)(2,1)}, u32[]{:S(2)}, u32[]{:S(2)}) async-start(bf16[8,256,896]{2,1,0:T(8,128)(2,1)} %get-tuple-element.42), calls=%async_computation.1 | async-start | bytes 7340032 | tf_op jit(solution)/shard_map/all_to_all | solution.py:1225
  317.6 2.6 copy-start.2
  323.0 5.9 %copy-start.1 = (bf16[512,768]{1,0:T(8,128)(2,1)S(1)}, bf16[512,768]{1,0:T(8,128)(2,1)}, u32[]{:S(2)}) copy-start(bf16[512,768]{1,0:T(8,128)(2,1)} %get-tuple-element.61) | copy-start | bytes 2359300
Sparse Core Ops, SparseCore 0:
  115.0 85.4 reduce-scatter.4
  202.8 107.1 reduce-scatter.2

commit v3 on v2

--- a/solution.py
+++ b/solution.py
@@ -23,7 +23,8 @@
 SECOND = 512.0
 SLOTS = 256
 ROW_TILE = 256
-FF_TILE = 512
+FF_TILE = 256
+THIRDS = 3
 
 
 def offset_bucket(offsets, buckets):
@@ -181,39 +182,46 @@
     routes_ref,
     prio_ref,
     span_ref,
+    win_ref,
     qkv_out,
     prob_out,
     mixed_out,
     hidden_out,
     normed2_out,
-    rows_ref,
-    cotrows_ref,
-    resg_ref,
-    gatecol_ref,
+    rows_out,
+    cotrows_out,
+    gatecol_out,
     token_ref,
     info_ref,
+    resgt_out,
+    act_out,
+    slope_out,
+    gout_out,
     qkv_ref,
     prob_ref,
     mixed_ref,
     hidden_ref,
     normed2_ref,
-    near_ref,
-    mask_ref,
     meta_ref,
     gate_ref,
     meta_all,
     gate_all,
     gat_c,
     gat_n,
-    acc_c,
-    acc_n,
     acc_g,
     pos_ref,
+    win_v,
+    rows_ref,
+    cotrows_ref,
+    gatecol_ref,
+    resgt_ref,
     send_sem,
     recv_sem,
     small_send,
     small_recv,
     out_sem,
+    in_sem,
+    tile_sem,
 ):
     g = lax.axis_index("group")
     me = lax.axis_index("expert")
@@ -248,9 +256,8 @@
     started = []
 
     def go(*args):
-        copy = send(*args)
-        copy.start()
-        started.append(copy)
+        send(*args).start()
+        started.append(functools.partial(send, *args))
 
     def arrived(which, mask, chunk):
         rows = pl.ds(chunk * half, half)
@@ -269,24 +276,32 @@
         go(which, 1, chunk, 0, 4)
         go(which, 2, chunk, 0, 1)
 
-    def relay(which):
-        arrived(which, 2, 0)
-        go(which, 3, 0, 2, 4)
-        arrived(which, 4, 1)
-        go(which, 3, 1, 4, 2)
-
-    def small(src, dst, index):
+    def own_out_all(which):
+        for chunk in range(2):
+            go(which, 0, chunk, 0, 2)
+            go(which, 1, 1 - chunk, 0, 4)
+        for chunk in range(2):
+            go(which, 2, chunk, 0, 1)
+
+    def relay(which, chunk, wait=True):
+        if wait:
+            arrived(which, 4 if chunk else 2, chunk)
+        go(which, 3, chunk, 4 if chunk else 2, 2 if chunk else 4)
+
+    def small_copy(src, dst, index, mask):
+        return pltpu.make_async_remote_copy(
+            src_ref=src,
+            dst_ref=dst.at[me],
+            send_sem=small_send.at[index, mask],
+            recv_sem=small_recv.at[index, mask],
+            device_id=device(mask),
+            device_id_type=MESH,
+        )
+
+    def small(*args):
         for mask in range(1, experts):
-            copy = pltpu.make_async_remote_copy(
-                src_ref=src,
-                dst_ref=dst.at[me],
-                send_sem=small_send.at[index, mask],
-                recv_sem=small_recv.at[index, mask],
-                device_id=device(mask),
-                device_id_type=MESH,
-            )
-            copy.start()
-            started.append(copy)
+            small_copy(*args, mask).start()
+            started.append(functools.partial(small_copy, *args, mask))
 
     def small_arrived(dst, index):
         for mask in range(1, experts):
@@ -300,8 +315,12 @@
                 device_id_type=MESH,
             ).wait_recv()
 
-    own_out(0, 0)
-    own_out(0, 1)
+    own_out_all(0)
+
+    def win_load():
+        return pltpu.make_async_copy(win_ref, win_v, in_sem.at[2])
+
+    win_load().start()
 
     hits = choice_hits(routes_ref[...], experts)
     ranks = ranks_by_priority(hits, prio_ref[...])
@@ -310,38 +329,61 @@
     meta_all[me] = meta
     small(meta_ref, meta_all, 0)
 
-    attn_setup(span_ref, table_ref, onehot_ref, near_ref, mask_ref)
-    for row0 in range(0, seq_len, 128):
-        rows = slice(row0, row0 + 128)
-        x = tokens_ref[rows, :].astype(FULL)
-        inv = lax.rsqrt(jnp.mean(x * x, axis=1, keepdims=True) + EPS)
-        n1 = (x * inv * gain1_ref[...][None, :]).astype(LOW)
-        qkv_ref[rows, :] = dot_nn(n1, wqkv_ref[...]).astype(LOW)
-    outs = [pltpu.make_async_copy(qkv_ref, qkv_out, out_sem.at[0])]
-    outs[0].start()
-
-    logits = []
-    for chunk in range(2):
-        row0 = chunk * half
-        rows = slice(row0, row0 + half)
-        attn_block(row0, half, qkv_ref, near_ref, mask_ref, prob_ref, mixed_ref)
-        hidden = tokens_ref[rows, :].astype(FULL) + dot_nn(mixed_ref[rows, :], wproj_ref[...])
-        hidden_ref[rows, :] = hidden
-        inv = lax.rsqrt(jnp.mean(hidden * hidden, axis=1, keepdims=True) + EPS)
-        n2 = (hidden * inv * gain2_ref[...][None, :]).astype(LOW)
-        normed2_ref[rows, :] = n2
-        own_out(1, chunk)
-        logits.append(dot_nt(wrouter_ref[...], n2))
-        if chunk == 0:
-            relay(0)
-    for index, (src, dst) in enumerate(
-        ((prob_ref, prob_out), (mixed_ref, mixed_out), (hidden_ref, hidden_out), (normed2_ref, normed2_out))
-    ):
-        copy = pltpu.make_async_copy(src, dst, out_sem.at[index + 1])
-        copy.start()
-        outs.append(copy)
-
-    logits = jnp.concatenate(logits, axis=1)
+    own_pairs = (
+        (qkv_ref, qkv_out),
+        (prob_ref, prob_out),
+        (mixed_ref, mixed_out),
+        (hidden_ref, hidden_out),
+        (normed2_ref, normed2_out),
+        (cotrows_ref, cotrows_out),
+        (rows_ref, rows_out),
+        (gatecol_ref, gatecol_out),
+        (resgt_ref, resgt_out),
+    )
+
+    def own_copy(index):
+        src, dst = own_pairs[index]
+        return pltpu.make_async_copy(src, dst, out_sem.at[index])
+
+    def attention(wqkv_v, wproj_v, near_ref, mask_ref):
+        loads = [
+            pltpu.make_async_copy(src, dst, in_sem.at[i])
+            for i, (src, dst) in enumerate(((wqkv_ref, wqkv_v), (wproj_ref, wproj_v)))
+        ]
+        for copy in loads:
+            copy.start()
+        attn_setup(span_ref, table_ref, onehot_ref, near_ref, mask_ref)
+        loads[0].wait()
+        for row0 in range(0, seq_len, 128):
+            rows = slice(row0, row0 + 128)
+            x = tokens_ref[rows, :].astype(FULL)
+            inv = lax.rsqrt(jnp.mean(x * x, axis=1, keepdims=True) + EPS)
+            n1 = (x * inv * gain1_ref[...][None, :]).astype(LOW)
+            qkv_ref[rows, :] = dot_nn(n1, wqkv_v[...]).astype(LOW)
+        own_copy(0).start()
+        loads[1].wait()
+        for chunk in range(2):
+            row0 = chunk * half
+            rows = slice(row0, row0 + half)
+            attn_block(row0, half, qkv_ref, near_ref, mask_ref, prob_ref, mixed_ref)
+            hidden = tokens_ref[rows, :].astype(FULL) + dot_nn(mixed_ref[rows, :], wproj_v[...])
+            hidden_ref[rows, :] = hidden
+            inv = lax.rsqrt(jnp.mean(hidden * hidden, axis=1, keepdims=True) + EPS)
+            n2 = (hidden * inv * gain2_ref[...][None, :]).astype(LOW)
+            normed2_ref[rows, :] = n2
+            own_out(1, chunk)
+
+    pl.run_scoped(
+        attention,
+        pltpu.VMEM(wqkv_ref.shape, LOW),
+        pltpu.VMEM(wproj_ref.shape, LOW),
+        pltpu.VMEM((table_ref.shape[0], 128, 384), FULL),
+        pltpu.VMEM((seq_len, seq_len), FULL),
+    )
+    for index in range(1, 5):
+        own_copy(index).start()
+
+    logits = dot_nt(wrouter_ref[...], normed2_ref[...])
     unnormed = jnp.exp(logits - jnp.max(logits, axis=0, keepdims=True))
     probabilities = unnormed / jnp.sum(unnormed, axis=0, keepdims=True)
     picked = [jnp.sum(jnp.where(hit, probabilities, 0.0), axis=0, keepdims=True) for hit in hits]
@@ -388,94 +430,150 @@
         jnp.where(lane == 1, counts[1], jnp.where(lane == 2, base[0], base[1])),
     )
 
-    acc_c[...] = jnp.zeros_like(acc_c)
-    acc_n[...] = jnp.zeros_like(acc_n)
-    acc_g[...] = jnp.zeros_like(acc_g)
-
-    def compact(which, mask, chunk):
+    accs = (cotrows_ref, rows_ref)
+
+    def compact(which, mask):
         slot = lax.bitwise_xor(me, mask)
-        cols = slice(chunk * half, chunk * half + half)
-        acc = (acc_c, acc_n)[which]
+        acc = accs[which]
 
         @pl.loop(0, acc.shape[0] // ROW_TILE)
         def _(tile):
             row0 = pl.multiple_of(tile * ROW_TILE, ROW_TILE)
-            place = pos_ref[pl.ds(slot, 1), :][:, cols] - row0.astype(FULL)
-            at = lax.broadcasted_iota(jnp.int32, (ROW_TILE, half), 0).astype(FULL)
-            pick = jnp.where(at == place, 1.0, 0.0).astype(LOW)
-            if mask == 0:
-                data = owns[which][cols, :]
-            else:
-                data = gats[which][slot, cols, :]
-            acc[pl.ds(row0, ROW_TILE), :] += dot_nn(pick, data)
+            here = pl.ds(row0, ROW_TILE)
+            place = pos_ref[pl.ds(slot, 1), :] - row0.astype(FULL)
+            at = lax.broadcasted_iota(jnp.int32, (ROW_TILE, seq_len), 0).astype(FULL)
+            hit = at == place
+            pick = jnp.where(hit, 1.0, 0.0).astype(LOW)
+            data = owns[which][...] if mask == 0 else gats[which][slot]
+            got = dot_nn(pick, data).astype(LOW)
+            if mask:
+                got = got + acc[here, :]
+            acc[here, :] = got
             if which == 1:
-                g_row = gate_all[slot, pl.ds(me, 1), :][:, cols]
-                terms = [jnp.broadcast_to(t.astype(FULL), (8, half)) for t in split3(g_row)]
-                third = lax.broadcasted_iota(jnp.int32, (8, half), 0)
-                mat = jnp.where(
-                    third == 0, terms[0], jnp.where(third == 1, terms[1], jnp.where(third == 2, terms[2], 0.0))
-                ).astype(LOW)
-                acc_g[pl.ds(row0, ROW_TILE), :] += dot_nt(pick, mat)
+                gates_here = jnp.where(hit, gate_all[slot, pl.ds(me, 1), :], 0.0)
+                part = gates_here[:, 0:128]
+                for i in range(1, seq_len // 128):
+                    part = part + gates_here[:, i * 128 : i * 128 + 128]
+                if mask:
+                    part = part + acc_g[here, :]
+                acc_g[here, :] = part
+
+    def forward(which, mask, waits=(0, 1)):
+        for chunk in waits:
+            arrived(which, mask, chunk)
+        for chunk in range(2):
+            go(which, 3 + mask // 2, chunk, mask, 1)
 
     def take(which, mask):
         for chunk in range(2):
-            if mask:
-                arrived(which, mask, chunk)
-        if mask in (2, 4, 6):
-            for chunk in range(2):
-                go(which, 2 + mask // 2 + 0 * chunk + 1, chunk, mask, 1)
-        for chunk in range(2):
-            compact(which, mask, chunk)
-
-    def take_relayed(which, mask, chunk_done):
-        arrived(which, mask, 1 - chunk_done)
-        for chunk in range(2):
-            go(which, 3 + mask // 2, chunk, mask, 1)
-        for chunk in range(2):
-            compact(which, mask, chunk)
-
-    take(0, 0)
+            arrived(which, mask, chunk)
+        compact(which, mask)
+
+    relay(0, 0)
+    relay(0, 1)
+    forward(0, 2, (1,))
+    forward(0, 4, (0,))
+    compact(0, 0)
     take(0, 1)
-    take_relayed(0, 2, 0)
-    take_relayed(0, 4, 1)
-    take(0, 6)
+    compact(0, 2)
+    compact(0, 4)
     take(0, 3)
     take(0, 5)
-    relay(1)
+    relay(1, 0)
+    relay(1, 1)
+    small_arrived(gate_all, 1)
+    compact(1, 0)
+    take(1, 1)
+    forward(1, 2, (1,))
+    compact(1, 2)
+    forward(1, 4, (0,))
+    compact(1, 4)
+    forward(0, 6)
+    compact(0, 6)
     take(0, 7)
-    small_arrived(gate_all, 1)
-    take(1, 0)
-    take(1, 1)
-    take_relayed(1, 2, 0)
-    take_relayed(1, 4, 1)
+    own_copy(5).start()
     take(1, 3)
     take(1, 5)
-    take(1, 6)
+    forward(1, 6)
+    compact(1, 6)
     take(1, 7)
-
-    @pl.loop(0, acc_n.shape[0] // ROW_TILE)
-    def _(tile):
-        rows = pl.ds(pl.multiple_of(tile * ROW_TILE, ROW_TILE), ROW_TILE)
-        cot_rows = acc_c[rows, :]
-        gate_col = jnp.sum(acc_g[rows, :], axis=1, keepdims=True)
-        rows_ref[rows, :] = acc_n[rows, :].astype(LOW)
-        cotrows_ref[rows, :] = cot_rows.astype(LOW)
-        resg_ref[rows, :] = (gate_col * cot_rows).astype(LOW)
-        gatecol_ref[rows, :] = jnp.broadcast_to(gate_col, (ROW_TILE, 128))
-
-    for copy in outs:
-        copy.wait()
+    own_copy(6).start()
+
+    capacity = rows_ref.shape[0]
+    tiles = gout_out.shape[0]
+
+    def experts_first(act_v, slope_v, gout_v):
+        def tile_copies(tile):
+            return [
+                pltpu.make_async_copy(src.at[tile], dst, tile_sem.at[kind, tile])
+                for kind, (src, dst) in enumerate(
+                    (
+                        (act_v, act_out.at[tile * THIRDS]),
+                        (slope_v, slope_out.at[tile * THIRDS]),
+                        (gout_v, gout_out.at[tile]),
+                    )
+                )
+            ]
+
+        win_load().wait()
+
+        def scaled(row0):
+            rows = pl.ds(pl.multiple_of(row0, ROW_TILE), ROW_TILE)
+            gate_col = jnp.sum(acc_g[rows, :], axis=1, keepdims=True)
+            gatecol_ref[rows, :] = jnp.broadcast_to(gate_col, (ROW_TILE, 128))
+            resg = gate_col * cotrows_ref[rows, :].astype(FULL)
+            resgt_ref[:, rows] = jnp.transpose(resg.astype(LOW))
+
+        parts = capacity // ROW_TILE
+
+        @pl.loop(0, tiles)
+        def _(tile):
+            cols = pl.ds(pl.multiple_of(tile * THIRDS * FF_TILE, FF_TILE), FF_TILE)
+            for row0 in range(0, capacity, ROW_TILE):
+                here = slice(row0, row0 + ROW_TILE)
+                act, slope = gelu_and_slope(dot_nn(rows_ref[here, :], win_v[:, cols]))
+                act_v[tile, here, :] = act.astype(LOW)
+                slope_v[tile, here, :] = slope.astype(LOW)
+            scaled(tile * ROW_TILE)
+            for copy in tile_copies(tile)[:2]:
+                copy.start()
+
+        for part in range(tiles, parts):
+            scaled(part * ROW_TILE)
+        own_copy(7).start()
+        own_copy(8).start()
+
+        @pl.loop(0, tiles)
+        def _(tile):
+            gout_v[tile] = dot_nn(resgt_ref[...], act_v[tile]).astype(LOW)
+            tile_copies(tile)[2].start()
+
+        @pl.loop(0, tiles)
+        def _(tile):
+            for copy in tile_copies(tile):
+                copy.wait()
+
+    pl.run_scoped(
+        experts_first,
+        pltpu.VMEM((tiles, capacity, FF_TILE), LOW),
+        pltpu.VMEM((tiles, capacity, FF_TILE), LOW),
+        pltpu.VMEM((tiles, width, FF_TILE), LOW),
+    )
+
+    for index in range(9):
+        own_copy(index).wait()
     for copy in started:
-        copy.wait_send()
+        copy().wait_send()
 
 
 def attn_dispatch(
-    tokens, cot, gain1, wqkv, wproj, table, gain2, wrouter, routes, priority, span
+    tokens, cot, gain1, wqkv, wproj, table, gain2, wrouter, routes, priority, span, w_in, groups
 ):
     seq_len, width = tokens.shape
     buckets, heads = table.shape
     experts = wrouter.shape[1]
     capacity = 5 * seq_len // 2
+    ff = w_in.shape[1]
     sds = jax.ShapeDtypeStruct
     dma = pltpu.SemaphoreType.DMA
     return pl.pallas_call(
@@ -488,36 +586,42 @@
             sds((seq_len, width), LOW),
             sds((capacity, width), LOW),
             sds((capacity, width), LOW),
-            sds((capacity, width), LOW),
             sds((capacity, 128), FULL),
             sds((seq_len, 8), FULL),
             sds((experts, 128), FULL),
+            sds((width, capacity), LOW),
+            sds((ff // FF_TILE, capacity, FF_TILE), LOW),
+            sds((ff // FF_TILE, capacity, FF_TILE), LOW),
+            sds((groups, width, FF_TILE), LOW),
         ),
-        in_specs=[VM] * 11 + [SM],
-        out_specs=[HBM] * 5 + [VM] * 6,
+        in_specs=[VM] * 3 + [HBM] * 2 + [VM] * 6 + [SM, HBM],
+        out_specs=[HBM] * 8 + [VM] * 2 + [HBM] * 4,
         scratch_shapes=[
             pltpu.VMEM((seq_len, 3 * width), LOW),
             pltpu.VMEM((heads, seq_len, seq_len), LOW),
             pltpu.VMEM((seq_len, width), LOW),
             pltpu.VMEM((seq_len, width), FULL),
             pltpu.VMEM((seq_len, width), LOW),
-            pltpu.VMEM((heads, 128, 384), FULL),
-            pltpu.VMEM((seq_len, seq_len), FULL),
             pltpu.VMEM((experts, seq_len), FULL),
             pltpu.VMEM((experts, seq_len), FULL),
             pltpu.VMEM((experts, experts, seq_len), FULL),
             pltpu.VMEM((experts, experts, seq_len), FULL),
             pltpu.VMEM((experts, seq_len, width), LOW),
             pltpu.VMEM((experts, seq_len, width), LOW),
-            pltpu.VMEM((capacity, width), FULL),
-            pltpu.VMEM((capacity, width), FULL),
-            pltpu.VMEM((capacity, 8), FULL),
+            pltpu.VMEM((capacity, 128), FULL),
             pltpu.VMEM((experts, seq_len), FULL),
+            pltpu.VMEM(w_in.shape, LOW),
+            pltpu.VMEM((capacity, width), LOW),
+            pltpu.VMEM((capacity, width), LOW),
+            pltpu.VMEM((capacity, 128), FULL),
+            pltpu.VMEM((width, capacity), LOW),
             dma((2, 7, 2)),
             dma((2, 8, 2)),
             dma((2, 8)),
             dma((2, 8)),
-            dma((5,)),
+            dma((9,)),
+            dma((3,)),
+            dma((3, groups)),
         ],
         compiler_params=pltpu.CompilerParams(
             vmem_limit_bytes=60 * MIB, collective_id=0, has_side_effects=True
@@ -535,233 +639,254 @@
         routes.T,
         priority,
         span,
-    )
-
-
-def expert_first_kernel(rows_ref, resg_ref, win_ref, act_ref, slope_ref, gout_ref):
-    pre = dot_nn(rows_ref[...], win_ref[...])
-    act, slope = gelu_and_slope(pre)
-    act_ref[...] = act.astype(LOW)
-    slope_ref[...] = slope.astype(LOW)
-    gout_ref[...] = dot_tn(act_ref[...], resg_ref[...]).astype(LOW)
+        w_in,
+    )
 
 
 def gelu_and_slope(x):
     c = math.sqrt(2.0 / math.pi)
     square = x * x
-    t = jnp.tanh(x * (c + (c * 0.044715) * square))
-    cdf = 0.5 + 0.5 * t
-    slope = cdf + (0.5 * x) * (1.0 - t * t) * (c + (3.0 * c * 0.044715) * square)
-    return x * cdf, slope
-
-
-def expert_first(rows, resg, w_in):
-    capacity, width = rows.shape
-    ff = w_in.shape[1]
-    sds = jax.ShapeDtypeStruct
-    return pl.pallas_call(
-        expert_first_kernel,
-        grid=(ff // FF_TILE,),
-        out_shape=(
-            sds((capacity, ff), LOW),
-            sds((capacity, ff), LOW),
-            sds((ff, width), LOW),
-        ),
-        in_specs=[
-            pl.BlockSpec((capacity, width), lambda f: (0, 0)),
-            pl.BlockSpec((capacity, width), lambda f: (0, 0)),
-            pl.BlockSpec((width, FF_TILE), lambda f: (0, f)),
-        ],
-        out_specs=[
-            pl.BlockSpec((capacity, FF_TILE), lambda f: (0, f)),
-            pl.BlockSpec((capacity, FF_TILE), lambda f: (0, f)),
-            pl.BlockSpec((FF_TILE, width), lambda f: (f, 0)),
-        ],
-        compiler_params=pltpu.CompilerParams(vmem_limit_bytes=56 * MIB),
-        cost_estimate=pl.CostEstimate(
-            flops=4 * capacity * width * ff, bytes_accessed=40 * MIB, transcendentals=capacity * ff
-        ),
-    )(rows, resg, w_in)
-
-
-def pack_rows(source, info_ref, data, out_ref, slots):
-    info = info_ref[source : source + 1, :]
+    s = 0.5 * jnp.tanh(x * (c + (c * 0.044715) * square)) + 0.5
+    act = x * s
+    return act, s + act * (1.0 - s) * (2.0 * c + (6.0 * c * 0.044715) * square)
+
+
+def pack_rows(source, info_ref, data, slots):
+    info = info_ref[pl.ds(source, 1), :]
     slot = lax.broadcasted_iota(jnp.int32, (slots, 1), 0).astype(FULL)
     n0, n1, b0, b1 = [info[:, i : i + 1] for i in range(4)]
     place = jnp.where(slot < n0, b0 + slot, jnp.where(slot < n0 + n1, b1 + slot - n0, -1.0))
     at = lax.broadcasted_iota(jnp.int32, (slots, data.shape[0]), 1).astype(FULL)
     pick = jnp.where(at == place, 1.0, 0.0).astype(LOW)
-    out_ref[source] = dot_nn(pick, data[...]).astype(LOW)
-
-
-def expert_second_kernel(
-    cot_ref, gate_ref, act_ref, slope_ref, wout_ref, win_ref, info_ref, ig_ref, packed_ref, acc_ref, gg_ref, data_ref
+    return dot_nn(pick, data[...]).astype(LOW)
+
+
+def expert_first_kernel(rows_ref, resgt_ref, win_ref, act_in, slope_in, act_ref, slope_ref, gout_ref):
+    for row0 in range(0, rows_ref.shape[0], ROW_TILE):
+        here = slice(row0, row0 + ROW_TILE)
+        act, slope = gelu_and_slope(dot_nn(rows_ref[here, :], win_ref[...]))
+        act_ref[0, here, :] = act.astype(LOW)
+        slope_ref[0, here, :] = slope.astype(LOW)
+    gout_ref[0, 0] = dot_nn(resgt_ref[...], act_ref[0]).astype(LOW)
+
+
+def expert_first(rows, resg_t, w_in, act, slope, groups):
+    capacity, width = rows.shape
+    rest = THIRDS - 1
+    sds = jax.ShapeDtypeStruct
+
+    def tile(i):
+        return i // rest * THIRDS + 1 + i % rest
+
+    return pl.pallas_call(
+        expert_first_kernel,
+        grid=(groups * rest,),
+        out_shape=(
+            sds(act.shape, LOW),
+            sds(slope.shape, LOW),
+            sds((groups, rest, width, FF_TILE), LOW),
+        ),
+        in_specs=[
+            pl.BlockSpec((capacity, width), lambda i: (0, 0)),
+            pl.BlockSpec((width, capacity), lambda i: (0, 0)),
+            pl.BlockSpec((width, FF_TILE), lambda i: (0, tile(i))),
+            HBM,
+            HBM,
+        ],
+        out_specs=[
+            pl.BlockSpec((1, capacity, FF_TILE), lambda i: (tile(i), 0, 0)),
+            pl.BlockSpec((1, capacity, FF_TILE), lambda i: (tile(i), 0, 0)),
+            pl.BlockSpec((1, 1, width, FF_TILE), lambda i: (i // rest, i % rest, 0, 0)),
+        ],
+        input_output_aliases={3: 0, 4: 1},
+        compiler_params=pltpu.CompilerParams(vmem_limit_bytes=56 * MIB),
+        cost_estimate=pl.CostEstimate(
+            flops=4 * capacity * width * FF_TILE * groups * rest,
+            bytes_accessed=30 * MIB,
+            transcendentals=capacity * FF_TILE * groups * rest,
+        ),
+    )(rows, resg_t, w_in, act, slope)
+
+
+def expert_back_kernel(
+    cot_ref,
+    gate_ref,
+    rows_ref,
+    info_ref,
+    act_ref,
+    slope_ref,
+    wout_ref,
+    win_ref,
+    recv_ref,
+    packed_ref,
+    gin_ref,
+    act_v,
+    slope_v,
+    wout_v,
+    win_v,
+    ig_v,
+    acc_ref,
+    gg_ref,
+    data_ref,
+    send_ref,
+    rows_t,
+    gin_v,
+    load_sem,
+    slope_sem,
+    gin_sem,
+    send_sem,
+    recv_sem,
 ):
-    step = pl.program_id(0)
+    g = lax.axis_index("group")
+    me = lax.axis_index("expert")
+    experts, slots, wide = send_ref.shape
+    tiles, capacity, tile_width = act_v.shape
     width = cot_ref.shape[1]
 
-    @pl.when(step == 0)
-    def _():
-        acc_ref[...] = jnp.zeros_like(acc_ref)
-        gg_ref[...] = jnp.zeros_like(gg_ref)
-
-    back = dot_nt(cot_ref[...], wout_ref[...])
-    part = act_ref[...].astype(FULL) * back
-    total = part[:, 0:128]
-    for i in range(1, part.shape[1] // 128):
-        total = total + part[:, i * 128 : i * 128 + 128]
-    gg_ref[...] += total
-    ig = (slope_ref[...].astype(FULL) * (gate_ref[:, 0:1] * back)).astype(LOW)
-    ig_ref[...] = ig
-    acc_ref[...] += dot_nt(ig, win_ref[...])
-
-    @pl.when(step == pl.num_programs(0) - 1)
-    def _():
-        data_ref[:, :width] = acc_ref[...].astype(LOW)
-        gg = jnp.sum(gg_ref[...], axis=1, keepdims=True)
-        hi, mid, low = [t.astype(FULL) for t in split3(gg)]
-        lane = lax.broadcasted_iota(jnp.int32, (gg.shape[0], 128), 1)
-        data_ref[:, width:] = jnp.where(
-            lane == 0, hi, jnp.where(lane == 1, mid, jnp.where(lane == 2, low, 0.0))
-        ).astype(LOW)
-        for source in range(packed_ref.shape[0]):
-            pack_rows(source, info_ref, data_ref, packed_ref, packed_ref.shape[1])
-
-
-def expert_second(cot_rows, gate_col, act, slope, w_out, w_in, info):
+    def device(mask):
+        return (g, lax.bitwise_xor(me, mask))
+
+    def load(index):
+        src, dst = ((wout_ref, wout_v), (win_ref, win_v), (act_ref, act_v))[index]
+        return pltpu.make_async_copy(src, dst, load_sem.at[index])
+
+    def slope_load(tile):
+        slot = lax.rem(tile, 2)
+        return pltpu.make_async_copy(slope_ref.at[tile], slope_v.at[slot], slope_sem.at[slot])
+
+    load(0).start()
+    slope_load(0).start()
+    load(2).start()
+    load(1).start()
+    barrier = pltpu.get_barrier_semaphore()
+    for mask in range(1, experts):
+        pl.semaphore_signal(barrier, inc=1, device_id=device(mask), device_id_type=MESH)
+    pl.semaphore_wait(barrier, experts - 1)
+    acc_ref[...] = jnp.zeros_like(acc_ref)
+    gg_ref[...] = jnp.zeros_like(gg_ref)
+    for index in range(3):
+        load(index).wait()
+
+    def span(tile):
+        return pl.ds(pl.multiple_of(tile * tile_width, tile_width), tile_width)
+
+    @pl.loop(0, tiles)
+    def _(tile):
+        slope_load(tile).wait()
+
+        @pl.when(tile + 1 < tiles)
+        def _():
+            slope_load(tile + 1).start()
+
+        for row0 in range(0, capacity, ROW_TILE):
+            here = slice(row0, row0 + ROW_TILE)
+            back = dot_nt(cot_ref[here, :], wout_v[span(tile), :])
+            part = act_v[tile, here, :].astype(FULL) * back
+            gg_ref[here, :] += part[:, 0:128] + part[:, 128:256]
+            slope = slope_v[lax.rem(tile, 2), here, :].astype(FULL)
+            ig_v[tile, here, :] = (slope * (gate_ref[here, 0:1] * back)).astype(LOW)
+            acc_ref[here, :] += dot_nt(ig_v[tile, here, :], win_v[:, span(tile)])
+
+    data_ref[:, :width] = acc_ref[...].astype(LOW)
+    gg = jnp.sum(gg_ref[...], axis=1, keepdims=True)
+    hi, mid, low = [t.astype(FULL) for t in split3(gg)]
+    lane = lax.broadcasted_iota(jnp.int32, (capacity, 128), 1)
+    data_ref[:, width:] = jnp.where(
+        lane == 0, hi, jnp.where(lane == 1, mid, jnp.where(lane == 2, low, 0.0))
+    ).astype(LOW)
+
+    def exchange(mask):
+        return pltpu.make_async_remote_copy(
+            src_ref=send_ref.at[lax.bitwise_xor(me, mask)],
+            dst_ref=recv_ref.at[me],
+            send_sem=send_sem.at[mask],
+            recv_sem=recv_sem.at[mask],
+            device_id=device(mask),
+            device_id_type=MESH,
+        )
+
+    for mask in (6, 7, 2, 4, 3, 5, 1):
+        other = lax.bitwise_xor(me, mask)
+        send_ref[other] = pack_rows(other, info_ref, data_ref, slots)
+        exchange(mask).start()
+    recv_ref[me] = pack_rows(me, info_ref, data_ref, slots)
+
+    rows_t[...] = jnp.transpose(rows_ref[...])
+
+    def gin_copy(tile):
+        slot = lax.rem(tile, 2)
+        return pltpu.make_async_copy(gin_v.at[slot], gin_ref.at[:, span(tile)], gin_sem.at[slot])
+
+    @pl.loop(0, tiles)
+    def _(tile):
+        @pl.when(tile >= 2)
+        def _():
+            gin_copy(tile).wait()
+
+        gin_v[lax.rem(tile, 2)] = dot_nn(rows_t[...], ig_v[tile]).astype(LOW)
+        gin_copy(tile).start()
+
+    acc_ref[...] = jnp.zeros_like(acc_ref)
+
+    @pl.loop(0, tiles)
+    def _(tile):
+        for row0 in range(0, capacity, ROW_TILE):
+            here = slice(row0, row0 + ROW_TILE)
+            acc_ref[here, :] += dot_nn(act_v[tile, here, :], wout_v[span(tile), :])
+
+    gin_copy(0).wait()
+    gin_copy(1).wait()
+    data_ref[:, :width] = acc_ref[...].astype(LOW)
+
+    @pl.loop(0, experts)
+    def _(source):
+        packed_ref[source] = pack_rows(source, info_ref, data_ref.at[:, 0:width], slots)
+
+    for mask in range(1, experts):
+        exchange(mask).wait()
+
+
+def expert_back(cot_rows, gate_col, rows, info, act, slope, w_out, w_in):
     capacity, width = cot_rows.shape
+    tiles, _, tile_width = act.shape
     ff = w_in.shape[1]
     experts = info.shape[0]
     sds = jax.ShapeDtypeStruct
+    dma = pltpu.SemaphoreType.DMA
     return pl.pallas_call(
-        expert_second_kernel,
-        grid=(ff // FF_TILE,),
+        expert_back_kernel,
         out_shape=(
-            sds((capacity, ff), LOW),
             sds((experts, SLOTS, width + 128), LOW),
+            sds((experts, SLOTS, width), LOW),
+            sds((width, ff), LOW),
         ),
-        in_specs=[
-            pl.BlockSpec((capacity, width), lambda f: (0, 0)),
-            pl.BlockSpec((capacity, 128), lambda f: (0, 0)),
-            pl.BlockSpec((capacity, FF_TILE), lambda f: (0, f)),
-            pl.BlockSpec((capacity, FF_TILE), lambda f: (0, f)),
-            pl.BlockSpec((FF_TILE, width), lambda f: (f, 0)),
-            pl.BlockSpec((width, FF_TILE), lambda f: (0, f)),
-            pl.BlockSpec((experts, 128), lambda f: (0, 0)),
-        ],
-        out_specs=[
-            pl.BlockSpec((capacity, FF_TILE), lambda f: (0, f)),
-            pl.BlockSpec((experts, SLOTS, width + 128), lambda f: (0, 0, 0)),
-        ],
+        in_specs=[VM] * 4 + [HBM] * 4,
+        out_specs=[VM, VM, HBM],
         scratch_shapes=[
+            pltpu.VMEM(act.shape, LOW),
+            pltpu.VMEM((2, capacity, tile_width), LOW),
+            pltpu.VMEM(w_out.shape, LOW),
+            pltpu.VMEM(w_in.shape, LOW),
+            pltpu.VMEM(act.shape, LOW),
             pltpu.VMEM((capacity, width), FULL),
             pltpu.VMEM((capacity, 128), FULL),
             pltpu.VMEM((capacity, width + 128), LOW),
+            pltpu.VMEM((experts, SLOTS, width + 128), LOW),
+            pltpu.VMEM((width, capacity), LOW),
+            pltpu.VMEM((2, width, tile_width), LOW),
+            dma((3,)),
+            dma((2,)),
+            dma((2,)),
+            dma((experts,)),
+            dma((experts,)),
         ],
-        compiler_params=pltpu.CompilerParams(vmem_limit_bytes=56 * MIB),
+        compiler_params=pltpu.CompilerParams(
+            vmem_limit_bytes=60 * MIB, collective_id=2, has_side_effects=True
+        ),
         cost_estimate=pl.CostEstimate(
-            flops=4 * capacity * width * ff, bytes_accessed=50 * MIB, transcendentals=0
+            flops=8 * capacity * width * ff + 30_000_000_000, bytes_accessed=50 * MIB, transcendentals=0
         ),
-    )(cot_rows, gate_col, act, slope, w_out, w_in, info)
-
-
-def expert_inner_kernel(rows_ref, ig_ref, gin_ref, rows_t):
-    @pl.when(pl.program_id(0) == 0)
-    def _():
-        rows_t[...] = jnp.transpose(rows_ref[...])
-
-    gin_ref[...] = dot_nn(rows_t[...], ig_ref[...]).astype(LOW)
-
-
-def expert_inner(rows, ig):
-    capacity, width = rows.shape
-    ff = ig.shape[1]
-    return pl.pallas_call(
-        expert_inner_kernel,
-        grid=(ff // FF_TILE,),
-        out_shape=jax.ShapeDtypeStruct((width, ff), LOW),
-        in_specs=[
-            pl.BlockSpec((capacity, width), lambda f: (0, 0)),
-            pl.BlockSpec((capacity, FF_TILE), lambda f: (0, f)),
-        ],
-        out_specs=pl.BlockSpec((width, FF_TILE), lambda f: (0, f)),
-        scratch_shapes=[pltpu.VMEM((width, capacity), LOW)],
-        compiler_params=pltpu.CompilerParams(vmem_limit_bytes=56 * MIB),
-        cost_estimate=pl.CostEstimate(
-            flops=2 * capacity * width * ff, bytes_accessed=15 * MIB, transcendentals=0
-        ),
-    )(rows, ig)
-
-
-def expert_result_kernel(act_ref, wout_ref, info_ref, packed_ref, acc_ref, data_ref):
-    step = pl.program_id(0)
-
-    @pl.when(step == 0)
-    def _():
-        acc_ref[...] = jnp.zeros_like(acc_ref)
-
-    acc_ref[...] += dot_nn(act_ref[...], wout_ref[...])
-
-    @pl.when(step == pl.num_programs(0) - 1)
-    def _():
-        data_ref[...] = acc_ref[...].astype(LOW)
-        for source in range(packed_ref.shape[0]):
-            pack_rows(source, info_ref, data_ref, packed_ref, packed_ref.shape[1])
-
-
-def expert_result(act, w_out, info):
-    capacity, ff = act.shape
-    width = w_out.shape[1]
-    experts = info.shape[0]
-    return pl.pallas_call(
-        expert_result_kernel,
-        grid=(ff // FF_TILE,),
-        out_shape=jax.ShapeDtypeStruct((experts, SLOTS, width), LOW),
-        in_specs=[
-            pl.BlockSpec((capacity, FF_TILE), lambda f: (0, f)),
-            pl.BlockSpec((FF_TILE, width), lambda f: (f, 0)),
-            pl.BlockSpec((experts, 128), lambda f: (0, 0)),
-        ],
-        out_specs=pl.BlockSpec((experts, SLOTS, width), lambda f: (0, 0, 0)),
-        scratch_shapes=[pltpu.VMEM((capacity, width), FULL), pltpu.VMEM((capacity, width), LOW)],
-        compiler_params=pltpu.CompilerParams(vmem_limit_bytes=56 * MIB),
-        cost_estimate=pl.CostEstimate(
-            flops=2 * capacity * width * ff, bytes_accessed=20 * MIB, transcendentals=0
-        ),
-    )(act, w_out, info)
-
-
-def slot_picks(token_ref, slots):
-    at = lax.broadcasted_iota(jnp.int32, (token_ref.shape[0], slots), 1).astype(FULL)
-    return [jnp.where(at == token_ref[:, k : k + 1], 1.0, 0.0) for k in range(2)]
-
-
-def combine_kernel(hidden_ref, token_ref, back_ref, out_ref):
-    rows = 128
-    width = hidden_ref.shape[1]
-    for row0 in range(0, hidden_ref.shape[0], rows):
-        here = slice(row0, row0 + rows)
-        token = token_ref[here, :]
-        at = lax.broadcasted_iota(jnp.int32, (rows, back_ref.shape[0]), 1).astype(FULL)
-        picks = [jnp.where(at == token[:, k : k + 1], 1.0, 0.0).astype(LOW) for k in range(2)]
-        got = dot_nn(jnp.concatenate(picks, axis=0), back_ref[...])
-        out = hidden_ref[here, :] + token[:, 2:3] * got[:rows] + token[:, 3:4] * got[rows:]
-        out_ref[here, :] = out.astype(LOW)
-
-
-def combine(hidden, token, back):
-    return pl.pallas_call(
-        combine_kernel,
-        out_shape=jax.ShapeDtypeStruct(hidden.shape, LOW),
-        in_specs=[VM] * 3,
-        out_specs=VM,
-        compiler_params=pltpu.CompilerParams(vmem_limit_bytes=56 * MIB),
-        cost_estimate=pl.CostEstimate(
-            flops=4 * hidden.shape[0] * hidden.shape[1] * back.shape[0],
-            bytes_accessed=6 * MIB,
-            transcendentals=0,
-        ),
-    )(hidden, token, back)
+    )(cot_rows, gate_col, rows, info, act, slope, w_out, w_in)
 
 
 def attn_back_kernel(
@@ -770,16 +895,18 @@
     hidden_ref,
     normed2_ref,
     mixed_ref,
-    qkv_ref,
-    prob_ref,
+    qkv_hbm,
+    prob_hbm,
     recv_ref,
     token_ref,
     gain1_ref,
     gain2_ref,
-    wqkv_ref,
+    wqkv_hbm,
     wproj_ref,
     wrouter_ref,
     onehot_ref,
+    result_ref,
+    block_ref,
     gtok_ref,
     dense_out,
     small_out,
@@ -803,6 +930,12 @@
     small_in,
     small_plane,
     small_group,
+    qkv_ref,
+    prob_ref,
+    wqkv_ref,
+    back_ref,
+    load_sems,
+    back_sems,
     pair_sems,
     plane_sems,
     group_sems,
@@ -813,17 +946,25 @@
     seq_len, width = tokens_ref.shape
     experts = wrouter_ref.shape[0]
     chunks = part_ref.shape[0]
-    groups = group_in.shape[0]
+    groups = group_in.shape[1]
     tile = 128
     g = lax.axis_index("group")
     me = lax.axis_index("expert")
     parity = lax.rem(me, 2)
     mine = lax.div(me, 2)
-    summer = [(c * (groups - 1)) % groups for c in range(chunks)]
+    summer = [groups // 2 - 1 + c % 2 for c in range(chunks)]
 
     def device(mask):
         return (g, lax.bitwise_xor(me, mask))
 
+    def load(index):
+        src, dst = ((qkv_hbm, qkv_ref), (prob_hbm, prob_ref), (wqkv_hbm, wqkv_ref))[index]
+        return pltpu.make_async_copy(src, dst, load_sems.at[index])
+
+    own_result = pltpu.make_async_copy(result_ref.at[me], back_ref.at[me], load_sems.at[3])
+    for index in range(3):
+        load(index).start()
+    own_result.start()
     barrier = pltpu.get_barrier_semaphore()
     for mask in range(1, experts):
         pl.semaphore_signal(barrier, inc=1, device_id=device(mask), device_id_type=MESH)
@@ -848,6 +989,13 @@
     def go(copy):
         copy.start()
         started.append(copy)
+
+    def result_copy(mask):
+        other = lax.bitwise_xor(me, mask)
+        return remote(result_ref.at[other], back_ref.at[me], back_sems, (mask,), device(mask))
+
+    for mask in (2, 4, 3, 5, 1):
+        result_copy(mask).start()
 
     def pair_send(c):
         for chip in range(experts // 2):
@@ -888,7 +1036,7 @@
         @pl.when(g != summer[c])
         def _():
             remote(
-                plane_ref.at[c], group_in.at[g], group_sems, (g,), (jnp.int32(summer[c]), me)
+                plane_ref.at[c], group_in.at[c, g], group_sems, (c, g), (jnp.int32(summer[c]), me)
             ).start()
 
     def final_send(c):
@@ -898,9 +1046,9 @@
             for step in range(1, groups):
                 src = lax.rem(g + step, groups)
                 remote(
-                    plane_ref.at[c], group_in.at[src], group_sems, (src,), (src, me)
+                    plane_ref.at[c], group_in.at[c, src], group_sems, (c, src), (src, me)
                 ).wait_recv()
-                total = total + group_in[src].astype(FULL)
+                total = total + group_in[c, src].astype(FULL)
             dense_out[c] = total.astype(LOW)
             for step in range(1, groups):
                 where = (lax.rem(g + step, groups), me)
@@ -921,7 +1069,7 @@
 
         @pl.when(g != summer[c])
         def _():
-            remote(plane_ref.at[c], group_in.at[g], group_sems, (g,), where).wait_send()
+            remote(plane_ref.at[c], group_in.at[c, g], group_sems, (c, g), where).wait_send()
 
     ggain2 = jnp.zeros((8, width), FULL)
     lg_t = []
@@ -968,7 +1116,9 @@
     )
     pair_send(0)
     mgrad_t[...] = jnp.transpose(mgrad_ref[...])
+    load(0).wait()
     q_t[...] = jnp.transpose(qkv_ref[:, :width])
+    load(1).wait()
     up = lax.broadcasted_iota(jnp.int32, (128, 128), 0)
     across = lax.broadcasted_iota(jnp.int32, (128, 128), 1)
     flip = jnp.where(up + across == 127, 1.0, 0.0).astype(FULL)
@@ -1051,9 +1201,8 @@
         plane_send(c - 1)
         if c >= 2:
             group_send(c - 2)
-        if c >= 3:
-            final_send(c - 3)
-
+
+    load(2).wait()
     ggain1 = jnp.zeros((8, width), FULL)
     for row0 in range(0, seq_len, tile):
         rows = slice(row0, row0 + tile)
@@ -1069,8 +1218,8 @@
         gtok_ref[rows, :] = (hgrad_ref[rows, :] + inv * (scaled - unit * proj)).astype(LOW)
         if row0 == 0:
             plane_send(chunks - 1)
-        if row0 == tile:
-            group_send(chunks - 2)
+            for mask in (6, 7):
+                result_copy(mask).start()
     ggain1 = jnp.sum(ggain1, axis=0, keepdims=True)
 
     gtable = exact_nt(onehot_ref[...], diag_ref[...])
@@ -1087,8 +1236,8 @@
     for mask in range(1, experts):
         other = lax.bitwise_xor(me, mask)
         go(remote(small_ref.at[other], small_in.at[mask], small_sems, (mask,), device(mask)))
-    group_send(chunks - 1)
-    final_send(chunks - 3)
+    final_send(0)
+    group_send(2)
     total = small_ref[me]
     for mask in range(1, experts):
         remote(
@@ -1099,8 +1248,27 @@
     for step in range(1, groups):
         where = (lax.rem(g + step, groups), me)
         go(remote(small_plane, small_group.at[step], smallz_sems, (step,), where))
-    final_send(chunks - 2)
-    final_send(chunks - 1)
+    final_send(1)
+    group_send(3)
+    own_result.wait()
+    for mask in range(1, experts):
+        result_copy(mask).wait()
+
+    @pl.loop(0, seq_len // tile)
+    def _(step):
+        rows = pl.ds(pl.multiple_of(step * tile, tile), tile)
+        token = token_ref[rows, :]
+        at = lax.broadcasted_iota(jnp.int32, (tile, experts * SLOTS), 1).astype(FULL)
+        picks = [jnp.where(at == token[:, k : k + 1], 1.0, 0.0).astype(LOW) for k in range(2)]
+        got = dot_nn(
+            jnp.concatenate(picks, axis=0), back_ref[...].reshape(experts * SLOTS, width)
+        )
+        block_ref[rows, :] = (
+            hidden_ref[rows, :] + token[:, 2:3] * got[:tile] + token[:, 3:4] * got[tile:]
+        ).astype(LOW)
+
+    final_send(2)
+    final_send(3)
     for step in range(1, groups):
         remote(
             small_plane, small_group.at[step], smallz_sems, (step,), (lax.rem(g + step, groups), me)
@@ -1114,7 +1282,7 @@
 
 
 def attn_back(
-    tokens, cot, hidden, normed2, mixed, qkv, prob, recv, token, gain1, gain2, wqkv, wproj, wrouter, table, groups
+    tokens, cot, hidden, normed2, mixed, qkv, prob, recv, token, gain1, gain2, wqkv, wproj, wrouter, table, result, groups
 ):
     seq_len, width = tokens.shape
     buckets, heads = table.shape
@@ -1129,11 +1297,12 @@
         attn_back_kernel,
         out_shape=(
             sds((seq_len, width), LOW),
+            sds((seq_len, width), LOW),
             sds((chunks, shard, width), LOW),
             sds(small, FULL),
         ),
-        in_specs=[VM] * 15,
-        out_specs=[VM] * 3,
+        in_specs=[VM] * 5 + [HBM] * 2 + [VM] * 4 + [HBM] + [VM] * 3 + [HBM],
+        out_specs=[VM] * 4,
         scratch_shapes=[
             pltpu.VMEM((seq_len, width), FULL),
             pltpu.VMEM((seq_len, width), LOW),
@@ -1150,14 +1319,20 @@
             pltpu.VMEM((chunks, chips, shard, width), LOW),
             pltpu.VMEM((chunks, chips - 1, shard, width), LOW),
             pltpu.VMEM((chunks, shard, width), LOW),
-            pltpu.VMEM((groups, shard, width), LOW),
+            pltpu.VMEM((chunks, groups, shard, width), LOW),
             pltpu.VMEM((experts, *small), FULL),
             pltpu.VMEM((experts, *small), FULL),
             pltpu.VMEM(small, FULL),
             pltpu.VMEM((groups, *small), FULL),
+            pltpu.VMEM((seq_len, 3 * width), LOW),
+            pltpu.VMEM((heads, seq_len, seq_len), LOW),
+            pltpu.VMEM(wqkv.shape, LOW),
+            pltpu.VMEM(result.shape, LOW),
+            dma((4,)),
+            dma((2, experts)),
             dma((2, chunks, chips)),
             dma((2, chunks, chips - 1)),
-            dma((2, groups)),
+            dma((2, chunks, groups)),
             dma((2, chunks, groups - 1)),
             dma((2, experts)),
             dma((2, groups)),
@@ -1184,6 +1359,7 @@
         wproj,
         wrouter.T,
         jnp.asarray(near_onehot(buckets)),
+        result,
     )
 
 
@@ -1204,7 +1380,23 @@
 ):
     experts = w_router.shape[1]
     width = tokens.shape[1]
-    qkv, prob, mixed, hidden, normed2, rows, cot_rows, resg, gate_col, token, info = attn_dispatch(
+    groups = lax.axis_size("group")
+    (
+        qkv,
+        prob,
+        mixed,
+        hidden,
+        normed2,
+        rows,
+        cot_rows,
+        gate_col,
+        token,
+        info,
+        resg_t,
+        act,
+        slope,
+        outer_first,
+    ) = attn_dispatch(
         tokens,
         cotangent,
         gain_first,
@@ -1216,20 +1408,21 @@
         routes,
         priority,
         span_start,
-    )
-    act, slope, grad_outer = expert_first(rows, resg, w_in[0])
-    grad_out = lax.psum_scatter(
-        grad_outer[None], "group", scatter_dimension=1, tiled=True
-    ).astype(FULL)
-    ig, packed = expert_second(cot_rows, gate_col, act, slope, w_out[0], w_in[0], info)
-    recv = lax.all_to_all(packed, "expert", split_axis=0, concat_axis=0, tiled=True)
-    grad_inner = expert_inner(rows, ig)
+        w_in[0],
+        groups,
+    )
+    outer_first = lax.psum_scatter(outer_first, "group", scatter_dimension=0, tiled=True)
+    act, slope, outer_rest = expert_first(rows, resg_t, w_in[0], act, slope, groups)
+    outer_rest = lax.psum_scatter(outer_rest, "group", scatter_dimension=0, tiled=True)
+    outer = jnp.concatenate([outer_first[:, None], outer_rest], axis=1)
+    grad_out = jnp.swapaxes(outer, 2, 3).reshape(1, -1, width).astype(FULL)
+    recv, packed_out, grad_inner = expert_back(
+        cot_rows, gate_col, rows, info, act, slope, w_out[0], w_in[0]
+    )
     grad_in = lax.psum_scatter(
         grad_inner[None], "group", scatter_dimension=1, tiled=True
     ).astype(FULL)
-    packed_out = expert_result(act, w_out[0], info)
-    back = lax.all_to_all(packed_out, "expert", split_axis=0, concat_axis=0, tiled=True)
-    gtok, dense, small = attn_back(
+    block_out, gtok, dense, small = attn_back(
         tokens,
         cotangent,
         hidden,
@@ -1245,9 +1438,9 @@
         w_proj,
         w_router,
         bias_table,
-        lax.axis_size("group"),
-    )
-    block_out = combine(hidden, token, back.reshape(-1, width))
+        packed_out,
+        groups,
+    )
     shard = width // experts
     heads = bias_table.shape[1]
     per = bias_table.shape[0] // experts

time: 342 us -> 315 us (0.921)
  waiting for transfers between devices: 36.6 us -> 0.05 us
  Pallas kernels: 261 us -> 280 us
  starting transfers between devices: 8.39 us -> 0.12 us
    all_to_all x2 -> x0, waiting for transfers between devices: 36.6 us -> none  [the longest x1 36.6 us: on_device_fast(): lax.all_to_all(packed, 'expert', split_axis=0, concat_axis=0, tiled=True)]
    pallas_call x1, Pallas kernels: 91 us -> 117 us  [attn_back(): pl.pallas_call(attn_back_kernel, out_shape=(sds((seq_len, width), LOW), s...]
    pallas_call x1, Pallas kernels: 82.5 us -> 73.3 us  [attn_dispatch(): pl.pallas_call(attn_dispatch_kernel, out_shape=(sds((seq_len, 3 * width),...]
    all_to_all x2 -> x0, starting transfers between devices: 8.31 us -> none  [the longest x1 4.66 us: on_device_fast(): lax.all_to_all(packed, 'expert', split_axis=0, concat_axis=0, tiled=True)]
    pallas_call x5 -> x2, Pallas kernels: 87.2 us -> 89.8 us  [the longest x1 73 us: expert_back(): pl.pallas_call(expert_back_kernel, out_shape=(sds((experts, SLOTS, width...]
  transfers between devices with their start and end apart: 4 -> 3, of which waited for: 1 -> 0; matrix products, arithmetic and copies ran while one was open for 3% -> 4% of each run, Pallas kernels for 46% -> 67%
where the time goes in v3:
time: 315 us; the launch traced here: 311 us
  Pallas kernels  280 us (89%)
  between operations  14.9 us (5%)
  local copies, waits for them, and re-layouts  8.69 us (3%)
  other arithmetic  7.16 us (2%)
    pallas_call x1, Pallas kernels, attn_back(): pl.pallas_call(attn_back_kernel, out_shape=(sds((seq_len, width), LOW), s...  117 us
    pallas_call x1, Pallas kernels, attn_dispatch(): pl.pallas_call(attn_dispatch_kernel, out_shape=(sds((seq_len, 3 * width),...  73.3 us
    pallas_call x1, Pallas kernels, expert_back(): pl.pallas_call(expert_back_kernel, out_shape=(sds((experts, SLOTS, width...  73 us
    pallas_call x1, Pallas kernels, expert_first(): pl.pallas_call(expert_first_kernel, grid=(groups * rest,), out_shape=(sds...  16.8 us
  transfers between devices with their start and end apart: 3, of which 0 were waited for; matrix products, arithmetic and copies ran while one was open for 4% of the time, Pallas kernels for 67%

profile of v3, /device:TPU:8, one launch (start us, length us, event | category | flops | bytes accessed | tf_op | source)
XLA Modules:
  0.0 311.2 jit_solution(8624074760508382313)
XLA Ops:
  7.2 0.0 reduce-scatter.6.cloned.1.call-start
  7.9 73.3 %shard_map.222 = (bf16[512,2304]{1,0:T(8,128)(2,1)}, bf16[12,512,512]{2,1,0:T(8,128)(2,1)}, bf16[512,768]{1,0:T(8,128)(2,1)}, f32[512,768]{1,0:T(8,128)}, bf16[5...) custom-call(bf16[512,768]{1,0:T(8,128)(2,1)} %tokens_ref.3, ...), custom_call_target="tpu_custom_call" | custom-call | tf_op jit(solution)/shard_map/pallas_call | solution.py:579
  81.1 0.0 reduce-scatter.6.cloned.1.call-update
  81.2 0.0 reduce-scatter.8.cloned.1.call-start
  81.2 16.8 %shard_map.223 = (bf16[12,1280,256]{2,1,0:T(8,128)(2,1)}, bf16[12,1280,256]{2,1,0:T(8,128)(2,1)}, bf16[4,2,768,256]{3,2,1,0:T(8,128)(2,1)}) custom-call(bf16[1280,768]{1,0:T(8,128)(2,1)} %get-tuple-element.41.rows_ref, bf16[768,1280]{1,0:T(8,128)(2,1)} %get-tuple-element.43.resgt_ref, ...), custom_call_target="tpu_custom_call", output_to_operand_aliasing={{0}: (3, {}), {1}: (4, {})} | custom-call | flops 8053063680 | bytes 31457280 | tf_op jit(solution)/shard_map/pallas_call | solution.py:681
  98.0 0.0 reduce-scatter.8.cloned.1.call-update
  98.1 0.0 reduce-scatter.4.cloned.1.call-start
  98.1 73.0 %shard_map.224 = (bf16[8,256,896]{2,1,0:T(8,128)(2,1)}, bf16[8,256,768]{2,1,0:T(8,128)(2,1)}, bf16[768,3072]{1,0:T(8,128)(2,1)}) custom-call(bf16[1280,768]{1,0:T(8,128)(2,1)} %get-tuple-element.39.cot_ref, f32[1280,128]{1,0:T(8,128)} %get-tuple-element.40.gate_ref, bf16[1280,768]{1,0:T(8,128)(2,1)} %get-tuple-element.41.rows_ref, ...), custom_call_target="tpu_custom_call" | custom-call | flops 54159192064 | bytes 52428800 | tf_op jit(solution)/shard_map/pallas_call | solution.py:856
  171.1 0.0 reduce-scatter.4.cloned.1.call-update
  171.1 117.2 %shard_map.225 = (bf16[512,768]{1,0:T(8,128)(2,1)}, bf16[512,768]{1,0:T(8,128)(2,1)}, bf16[4,96,768]{2,1,0:T(8,128)(2,1)}, f32[16,128]{1,0:T(8,128)}) custom-call(bf16[512,768]{1,0:T(8,128)(2,1)} %tokens_ref.3, bf16[512,768]{1,0:T(8,128)(2,1)} %cot_ref.3, f32[512,768]{1,0:T(8,128)} %get-tuple-element.34.hidden_ref, ...), custom_call_target="tpu_custom_call" | custom-call | flops 30000001024 | bytes 31457280 | tf_op jit(solution)/shard_map/pallas_call | solution.py:1296
  288.3 1.3 slice.21
  289.6 1.1 slice_convert_fusion
  290.7 0.5 reshape.50
  291.2 0.0 copy-start.2
  291.2 0.6 copy.28
  291.8 1.5 reshape.47
  293.3 0.0 copy-done.2
  293.3 0.5 slice_bitcast_fusion.1
  293.8 0.6 slice_bitcast_fusion
  294.4 1.6 bitcast_convert_fusion
  296.1 0.0 reduce-scatter.6.cloned.1.call-done
  296.1 0.0 reduce-scatter.8.cloned.1.call-done
  296.1 1.4 convert_bitcast_fusion
  297.5 2.0 copy.29
  299.4 0.0 copy-start.1
  299.4 0.0 copy-start
  299.4 0.0 reduce-scatter.4.cloned.1.call-done
  299.4 3.1 convert_element_type.44
  302.5 0.0 copy-done.1
  302.5 0.9 copy.35
  303.4 0.0 copy-done
  303.4 0.9 copy.36
Async XLA Ops:
  7.2 288.9 %reduce-scatter.6.cloned.1.call-start = ((), (), s32[]{:S(2)}) async-start(), calls=%async_computation.4 | async-start | bytes 1966080 | tf_op jit(solution)/shard_map/reduce_scatter | solution.py:1414
  81.2 214.9 %reduce-scatter.8.cloned.1.call-start = ((), (), s32[]{:S(2)}) async-start(), calls=%async_computation.5 | async-start | bytes 3932160 | tf_op jit(solution)/shard_map/reduce_scatter | solution.py:1416
  98.1 201.4 %reduce-scatter.4.cloned.1.call-start = ((), (), s32[]{:S(2)}) async-start(), calls=%async_computation.3 | async-start | bytes 5898240 | tf_op jit(solution)/shard_map/reduce_scatter | solution.py:1422
  291.2 2.1 copy-start.2
  299.4 3.1 copy-start.1
  299.4 3.9 %copy-start = (bf16[512,768]{1,0:T(8,128)(2,1)S(1)}, bf16[512,768]{1,0:T(8,128)(2,1)}, u32[]{:S(2)}) copy-start(bf16[512,768]{1,0:T(8,128)(2,1)} %get-tuple-element.71) | copy-start | bytes 2359300
Sparse Core Ops, SparseCore 0:
  81.3 34.3 reduce-scatter.5
  118.0 59.8 reduce-scatter.7
  180.2 111.7 reduce-scatter.3

commit v4 on v3

--- a/solution.py
+++ b/solution.py
@@ -508,8 +508,8 @@
                 pltpu.make_async_copy(src.at[tile], dst, tile_sem.at[kind, tile])
                 for kind, (src, dst) in enumerate(
                     (
-                        (act_v, act_out.at[tile * THIRDS]),
-                        (slope_v, slope_out.at[tile * THIRDS]),
+                        (act_v, act_out.at[tile]),
+                        (slope_v, slope_out.at[tile]),
                         (gout_v, gout_out.at[tile]),
                     )
                 )
@@ -590,8 +590,8 @@
             sds((seq_len, 8), FULL),
             sds((experts, 128), FULL),
             sds((width, capacity), LOW),
-            sds((ff // FF_TILE, capacity, FF_TILE), LOW),
-            sds((ff // FF_TILE, capacity, FF_TILE), LOW),
+            sds((groups, capacity, FF_TILE), LOW),
+            sds((groups, capacity, FF_TILE), LOW),
             sds((groups, width, FF_TILE), LOW),
         ),
         in_specs=[VM] * 3 + [HBM] * 2 + [VM] * 6 + [SM, HBM],
@@ -661,65 +661,23 @@
     return dot_nn(pick, data[...]).astype(LOW)
 
 
-def expert_first_kernel(rows_ref, resgt_ref, win_ref, act_in, slope_in, act_ref, slope_ref, gout_ref):
-    for row0 in range(0, rows_ref.shape[0], ROW_TILE):
-        here = slice(row0, row0 + ROW_TILE)
-        act, slope = gelu_and_slope(dot_nn(rows_ref[here, :], win_ref[...]))
-        act_ref[0, here, :] = act.astype(LOW)
-        slope_ref[0, here, :] = slope.astype(LOW)
-    gout_ref[0, 0] = dot_nn(resgt_ref[...], act_ref[0]).astype(LOW)
-
-
-def expert_first(rows, resg_t, w_in, act, slope, groups):
-    capacity, width = rows.shape
-    rest = THIRDS - 1
-    sds = jax.ShapeDtypeStruct
-
-    def tile(i):
-        return i // rest * THIRDS + 1 + i % rest
-
-    return pl.pallas_call(
-        expert_first_kernel,
-        grid=(groups * rest,),
-        out_shape=(
-            sds(act.shape, LOW),
-            sds(slope.shape, LOW),
-            sds((groups, rest, width, FF_TILE), LOW),
-        ),
-        in_specs=[
-            pl.BlockSpec((capacity, width), lambda i: (0, 0)),
-            pl.BlockSpec((width, capacity), lambda i: (0, 0)),
-            pl.BlockSpec((width, FF_TILE), lambda i: (0, tile(i))),
-            HBM,
-            HBM,
-        ],
-        out_specs=[
-            pl.BlockSpec((1, capacity, FF_TILE), lambda i: (tile(i), 0, 0)),
-            pl.BlockSpec((1, capacity, FF_TILE), lambda i: (tile(i), 0, 0)),
-            pl.BlockSpec((1, 1, width, FF_TILE), lambda i: (i // rest, i % rest, 0, 0)),
-        ],
-        input_output_aliases={3: 0, 4: 1},
-        compiler_params=pltpu.CompilerParams(vmem_limit_bytes=56 * MIB),
-        cost_estimate=pl.CostEstimate(
-            flops=4 * capacity * width * FF_TILE * groups * rest,
-            bytes_accessed=30 * MIB,
-            transcendentals=capacity * FF_TILE * groups * rest,
-        ),
-    )(rows, resg_t, w_in, act, slope)
-
-
-def expert_back_kernel(
+def expert_kernel(
     cot_ref,
     gate_ref,
     rows_ref,
     info_ref,
+    resgt_hbm,
     act_ref,
     slope_ref,
+    outer_ref,
     wout_ref,
     win_ref,
     recv_ref,
     packed_ref,
     gin_ref,
+    gout_ref,
+    up_in,
+    down_in,
     act_v,
     slope_v,
     wout_v,
@@ -729,63 +687,236 @@
     gg_ref,
     data_ref,
     send_ref,
-    rows_t,
+    turned,
     gin_v,
+    outer_v,
+    fold_ref,
+    took_ref,
+    total_ref,
+    packed_v,
+    gout_v,
     load_sem,
+    act_sem,
     slope_sem,
+    outer_sem,
     gin_sem,
+    own_sem,
+    took_sem,
+    total_sem,
     send_sem,
     recv_sem,
+    fold_sems,
 ):
     g = lax.axis_index("group")
     me = lax.axis_index("expert")
     experts, slots, wide = send_ref.shape
     tiles, capacity, tile_width = act_v.shape
     width = cot_ref.shape[1]
+    groups = act_ref.shape[0]
+    thirds = tiles // groups
+    last = groups - 1
+    copies = last * thirds
+    arrivals = (up_in, down_in)
 
     def device(mask):
         return (g, lax.bitwise_xor(me, mask))
 
     def load(index):
-        src, dst = ((wout_ref, wout_v), (win_ref, win_v), (act_ref, act_v))[index]
+        src, dst = ((wout_ref, wout_v), (win_ref, win_v), (resgt_hbm, turned))[index]
         return pltpu.make_async_copy(src, dst, load_sem.at[index])
+
+    def act_load(tile):
+        return pltpu.make_async_copy(act_ref.at[tile], act_v.at[tile], act_sem.at[tile])
 
     def slope_load(tile):
         slot = lax.rem(tile, 2)
         return pltpu.make_async_copy(slope_ref.at[tile], slope_v.at[slot], slope_sem.at[slot])
 
+    def outer_load(tile):
+        return pltpu.make_async_copy(outer_ref.at[tile], outer_v.at[tile], outer_sem.at[tile])
+
+    for tile in range(groups):
+        outer_load(tile).start()
     load(0).start()
     slope_load(0).start()
+    act_load(0).start()
+    load(1).start()
+    for tile in range(1, groups):
+        act_load(tile).start()
     load(2).start()
-    load(1).start()
     barrier = pltpu.get_barrier_semaphore()
     for mask in range(1, experts):
         pl.semaphore_signal(barrier, inc=1, device_id=device(mask), device_id_type=MESH)
-    pl.semaphore_wait(barrier, experts - 1)
+    for step in range(1, groups):
+        pl.semaphore_signal(
+            barrier, inc=1, device_id=(lax.rem(g + step, groups), me), device_id_type=MESH
+        )
+    pl.semaphore_wait(barrier, experts - 1 + groups - 1)
+    for tile in range(groups):
+        outer_load(tile).wait()
+
+    def fold_tile(way, k):
+        return (k % last if way else last - k % last), k // last
+
+    def fold_copy(way, k, src):
+        shard_at, third = fold_tile(way, k)
+        there = arrivals[way].at[shard_at, third]
+        return pltpu.make_async_remote_copy(
+            src_ref=there if src is None else src,
+            dst_ref=there,
+            send_sem=fold_sems.at[0, way, k],
+            recv_sem=fold_sems.at[1, way, k],
+            device_id=(lax.rem(g + (last if way else 1), groups), me),
+            device_id_type=MESH,
+        )
+
+    def take_tile(way, src):
+        return pltpu.make_async_copy(src, took_ref.at[way], took_sem.at[way])
+
+    def fold_source(*which):
+        for k in which:
+            for way in range(2):
+                shard_at, third = fold_tile(way, k)
+
+                @pl.when(g == way * last)
+                def _():
+                    fold_copy(way, k, outer_v.at[third * groups + shard_at]).start()
+
+    def passed(way, here):
+        return [
+            k
+            for k in range(copies)
+            if ((fold_tile(way, k)[0] < here) if way else (fold_tile(way, k)[0] > here))
+        ]
+
+    def fold_role(hop, k, act):
+        for way in range(2):
+            here = last - hop if way else hop
+            order = passed(way, here)
+            if k in order:
+                pl.when(g == here)(functools.partial(act, way, k, order, order.index(k)))
+
+    def fold_fetch(hop, k):
+        def act(way, k, order, nth):
+            shard_at, third = fold_tile(way, k)
+            fold_copy(way, k, None).wait_recv()
+            take_tile(way, arrivals[way].at[shard_at, third]).start()
+
+        fold_role(hop, k, act)
+
+    def fold_push(hop, k):
+        def act(way, k, order, nth):
+            shard_at, third = fold_tile(way, k)
+            if nth >= 2:
+                fold_copy(way, order[nth - 2], None).wait_send()
+            take_tile(way, arrivals[way].at[shard_at, third]).wait()
+            own = outer_v[third * groups + shard_at].astype(FULL)
+            fold_ref[way, nth % 2] = (own + took_ref[way].astype(FULL)).astype(LOW)
+            fold_copy(way, k, fold_ref.at[way, nth % 2]).start()
+
+        fold_role(hop, k, act)
+
+    def fold_final(third):
+        total_ref[...] = outer_v[third * groups + g].astype(FULL)
+        for way, (some, at) in enumerate(((g > 0, last - g), (g < last, g))):
+
+            @pl.when(some)
+            def _():
+                here = arrivals[way].at[g, third]
+                k = third * last + at
+                pltpu.make_async_remote_copy(
+                    src_ref=here,
+                    dst_ref=here,
+                    send_sem=fold_sems.at[0, way, k],
+                    recv_sem=fold_sems.at[1, way, k],
+                    device_id=(lax.rem(g + 1, groups), me),
+                    device_id_type=MESH,
+                ).wait_recv()
+                take_tile(way, here).start()
+                take_tile(way, here).wait()
+                total_ref[...] += took_ref[way].astype(FULL)
+
+        gout_v[third * tile_width : (third + 1) * tile_width, :] = jnp.transpose(total_ref[...])
+        gout_copy(third).start()
+
+    def gout_copy(third):
+        here = pl.ds(third * tile_width, tile_width)
+        return pltpu.make_async_copy(gout_v.at[here, :], gout_ref.at[here, :], total_sem.at[third])
+
+    def fold_sent():
+        for way in range(2):
+            for k in range(copies):
+
+                @pl.when(g == way * last)
+                def _():
+                    fold_copy(way, k, None).wait_send()
+
+            for hop in range(1, last):
+                here = last - hop if way else hop
+                for k in passed(way, here)[-2:]:
+
+                    @pl.when(g == here)
+                    def _():
+                        fold_copy(way, k, None).wait_send()
+
+    fold_source(*range(last))
     acc_ref[...] = jnp.zeros_like(acc_ref)
     gg_ref[...] = jnp.zeros_like(gg_ref)
-    for index in range(3):
+    for index in range(2):
         load(index).wait()
 
     def span(tile):
-        return pl.ds(pl.multiple_of(tile * tile_width, tile_width), tile_width)
-
-    @pl.loop(0, tiles)
-    def _(tile):
-        slope_load(tile).wait()
-
-        @pl.when(tile + 1 < tiles)
-        def _():
-            slope_load(tile + 1).start()
-
+        at = lax.rem(tile, groups) * thirds + lax.div(tile, groups)
+        return pl.ds(pl.multiple_of(at * tile_width, tile_width), tile_width)
+
+    def back_tile(tile, slope_slot):
         for row0 in range(0, capacity, ROW_TILE):
             here = slice(row0, row0 + ROW_TILE)
             back = dot_nt(cot_ref[here, :], wout_v[span(tile), :])
             part = act_v[tile, here, :].astype(FULL) * back
             gg_ref[here, :] += part[:, 0:128] + part[:, 128:256]
-            slope = slope_v[lax.rem(tile, 2), here, :].astype(FULL)
+            slope = slope_v[slope_slot, here, :].astype(FULL)
             ig_v[tile, here, :] = (slope * (gate_ref[here, 0:1] * back)).astype(LOW)
             acc_ref[here, :] += dot_nt(ig_v[tile, here, :], win_v[:, span(tile)])
+
+    @pl.loop(0, groups)
+    def _(tile):
+        slope_load(tile).wait()
+        act_load(tile).wait()
+
+        @pl.when(tile + 1 < groups)
+        def _():
+            slope_load(tile + 1).start()
+
+        back_tile(tile, lax.rem(tile, 2))
+
+    load(2).wait()
+    fold_fetch(1, 0)
+
+    def own_tiles(first, count):
+        @pl.loop(first, first + count)
+        def _(tile):
+            for row0 in range(0, capacity, ROW_TILE):
+                here = slice(row0, row0 + ROW_TILE)
+                act, slope = gelu_and_slope(dot_nn(rows_ref[here, :], win_v[:, span(tile)]))
+                act_v[tile, here, :] = act.astype(LOW)
+                slope_v[0, here, :] = slope.astype(LOW)
+            outer_v[tile] = dot_nn(turned[...], act_v[tile]).astype(LOW)
+            back_tile(tile, 0)
+
+    own_tiles(groups, 2)
+    fold_push(1, 0)
+    own_tiles(groups + 2, groups - 2)
+    fold_source(*range(last, 2 * last))
+    fold_fetch(1, 1)
+    own_tiles(2 * groups, 2)
+    fold_push(1, 1)
+    fold_fetch(1, 2)
+    fold_fetch(2, 0)
+    own_tiles(2 * groups + 2, groups - 2)
+    fold_source(*range(2 * last, 3 * last))
+    fold_push(1, 2)
+    fold_push(2, 0)
 
     data_ref[:, :width] = acc_ref[...].astype(LOW)
     gg = jnp.sum(gg_ref[...], axis=1, keepdims=True)
@@ -809,84 +940,142 @@
         other = lax.bitwise_xor(me, mask)
         send_ref[other] = pack_rows(other, info_ref, data_ref, slots)
         exchange(mask).start()
-    recv_ref[me] = pack_rows(me, info_ref, data_ref, slots)
-
-    rows_t[...] = jnp.transpose(rows_ref[...])
+        if mask == 4:
+            fold_fetch(1, 3)
+    send_ref[me] = pack_rows(me, info_ref, data_ref, slots)
+    own_rows = pltpu.make_async_copy(send_ref.at[me], recv_ref.at[me], own_sem)
+    own_rows.start()
+    fold_push(1, 3)
+    fold_fetch(1, 4)
+
+    turned[...] = jnp.transpose(rows_ref[...])
 
     def gin_copy(tile):
         slot = lax.rem(tile, 2)
-        return pltpu.make_async_copy(gin_v.at[slot], gin_ref.at[:, span(tile)], gin_sem.at[slot])
-
-    @pl.loop(0, tiles)
-    def _(tile):
-        @pl.when(tile >= 2)
-        def _():
-            gin_copy(tile).wait()
-
-        gin_v[lax.rem(tile, 2)] = dot_nn(rows_t[...], ig_v[tile]).astype(LOW)
-        gin_copy(tile).start()
+        cols = pl.ds(pl.multiple_of(lax.div(tile, groups) * tile_width, tile_width), tile_width)
+        return pltpu.make_async_copy(
+            gin_v.at[slot], gin_ref.at[:, lax.rem(tile, groups), :, cols], gin_sem.at[slot]
+        )
+
+    def gin_tiles(first, count):
+        @pl.loop(first, first + count)
+        def _(tile):
+            @pl.when(tile >= 2)
+            def _():
+                gin_copy(tile).wait()
+
+            got = dot_nn(turned[...], ig_v[tile]).astype(LOW)
+            gin_v[lax.rem(tile, 2)] = got.reshape(gin_v.shape[1:])
+            gin_copy(tile).start()
+
+    gin_tiles(0, tiles // 2)
+    fold_push(1, 4)
+    gin_tiles(tiles // 2, tiles // 2)
+    fold_fetch(1, 5)
+    fold_fetch(2, 3)
 
     acc_ref[...] = jnp.zeros_like(acc_ref)
 
-    @pl.loop(0, tiles)
-    def _(tile):
-        for row0 in range(0, capacity, ROW_TILE):
-            here = slice(row0, row0 + ROW_TILE)
-            acc_ref[here, :] += dot_nn(act_v[tile, here, :], wout_v[span(tile), :])
-
+    def result_tiles(first, count):
+        @pl.loop(first, first + count)
+        def _(tile):
+            for row0 in range(0, capacity, ROW_TILE):
+                here = slice(row0, row0 + ROW_TILE)
+                acc_ref[here, :] += dot_nn(act_v[tile, here, :], wout_v[span(tile), :])
+
+    result_tiles(0, tiles // 2)
+    fold_push(1, 5)
+    fold_push(2, 3)
+    result_tiles(tiles // 2, tiles // 2)
+    fold_fetch(1, 6)
     gin_copy(0).wait()
     gin_copy(1).wait()
     data_ref[:, :width] = acc_ref[...].astype(LOW)
 
     @pl.loop(0, experts)
     def _(source):
-        packed_ref[source] = pack_rows(source, info_ref, data_ref.at[:, 0:width], slots)
-
+        packed_v[source] = pack_rows(source, info_ref, data_ref.at[:, 0:width], slots)
+
+    packed_copy = pltpu.make_async_copy(packed_v, packed_ref, total_sem.at[thirds])
+    packed_copy.start()
+    fold_push(1, 6)
+    fold_final(0)
+    fold_fetch(1, 7)
+    fold_push(1, 7)
+    fold_fetch(2, 6)
+    fold_push(2, 6)
+    fold_final(1)
+    fold_fetch(1, 8)
+    fold_push(1, 8)
+    fold_final(2)
+    packed_copy.wait()
+    for third in range(thirds):
+        gout_copy(third).wait()
+    own_rows.wait()
     for mask in range(1, experts):
         exchange(mask).wait()
-
-
-def expert_back(cot_rows, gate_col, rows, info, act, slope, w_out, w_in):
+    fold_sent()
+
+
+def expert_call(cot_rows, gate_col, rows, info, resg_t, act, slope, outer, w_out, w_in):
     capacity, width = cot_rows.shape
-    tiles, _, tile_width = act.shape
+    groups, _, tile_width = act.shape
     ff = w_in.shape[1]
+    tiles = ff // tile_width
     experts = info.shape[0]
     sds = jax.ShapeDtypeStruct
     dma = pltpu.SemaphoreType.DMA
-    return pl.pallas_call(
-        expert_back_kernel,
+    arrival = sds((groups, tiles // groups, width, tile_width), LOW)
+    outs = pl.pallas_call(
+        expert_kernel,
         out_shape=(
             sds((experts, SLOTS, width + 128), LOW),
             sds((experts, SLOTS, width), LOW),
-            sds((width, ff), LOW),
+            sds((groups, groups, width // groups, ff // groups), LOW),
+            sds((ff // groups, width), FULL),
+            arrival,
+            arrival,
         ),
-        in_specs=[VM] * 4 + [HBM] * 4,
-        out_specs=[VM, VM, HBM],
+        in_specs=[VM] * 4 + [HBM] * 6,
+        out_specs=[HBM] * 6,
         scratch_shapes=[
-            pltpu.VMEM(act.shape, LOW),
+            pltpu.VMEM((tiles, capacity, tile_width), LOW),
             pltpu.VMEM((2, capacity, tile_width), LOW),
             pltpu.VMEM(w_out.shape, LOW),
             pltpu.VMEM(w_in.shape, LOW),
-            pltpu.VMEM(act.shape, LOW),
+            pltpu.VMEM((tiles, capacity, tile_width), LOW),
             pltpu.VMEM((capacity, width), FULL),
             pltpu.VMEM((capacity, 128), FULL),
             pltpu.VMEM((capacity, width + 128), LOW),
             pltpu.VMEM((experts, SLOTS, width + 128), LOW),
             pltpu.VMEM((width, capacity), LOW),
+            pltpu.VMEM((2, groups, width // groups, tile_width), LOW),
+            pltpu.VMEM((tiles, width, tile_width), LOW),
+            pltpu.VMEM((2, 2, width, tile_width), LOW),
             pltpu.VMEM((2, width, tile_width), LOW),
+            pltpu.VMEM((width, tile_width), FULL),
+            pltpu.VMEM((experts, SLOTS, width), LOW),
+            pltpu.VMEM((ff // groups, width), FULL),
             dma((3,)),
+            dma((groups,)),
             dma((2,)),
+            dma((groups,)),
             dma((2,)),
+            dma,
+            dma((2,)),
+            dma((tiles // groups + 1,)),
             dma((experts,)),
             dma((experts,)),
+            dma((2, 2, (groups - 1) * (tiles // groups))),
         ],
         compiler_params=pltpu.CompilerParams(
-            vmem_limit_bytes=60 * MIB, collective_id=2, has_side_effects=True
+            vmem_limit_bytes=62 * MIB, collective_id=2, has_side_effects=True
         ),
         cost_estimate=pl.CostEstimate(
-            flops=8 * capacity * width * ff + 30_000_000_000, bytes_accessed=50 * MIB, transcendentals=0
+            flops=12 * capacity * width * ff, bytes_accessed=50 * MIB, transcendentals=0
         ),
-    )(cot_rows, gate_col, rows, info, act, slope, w_out, w_in)
+    )(cot_rows, gate_col, rows, info, resg_t, act, slope, outer, w_out, w_in)
+    return outs[:4]
 
 
 def attn_back_kernel(
@@ -906,10 +1095,14 @@
     wrouter_ref,
     onehot_ref,
     result_ref,
+    gin_ref,
     block_ref,
     gtok_ref,
     dense_out,
     small_out,
+    gin_out,
+    up_in,
+    down_in,
     hgrad_ref,
     mgrad_ref,
     mgrad_t,
@@ -934,6 +1127,12 @@
     prob_ref,
     wqkv_ref,
     back_ref,
+    fold_ref,
+    took_ref,
+    total_ref,
+    fold_sems,
+    took_sems,
+    total_sems,
     load_sems,
     back_sems,
     pair_sems,
@@ -1071,6 +1270,117 @@
         def _():
             remote(plane_ref.at[c], group_in.at[c, g], group_sems, (c, g), where).wait_send()
 
+    parts = gin_ref.shape[1]
+    last = groups - 1
+    copies = last * parts
+    arrivals = (up_in, down_in)
+
+    def fold_tile(way, k):
+        return (k // parts if way else last - k // parts), k % parts
+
+    def fold_copy(way, k, src):
+        shard_at, tile_at = fold_tile(way, k)
+        there = arrivals[way].at[shard_at, tile_at]
+        step = last if way else 1
+        where = (lax.rem(g + step, groups), me)
+        return pltpu.make_async_remote_copy(
+            src_ref=there if src is None else src,
+            dst_ref=there,
+            send_sem=fold_sems.at[0, way, k],
+            recv_sem=fold_sems.at[1, way, k],
+            device_id=where,
+            device_id_type=MESH,
+        )
+
+    def take_tile(way, which, src):
+        return pltpu.make_async_copy(src, took_ref.at[way, which], took_sems.at[way, which])
+
+    def fold_source(k):
+        for way in range(2):
+
+            @pl.when(g == way * last)
+            def _():
+                fold_copy(way, k, gin_ref.at[fold_tile(way, k)]).start()
+
+    def fold_place(way, k):
+        main = (g == 1) if way == 0 else (g == last - 1)
+        return jnp.where(main, k, (last - 1) * parts + k)
+
+    def fold_role(hop, k, act):
+        for way in range(2):
+            shard_at, tile_at = fold_tile(way, k)
+            here = last - hop if way else hop
+            if (shard_at < here) if way else (shard_at > here):
+                pl.when(g == here)(functools.partial(act, way, k, shard_at, tile_at))
+
+    def fold_fetch(hop, k):
+        def act(way, k, shard_at, tile_at):
+            take_tile(way, 0, gin_ref.at[shard_at, tile_at]).start()
+            fold_copy(way, k, None).wait_recv()
+            take_tile(way, 1, arrivals[way].at[shard_at, tile_at]).start()
+
+        fold_role(hop, k, act)
+
+    def fold_push(hop, k):
+        def act(way, k, shard_at, tile_at):
+            take_tile(way, 0, gin_ref.at[shard_at, tile_at]).wait()
+            take_tile(way, 1, arrivals[way].at[shard_at, tile_at]).wait()
+            place = fold_place(way, k)
+            total = took_ref[way, 0].astype(FULL) + took_ref[way, 1].astype(FULL)
+            fold_ref[place] = total.astype(LOW)
+            fold_copy(way, k, fold_ref.at[place]).start()
+
+        fold_role(hop, k, act)
+
+    def fold_final(tile_at):
+        own = take_tile(0, 0, gin_ref.at[g, tile_at])
+        own.start()
+        cases = ((g > 0, up_in, (last - g) * parts + tile_at), (g < last, down_in, g * parts + tile_at))
+        for way, (some, arrival, k) in enumerate(cases):
+
+            @pl.when(some)
+            def _():
+                here = arrival.at[g, tile_at]
+                pltpu.make_async_remote_copy(
+                    src_ref=here,
+                    dst_ref=here,
+                    send_sem=fold_sems.at[0, way, k],
+                    recv_sem=fold_sems.at[1, way, k],
+                    device_id=(lax.rem(g + 1, groups), me),
+                    device_id_type=MESH,
+                ).wait_recv()
+                take_tile(way, 1, here).start()
+
+        own.wait()
+        if tile_at >= 2:
+            final_copy(tile_at - 2).wait()
+        total_ref[tile_at % 2] = took_ref[0, 0].astype(FULL)
+        for way, (some, arrival, k) in enumerate(cases):
+
+            @pl.when(some)
+            def _():
+                take_tile(way, 1, arrival.at[g, tile_at]).wait()
+                total_ref[tile_at % 2] += took_ref[way, 1].astype(FULL)
+
+        final_copy(tile_at).start()
+
+    def final_copy(tile_at):
+        cols = pl.ds(tile_at * total_ref.shape[2], total_ref.shape[2])
+        return pltpu.make_async_copy(
+            total_ref.at[tile_at % 2], gin_out.at[:, cols], total_sems.at[tile_at % 2]
+        )
+
+    def fold_sent():
+        for way in range(2):
+            for k in range(copies):
+                shard_at, _ = fold_tile(way, k)
+
+                @pl.when((g > shard_at) if way else (g < shard_at))
+                def _():
+                    fold_copy(way, k, None).wait_send()
+
+    for k in range(3):
+        fold_source(k)
     ggain2 = jnp.zeros((8, width), FULL)
     lg_t = []
     for row0 in range(0, seq_len, tile):
@@ -1105,6 +1415,11 @@
         x = tokens_ref[rows, :].astype(FULL)
         inv = lax.rsqrt(jnp.mean(x * x, axis=1, keepdims=True) + EPS)
         dqkv_ref[rows, :width] = (x * inv * gain1_ref[...][None, :]).astype(LOW)
+        if row0 == tile:
+            fold_source(3)
+        if row0 == 3 * tile:
+            fold_fetch(1, 0)
+            fold_source(4)
     ggain2 = jnp.sum(ggain2, axis=0, keepdims=True)
     logit_grad_t = jnp.concatenate(lg_t, axis=1).astype(LOW)
     grouter = dot_nn(logit_grad_t, normed2_ref[...])
@@ -1115,6 +1430,8 @@
         .reshape(experts, width // experts, width)
     )
     pair_send(0)
+    fold_push(1, 0)
+    fold_fetch(1, 1)
     mgrad_t[...] = jnp.transpose(mgrad_ref[...])
     load(0).wait()
     q_t[...] = jnp.transpose(qkv_ref[:, :width])
@@ -1201,6 +1518,15 @@
         plane_send(c - 1)
         if c >= 2:
             group_send(c - 2)
+        fold_push(1, c)
+        fold_source(c + 4)
+        if c < chunks - 1:
+            fold_fetch(1, c + 1)
+        if c == 2:
+            fold_fetch(2, 0)
+        if c == 3:
+            fold_push(2, 0)
+            fold_fetch(2, 1)
 
     load(2).wait()
     ggain1 = jnp.zeros((8, width), FULL)
@@ -1220,6 +1546,12 @@
             plane_send(chunks - 1)
             for mask in (6, 7):
                 result_copy(mask).start()
+            fold_fetch(1, 4)
+            fold_push(2, 1)
+        if row0 == 2 * tile:
+            fold_push(1, 4)
+            fold_fetch(2, 2)
+            fold_source(8)
     ggain1 = jnp.sum(ggain1, axis=0, keepdims=True)
 
     gtable = exact_nt(onehot_ref[...], diag_ref[...])
@@ -1236,8 +1568,13 @@
     for mask in range(1, experts):
         other = lax.bitwise_xor(me, mask)
         go(remote(small_ref.at[other], small_in.at[mask], small_sems, (mask,), device(mask)))
+    fold_source(9)
+    fold_fetch(1, 5)
+    fold_push(2, 2)
     final_send(0)
     group_send(2)
+    fold_push(1, 5)
+    fold_fetch(2, 3)
     total = small_ref[me]
     for mask in range(1, experts):
         remote(
@@ -1248,11 +1585,19 @@
     for step in range(1, groups):
         where = (lax.rem(g + step, groups), me)
         go(remote(small_plane, small_group.at[step], smallz_sems, (step,), where))
+    fold_fetch(1, 6)
+    fold_push(2, 3)
     final_send(1)
     group_send(3)
+    fold_source(10)
+    fold_source(11)
+    fold_push(1, 6)
+    fold_fetch(1, 7)
     own_result.wait()
     for mask in range(1, experts):
         result_copy(mask).wait()
+
+    fold_push(1, 7)
 
     @pl.loop(0, seq_len // tile)
     def _(step):
@@ -1267,8 +1612,14 @@
             hidden_ref[rows, :] + token[:, 2:3] * got[:tile] + token[:, 3:4] * got[tile:]
         ).astype(LOW)
 
+    fold_final(0)
     final_send(2)
+    fold_final(1)
     final_send(3)
+    for tile_at in range(2, parts):
+        fold_final(tile_at)
+    for tile_at in range(parts - 2, parts):
+        final_copy(tile_at).wait()
     for step in range(1, groups):
         remote(
             small_plane, small_group.at[step], smallz_sems, (step,), (lax.rem(g + step, groups), me)
@@ -1277,12 +1628,13 @@
     small_out[...] = total
     for c in range(chunks):
         finish(c)
+    fold_sent()
     for copy in started:
         copy.wait_send()
 
 
 def attn_back(
-    tokens, cot, hidden, normed2, mixed, qkv, prob, recv, token, gain1, gain2, wqkv, wproj, wrouter, table, result, groups
+    tokens, cot, hidden, normed2, mixed, qkv, prob, recv, token, gain1, gain2, wqkv, wproj, wrouter, table, result, gin, groups
 ):
     seq_len, width = tokens.shape
     buckets, heads = table.shape
@@ -1293,16 +1645,19 @@
     small = (16, 128)
     sds = jax.ShapeDtypeStruct
     dma = pltpu.SemaphoreType.DMA
-    return pl.pallas_call(
+    outs = pl.pallas_call(
         attn_back_kernel,
         out_shape=(
             sds((seq_len, width), LOW),
             sds((seq_len, width), LOW),
             sds((chunks, shard, width), LOW),
             sds(small, FULL),
+            sds((gin.shape[2], gin.shape[1] * gin.shape[3]), FULL),
+            sds(gin.shape, LOW),
+            sds(gin.shape, LOW),
         ),
-        in_specs=[VM] * 5 + [HBM] * 2 + [VM] * 4 + [HBM] + [VM] * 3 + [HBM],
-        out_specs=[VM] * 4,
+        in_specs=[VM] * 5 + [HBM] * 2 + [VM] * 4 + [HBM] + [VM] * 3 + [HBM] * 2,
+        out_specs=[VM] * 4 + [HBM] * 3,
         scratch_shapes=[
             pltpu.VMEM((seq_len, width), FULL),
             pltpu.VMEM((seq_len, width), LOW),
@@ -1328,6 +1683,12 @@
             pltpu.VMEM((heads, seq_len, seq_len), LOW),
             pltpu.VMEM(wqkv.shape, LOW),
             pltpu.VMEM(result.shape, LOW),
+            pltpu.VMEM((groups * (groups - 1), *gin.shape[2:]), LOW),
+            pltpu.VMEM((2, 2, *gin.shape[2:]), LOW),
+            pltpu.VMEM((2, *gin.shape[2:]), FULL),
+            dma((2, 2, (groups - 1) * gin.shape[1])),
+            dma((2, 2)),
+            dma((2,)),
             dma((4,)),
             dma((2, experts)),
             dma((2, chunks, chips)),
@@ -1360,7 +1721,105 @@
         wrouter.T,
         jnp.asarray(near_onehot(buckets)),
         result,
-    )
+        gin,
+    )
+    return outs[:5]
+
+
+def outputs_kernel(
+    block_in,
+    gtok_in,
+    gin_in,
+    gout_in,
+    dense_ref,
+    small_ref,
+    block_ref,
+    gtok_ref,
+    gain1_ref,
+    qkv_ref,
+    proj_ref,
+    table_ref,
+    gain2_ref,
+    router_ref,
+    gin_ref,
+    gout_ref,
+    gin_v,
+    gout_v,
+    block_v,
+    gtok_v,
+    sems,
+):
+    passed = (
+        (gin_in, gin_v, gin_ref.at[0]),
+        (gout_in, gout_v, gout_ref.at[0]),
+        (block_in, block_v, block_ref),
+        (gtok_in, gtok_v, gtok_ref),
+    )
+    pieces = 4
+    copies = []
+    for i, (src, mid, dst) in enumerate(passed):
+        rows = src.shape[0] // pieces
+        for piece in range(pieces):
+            here = pl.ds(piece * rows, rows)
+            copies.append(
+                [
+                    pltpu.make_async_copy(a.at[here, :], b.at[here, :], sems.at[way, i, piece])
+                    for way, (a, b) in enumerate(((src, mid), (mid, dst)))
+                ]
+            )
+    for copy_in, _ in copies:
+        copy_in.start()
+    chunks, shard, width = dense_ref.shape
+    experts = router_ref.shape[0]
+    stripe = width // (chunks - 1)
+    proj_ref[...] = dense_ref[0].astype(FULL)
+    for c in range(1, chunks):
+        for third in range(3):
+            col = third * width + (c - 1) * stripe
+            qkv_ref[:, col : col + stripe] = dense_ref[
+                c, :, third * stripe : third * stripe + stripe
+            ].astype(FULL)
+    gain1_ref[...] = small_ref[0:1, 0:shard]
+    gain2_ref[...] = small_ref[1:2, 0:shard]
+    router_ref[...] = small_ref[2 : 2 + experts, 0:shard]
+    per, heads = table_ref.shape
+    table_ref[...] = small_ref[2 + experts : 2 + experts + per, 0:heads]
+    for copy_in, copy_out in copies:
+        copy_in.wait()
+        copy_out.start()
+    for _, copy_out in copies:
+        copy_out.wait()
+
+
+def outputs(block, gtok, gin, gout, dense, small, experts, table_shape):
+    chunks, shard, width = dense.shape
+    buckets, heads = table_shape
+    sds = jax.ShapeDtypeStruct
+    return pl.pallas_call(
+        outputs_kernel,
+        out_shape=(
+            sds(block.shape, LOW),
+            sds(gtok.shape, LOW),
+            sds((1, shard), FULL),
+            sds((shard, 3 * width), FULL),
+            sds((shard, width), FULL),
+            sds((buckets // experts, heads), FULL),
+            sds((1, shard), FULL),
+            sds((experts, shard), FULL),
+            sds((1, *gin.shape), FULL),
+            sds((1, *gout.shape), FULL),
+        ),
+        in_specs=[HBM] * 4 + [VM] * 2,
+        out_specs=[HBM] * 2 + [VM] * 6 + [HBM] * 2,
+        scratch_shapes=[
+            pltpu.VMEM(gin.shape, FULL),
+            pltpu.VMEM(gout.shape, FULL),
+            pltpu.VMEM(block.shape, LOW),
+            pltpu.VMEM(gtok.shape, LOW),
+            pltpu.SemaphoreType.DMA((2, 4, 4)),
+        ],
+        compiler_params=pltpu.CompilerParams(vmem_limit_bytes=32 * MIB),
+    )(block, gtok, gin, gout, dense, small)
 
 
 def on_device_fast(
@@ -1411,18 +1870,10 @@
         w_in[0],
         groups,
     )
-    outer_first = lax.psum_scatter(outer_first, "group", scatter_dimension=0, tiled=True)
-    act, slope, outer_rest = expert_first(rows, resg_t, w_in[0], act, slope, groups)
-    outer_rest = lax.psum_scatter(outer_rest, "group", scatter_dimension=0, tiled=True)
-    outer = jnp.concatenate([outer_first[:, None], outer_rest], axis=1)
-    grad_out = jnp.swapaxes(outer, 2, 3).reshape(1, -1, width).astype(FULL)
-    recv, packed_out, grad_inner = expert_back(
-        cot_rows, gate_col, rows, info, act, slope, w_out[0], w_in[0]
-    )
-    grad_in = lax.psum_scatter(
-        grad_inner[None], "group", scatter_dimension=1, tiled=True
-    ).astype(FULL)
-    block_out, gtok, dense, small = attn_back(
+    recv, packed_out, grad_inner, grad_out = expert_call(
+        cot_rows, gate_col, rows, info, resg_t, act, slope, outer_first, w_out[0], w_in[0]
+    )
+    block_out, gtok, dense, small, grad_in = attn_back(
         tokens,
         cotangent,
         hidden,
@@ -1439,27 +1890,16 @@
         w_router,
         bias_table,
         packed_out,
+        grad_inner,
         groups,
     )
-    shard = width // experts
-    heads = bias_table.shape[1]
-    per = bias_table.shape[0] // experts
-    stripe = width // (dense.shape[0] - 1)
-    grad_qkv = (
-        dense[1:].reshape(-1, shard, 3, stripe).transpose(1, 2, 0, 3).reshape(shard, 3 * width)
-    )
-    return (
-        block_out,
-        gtok,
-        small[0, :shard],
-        grad_qkv.astype(FULL),
-        dense[0].astype(FULL),
-        small[2 + experts : 2 + experts + per, :heads],
-        small[1, :shard],
-        small[2 : 2 + experts, :shard].T,
-        grad_in,
-        grad_out,
-    )
+    final = list(
+        outputs(block_out, gtok, grad_in, grad_out, dense, small, experts, bias_table.shape)
+    )
+    final[2] = final[2].reshape(-1)
+    final[6] = final[6].reshape(-1)
+    final[7] = final[7].T
+    return tuple(final)
 
 
 def bucket_table(seq_len, buckets):

time: 315 us -> 296 us (0.940)
  between operations: 14.9 us -> 1.55 us
  other arithmetic: 7.16 us -> 0 us
  Pallas kernels: 280 us -> 285 us
    pallas_call x2, Pallas kernels: 89.8 us -> 106 us  [the longest x1 99.4 us: expert_call(): pl.pallas_call(expert_kernel, out_shape=(sds((experts, SLOTS, width + 128...]
    pallas_call x1, Pallas kernels: 117 us -> 106 us  [attn_back(): pl.pallas_call(attn_back_kernel, out_shape=(sds((seq_len, width), LOW), s...]
    convert_element_type x4 -> x0, other arithmetic: 7.16 us -> none  [the longest x1 3.05 us: on_device_fast(): grad_in = lax.psum_scatter(grad_inner[None], 'group', scatter_dimension=1...]
    convert_element_type x4 -> x0, local copies, waits for them, and re-layouts: 4.55 us -> none  [the longest x3 2.6 us: on_device_fast(): grad_qkv.astype(FULL)]
    unnamed x8 -> x12, local copies, waits for them, and re-layouts: 1.77 us -> 5.69 us
  transfers between devices with their start and end apart: 3 -> 0, of which waited for: 0 -> 0; matrix products, arithmetic and copies ran while one was open for 4% -> 0% of each run, Pallas kernels for 67% -> 0%
where the time goes in v4:
time: 296 us; the launch traced here: 293 us
  Pallas kernels  285 us (96%)
  local copies, waits for them, and re-layouts  5.69 us (2%)
    pallas_call x1, Pallas kernels, attn_back(): pl.pallas_call(attn_back_kernel, out_shape=(sds((seq_len, width), LOW), s...  106 us
    pallas_call x1, Pallas kernels, expert_call(): pl.pallas_call(expert_kernel, out_shape=(sds((experts, SLOTS, width + 128...  99.4 us
    pallas_call x1, Pallas kernels, attn_dispatch(): pl.pallas_call(attn_dispatch_kernel, out_shape=(sds((seq_len, 3 * width),...  73.2 us
    pallas_call x1, Pallas kernels, outputs(): pl.pallas_call(outputs_kernel, out_shape=(sds(block.shape, LOW), sds(gtok...  7 us

profile of v4, /device:TPU:8, one launch (start us, length us, event | category | flops | bytes accessed | tf_op | source)
XLA Modules:
  0.0 292.5 jit_solution(10652258564082315035)
XLA Ops:
  1.3 73.2 %shard_map.222 = (bf16[512,2304]{1,0:T(8,128)(2,1)}, bf16[12,512,512]{2,1,0:T(8,128)(2,1)}, bf16[512,768]{1,0:T(8,128)(2,1)}, f32[512,768]{1,0:T(8,128)}, bf16[5...) custom-call(bf16[512,768]{1,0:T(8,128)(2,1)} %tokens_ref.3, ...), custom_call_target="tpu_custom_call" | custom-call | tf_op jit(solution)/shard_map/pallas_call | solution.py:579
  74.5 99.4 %shard_map.223 = (bf16[8,256,896]{2,1,0:T(8,128)(2,1)}, bf16[8,256,768]{2,1,0:T(8,128)(2,1)}, bf16[4,4,192,768]{3,2,1,0:T(8,128)(2,1)}, f32[768,768]{1,0:T(8,128...) custom-call(bf16[1280,768]{1,0:T(8,128)(2,1)} %get-tuple-element.48.cot_ref, ...), custom_call_target="tpu_custom_call" | custom-call | flops 36238786560 | bytes 52428800 | tf_op jit(solution)/shard_map/pallas_call | solution.py:1029
  173.9 0.0 copy-start
  173.9 105.7 %shard_map.224 = (bf16[512,768]{1,0:T(8,128)(2,1)}, bf16[512,768]{1,0:T(8,128)(2,1)}, bf16[4,96,768]{2,1,0:T(8,128)(2,1)}, f32[16,128]{1,0:T(8,128)}, f32[192,30...) custom-call(bf16[512,768]{1,0:T(8,128)(2,1)} %tokens_ref.3, ...), custom_call_target="tpu_custom_call" | custom-call | flops 30000001024 | bytes 31457280 | tf_op jit(solution)/shard_map/pallas_call | solution.py:1648
  279.6 0.0 copy-done
  279.6 0.0 copy-start.1
  279.6 1.7 copy-done.1
  281.3 0.0 copy-start.2
  281.3 1.1 copy-done.2
  282.4 0.0 copy-start.3
  282.4 1.1 copy-done.3
  283.6 0.0 copy-start.4
  283.6 1.1 copy-done.4
  284.6 0.0 copy-start.5
  284.6 0.7 copy-done.5
  285.3 7.0 %shard_map.225 = (bf16[512,768]{1,0:T(8,128)(2,1)}, bf16[512,768]{1,0:T(8,128)(2,1)}, f32[1,96]{1,0:T(1,128)}, f32[96,2304]{1,0:T(8,128)}, f32[96,768]{1,0:T(8,1...) custom-call(bf16[512,768]{1,0:T(8,128)(2,1)S(1)} %copy-done.2, ...), custom_call_target="tpu_custom_call" | custom-call | tf_op jit(solution)/shard_map/pallas_call | solution.py:1798
Async XLA Ops:
  173.9 105.8 %copy-start = (f32[768,768]{1,0:T(8,128)S(1)}, f32[768,768]{1,0:T(8,128)}, u32[]{:S(2)}) copy-start(f32[768,768]{1,0:T(8,128)} %get-tuple-element.63.gout_in) | copy-start | bytes 7077892
  279.6 1.7 copy-start.1
  281.3 1.1 copy-start.2
  282.4 1.1 copy-start.3
  283.6 1.1 copy-start.4
  284.6 0.7 copy-start.5

commit v5 on v4

--- a/solution.py
+++ b/solution.py
@@ -23,6 +23,7 @@
 SECOND = 512.0
 SLOTS = 256
 ROW_TILE = 256
+EARLY = 2
 FF_TILE = 256
 THIRDS = 3
 
@@ -676,6 +677,8 @@
     packed_ref,
     gin_ref,
     gout_ref,
+    early_up,
+    early_down,
     up_in,
     down_in,
     act_v,
@@ -706,6 +709,7 @@
     send_sem,
     recv_sem,
     fold_sems,
+    early_sems,
 ):
     g = lax.axis_index("group")
     me = lax.axis_index("expert")
@@ -990,6 +994,37 @@
     fold_fetch(1, 6)
     gin_copy(0).wait()
     gin_copy(1).wait()
+
+    def early_copy(way, k):
+        return pltpu.make_async_remote_copy(
+            src_ref=gin_ref.at[0 if way else last, k],
+            dst_ref=(early_up, early_down)[way].at[k],
+            send_sem=early_sems.at[0, way, k],
+            recv_sem=early_sems.at[1, way, k],
+            device_id=(lax.rem(g + (last if way else 1), groups), me),
+            device_id_type=MESH,
+        )
+
+    def early_each(act):
+        for way in range(2):
+            for k in range(EARLY):
+                act(way, k)
+
+    def early_start(way, k):
+        @pl.when(g == way * last)
+        def _():
+            early_copy(way, k).start()
+
+    def early_end(way, k):
+        @pl.when(g == way * last)
+        def _():
+            early_copy(way, k).wait_send()
+
+        @pl.when(g == (last - 1 if way else 1))
+        def _():
+            early_copy(way, k).wait_recv()
+
+    early_each(early_start)
     data_ref[:, :width] = acc_ref[...].astype(LOW)
 
     @pl.loop(0, experts)
@@ -1015,6 +1050,7 @@
     for mask in range(1, experts):
         exchange(mask).wait()
     fold_sent()
+    early_each(early_end)
 
 
 def expert_call(cot_rows, gate_col, rows, info, resg_t, act, slope, outer, w_out, w_in):
@@ -1025,6 +1061,7 @@
     experts = info.shape[0]
     sds = jax.ShapeDtypeStruct
     dma = pltpu.SemaphoreType.DMA
+    early = sds((EARLY, width // groups, ff // groups), LOW)
     arrival = sds((groups, tiles // groups, width, tile_width), LOW)
     outs = pl.pallas_call(
         expert_kernel,
@@ -1033,11 +1070,13 @@
             sds((experts, SLOTS, width), LOW),
             sds((groups, groups, width // groups, ff // groups), LOW),
             sds((ff // groups, width), FULL),
+            early,
+            early,
             arrival,
             arrival,
         ),
         in_specs=[VM] * 4 + [HBM] * 6,
-        out_specs=[HBM] * 6,
+        out_specs=[HBM] * 8,
         scratch_shapes=[
             pltpu.VMEM((tiles, capacity, tile_width), LOW),
             pltpu.VMEM((2, capacity, tile_width), LOW),
@@ -1067,6 +1106,7 @@
             dma((experts,)),
             dma((experts,)),
             dma((2, 2, (groups - 1) * (tiles // groups))),
+            dma((2, 2, EARLY)),
         ],
         compiler_params=pltpu.CompilerParams(
             vmem_limit_bytes=62 * MIB, collective_id=2, has_side_effects=True
@@ -1075,7 +1115,7 @@
             flops=12 * capacity * width * ff, bytes_accessed=50 * MIB, transcendentals=0
         ),
     )(cot_rows, gate_col, rows, info, resg_t, act, slope, outer, w_out, w_in)
-    return outs[:4]
+    return outs[:6]
 
 
 def attn_back_kernel(
@@ -1096,6 +1136,8 @@
     onehot_ref,
     result_ref,
     gin_ref,
+    early_up,
+    early_down,
     block_ref,
     gtok_ref,
     dense_out,
@@ -1313,18 +1355,24 @@
             if (shard_at < here) if way else (shard_at > here):
                 pl.when(g == here)(functools.partial(act, way, k, shard_at, tile_at))
 
+    def arrived(hop, way, k):
+        if hop == 1 and k < EARLY:
+            return (early_up, early_down)[way].at[k]
+        return arrivals[way].at[fold_tile(way, k)]
+
     def fold_fetch(hop, k):
         def act(way, k, shard_at, tile_at):
             take_tile(way, 0, gin_ref.at[shard_at, tile_at]).start()
-            fold_copy(way, k, None).wait_recv()
-            take_tile(way, 1, arrivals[way].at[shard_at, tile_at]).start()
+            if not (hop == 1 and k < EARLY):
+                fold_copy(way, k, None).wait_recv()
+            take_tile(way, 1, arrived(hop, way, k)).start()
 
         fold_role(hop, k, act)
 
     def fold_push(hop, k):
         def act(way, k, shard_at, tile_at):
             take_tile(way, 0, gin_ref.at[shard_at, tile_at]).wait()
-            take_tile(way, 1, arrivals[way].at[shard_at, tile_at]).wait()
+            take_tile(way, 1, arrived(hop, way, k)).wait()
             place = fold_place(way, k)
             total = took_ref[way, 0].astype(FULL) + took_ref[way, 1].astype(FULL)
             fold_ref[place] = total.astype(LOW)
@@ -1374,13 +1422,17 @@
         for way in range(2):
             for k in range(copies):
                 shard_at, _ = fold_tile(way, k)
-
-                @pl.when((g > shard_at) if way else (g < shard_at))
+                sends = (g > shard_at) if way else (g < shard_at)
+                if k < EARLY:
+                    sends = sends & (g != way * last)
+
+                @pl.when(sends)
                 def _():
                     fold_copy(way, k, None).wait_send()
 
-    for k in range(3):
+    for k in range(EARLY, EARLY + 3):
         fold_source(k)
+    fold_fetch(1, 0)
     ggain2 = jnp.zeros((8, width), FULL)
     lg_t = []
     for row0 in range(0, seq_len, tile):
@@ -1416,10 +1468,13 @@
         inv = lax.rsqrt(jnp.mean(x * x, axis=1, keepdims=True) + EPS)
         dqkv_ref[rows, :width] = (x * inv * gain1_ref[...][None, :]).astype(LOW)
         if row0 == tile:
-            fold_source(3)
+            fold_source(5)
+            fold_push(1, 0)
+            fold_fetch(1, 1)
         if row0 == 3 * tile:
-            fold_fetch(1, 0)
-            fold_source(4)
+            fold_source(6)
+            fold_push(1, 1)
+            fold_fetch(1, 2)
     ggain2 = jnp.sum(ggain2, axis=0, keepdims=True)
     logit_grad_t = jnp.concatenate(lg_t, axis=1).astype(LOW)
     grouter = dot_nn(logit_grad_t, normed2_ref[...])
@@ -1430,8 +1485,9 @@
         .reshape(experts, width // experts, width)
     )
     pair_send(0)
-    fold_push(1, 0)
-    fold_fetch(1, 1)
+    fold_push(1, 2)
+    fold_fetch(1, 3)
+    fold_fetch(2, 0)
     mgrad_t[...] = jnp.transpose(mgrad_ref[...])
     load(0).wait()
     q_t[...] = jnp.transpose(qkv_ref[:, :width])
@@ -1518,15 +1574,11 @@
         plane_send(c - 1)
         if c >= 2:
             group_send(c - 2)
-        fold_push(1, c)
-        fold_source(c + 4)
-        if c < chunks - 1:
-            fold_fetch(1, c + 1)
-        if c == 2:
-            fold_fetch(2, 0)
-        if c == 3:
-            fold_push(2, 0)
-            fold_fetch(2, 1)
+        fold_push(1, c + 2)
+        fold_push(2, c - 1)
+        fold_source(c + 6)
+        fold_fetch(1, c + 3)
+        fold_fetch(2, c)
 
     load(2).wait()
     ggain1 = jnp.zeros((8, width), FULL)
@@ -1546,12 +1598,9 @@
             plane_send(chunks - 1)
             for mask in (6, 7):
                 result_copy(mask).start()
-            fold_fetch(1, 4)
-            fold_push(2, 1)
+            fold_push(2, 3)
         if row0 == 2 * tile:
-            fold_push(1, 4)
-            fold_fetch(2, 2)
-            fold_source(8)
+            fold_push(1, 6)
     ggain1 = jnp.sum(ggain1, axis=0, keepdims=True)
 
     gtable = exact_nt(onehot_ref[...], diag_ref[...])
@@ -1568,13 +1617,9 @@
     for mask in range(1, experts):
         other = lax.bitwise_xor(me, mask)
         go(remote(small_ref.at[other], small_in.at[mask], small_sems, (mask,), device(mask)))
-    fold_source(9)
-    fold_fetch(1, 5)
-    fold_push(2, 2)
     final_send(0)
     group_send(2)
-    fold_push(1, 5)
-    fold_fetch(2, 3)
+    fold_fetch(1, 7)
     total = small_ref[me]
     for mask in range(1, experts):
         remote(
@@ -1585,19 +1630,14 @@
     for step in range(1, groups):
         where = (lax.rem(g + step, groups), me)
         go(remote(small_plane, small_group.at[step], smallz_sems, (step,), where))
-    fold_fetch(1, 6)
-    fold_push(2, 3)
+    fold_push(1, 7)
     final_send(1)
     group_send(3)
     fold_source(10)
     fold_source(11)
-    fold_push(1, 6)
-    fold_fetch(1, 7)
     own_result.wait()
     for mask in range(1, experts):
         result_copy(mask).wait()
-
-    fold_push(1, 7)
 
     @pl.loop(0, seq_len // tile)
     def _(step):
@@ -1634,7 +1674,7 @@
 
 
 def attn_back(
-    tokens, cot, hidden, normed2, mixed, qkv, prob, recv, token, gain1, gain2, wqkv, wproj, wrouter, table, result, gin, groups
+    tokens, cot, hidden, normed2, mixed, qkv, prob, recv, token, gain1, gain2, wqkv, wproj, wrouter, table, result, gin, early_up, early_down, groups
 ):
     seq_len, width = tokens.shape
     buckets, heads = table.shape
@@ -1656,7 +1696,7 @@
             sds(gin.shape, LOW),
             sds(gin.shape, LOW),
         ),
-        in_specs=[VM] * 5 + [HBM] * 2 + [VM] * 4 + [HBM] + [VM] * 3 + [HBM] * 2,
+        in_specs=[VM] * 5 + [HBM] * 2 + [VM] * 4 + [HBM] + [VM] * 3 + [HBM] * 4,
         out_specs=[VM] * 4 + [HBM] * 3,
         scratch_shapes=[
             pltpu.VMEM((seq_len, width), FULL),
@@ -1722,6 +1762,8 @@
         jnp.asarray(near_onehot(buckets)),
         result,
         gin,
+        early_up,
+        early_down,
     )
     return outs[:5]
 
@@ -1818,7 +1860,7 @@
             pltpu.VMEM(gtok.shape, LOW),
             pltpu.SemaphoreType.DMA((2, 4, 4)),
         ],
-        compiler_params=pltpu.CompilerParams(vmem_limit_bytes=32 * MIB),
+        compiler_params=pltpu.CompilerParams(vmem_limit_bytes=60 * MIB),
     )(block, gtok, gin, gout, dense, small)
 
 
@@ -1870,7 +1912,7 @@
         w_in[0],
         groups,
     )
-    recv, packed_out, grad_inner, grad_out = expert_call(
+    recv, packed_out, grad_inner, grad_out, early_up, early_down = expert_call(
         cot_rows, gate_col, rows, info, resg_t, act, slope, outer_first, w_out[0], w_in[0]
     )
     block_out, gtok, dense, small, grad_in = attn_back(
@@ -1891,6 +1933,8 @@
         bias_table,
         packed_out,
         grad_inner,
+        early_up,
+        early_down,
         groups,
     )
     final = list(

time: 296 us -> 283 us (0.956)
  Pallas kernels: 285 us -> 278 us
  local copies, waits for them, and re-layouts: 5.69 us -> 0 us
    pallas_call x1, Pallas kernels: 106 us -> 97.6 us  [attn_back(): pl.pallas_call(attn_back_kernel, out_shape=(sds((seq_len, width), LOW), s...]
    unnamed x12 -> x0, local copies, waits for them, and re-layouts: 5.69 us -> none
where the time goes in v5:
time: 283 us; the launch traced here: 279 us
  Pallas kernels  278 us (98%)
    pallas_call x1, Pallas kernels, expert_call(): pl.pallas_call(expert_kernel, out_shape=(sds((experts, SLOTS, width + 128...  99.5 us
    pallas_call x1, Pallas kernels, attn_back(): pl.pallas_call(attn_back_kernel, out_shape=(sds((seq_len, width), LOW), s...  97.6 us
    pallas_call x1, Pallas kernels, attn_dispatch(): pl.pallas_call(attn_dispatch_kernel, out_shape=(sds((seq_len, 3 * width),...  73.2 us
    pallas_call x1, Pallas kernels, outputs(): pl.pallas_call(outputs_kernel, out_shape=(sds(block.shape, LOW), sds(gtok...  7.63 us

profile of v5, /device:TPU:8, one launch (start us, length us, event | category | flops | bytes accessed | tf_op | source)
XLA Modules:
  0.0 279.5 jit_solution(3497628774206225183)
XLA Ops:
  1.3 73.2 %shard_map.222 = (bf16[512,2304]{1,0:T(8,128)(2,1)}, bf16[12,512,512]{2,1,0:T(8,128)(2,1)}, bf16[512,768]{1,0:T(8,128)(2,1)}, f32[512,768]{1,0:T(8,128)}, bf16[5...) custom-call(bf16[512,768]{1,0:T(8,128)(2,1)} %tokens_ref.3, ...), custom_call_target="tpu_custom_call" | custom-call | tf_op jit(solution)/shard_map/pallas_call | solution.py:580
  74.5 99.5 %shard_map.223 = (bf16[8,256,896]{2,1,0:T(8,128)(2,1)}, bf16[8,256,768]{2,1,0:T(8,128)(2,1)}, bf16[4,4,192,768]{3,2,1,0:T(8,128)(2,1)}, f32[768,768]{1,0:T(8,128...) custom-call(bf16[1280,768]{1,0:T(8,128)(2,1)} %get-tuple-element.50., ...), custom_call_target="tpu_custom_call" | custom-call | flops 36238786560 | bytes 52428800 | tf_op jit(solution)/shard_map/pallas_call | solution.py:1066
  174.0 97.6 %shard_map.224 = (bf16[512,768]{1,0:T(8,128)(2,1)}, bf16[512,768]{1,0:T(8,128)(2,1)}, bf16[4,96,768]{2,1,0:T(8,128)(2,1)}, f32[16,128]{1,0:T(8,128)}, f32[192,30...) custom-call(bf16[512,768]{1,0:T(8,128)(2,1)} %tokens_ref.3, ...), custom_call_target="tpu_custom_call" | custom-call | flops 30000001024 | bytes 31457280 | tf_op jit(solution)/shard_map/pallas_call | solution.py:1688
  271.6 7.6 %shard_map.225 = (bf16[512,768]{1,0:T(8,128)(2,1)}, bf16[512,768]{1,0:T(8,128)(2,1)}, f32[1,96]{1,0:T(1,128)}, f32[96,2304]{1,0:T(8,128)}, f32[96,768]{1,0:T(8,1...) custom-call(bf16[512,768]{1,0:T(8,128)(2,1)} %get-tuple-element.64.b, ...), custom_call_target="tpu_custom_call" | custom-call | tf_op jit(solution)/shard_map/pallas_call | solution.py:1840

commit v6 on v5

--- a/solution.py
+++ b/solution.py
@@ -663,9 +663,9 @@
 
 
 def expert_kernel(
-    cot_ref,
-    gate_ref,
-    rows_ref,
+    cot_hbm,
+    gate_hbm,
+    rows_hbm,
     info_ref,
     resgt_hbm,
     act_ref,
@@ -681,6 +681,9 @@
     early_down,
     up_in,
     down_in,
+    cot_ref,
+    gate_ref,
+    rows_ref,
     act_v,
     slope_v,
     wout_v,
@@ -726,7 +729,14 @@
         return (g, lax.bitwise_xor(me, mask))
 
     def load(index):
-        src, dst = ((wout_ref, wout_v), (win_ref, win_v), (resgt_hbm, turned))[index]
+        src, dst = (
+            (wout_ref, wout_v),
+            (win_ref, win_v),
+            (resgt_hbm, turned),
+            (cot_hbm, cot_ref),
+            (gate_hbm, gate_ref),
+            (rows_hbm, rows_ref),
+        )[index]
         return pltpu.make_async_copy(src, dst, load_sem.at[index])
 
     def act_load(tile):
@@ -741,12 +751,15 @@
 
     for tile in range(groups):
         outer_load(tile).start()
+    load(3).start()
+    load(4).start()
     load(0).start()
     slope_load(0).start()
     act_load(0).start()
     load(1).start()
     for tile in range(1, groups):
         act_load(tile).start()
+    load(5).start()
     load(2).start()
     barrier = pltpu.get_barrier_semaphore()
     for mask in range(1, experts):
@@ -866,7 +879,7 @@
     fold_source(*range(last))
     acc_ref[...] = jnp.zeros_like(acc_ref)
     gg_ref[...] = jnp.zeros_like(gg_ref)
-    for index in range(2):
+    for index in (0, 1, 3, 4, 5):
         load(index).wait()
 
     def span(tile):
@@ -1075,9 +1088,12 @@
             arrival,
             arrival,
         ),
-        in_specs=[VM] * 4 + [HBM] * 6,
+        in_specs=[HBM] * 3 + [VM] + [HBM] * 6,
         out_specs=[HBM] * 8,
         scratch_shapes=[
+            pltpu.VMEM(cot_rows.shape, LOW),
+            pltpu.VMEM(gate_col.shape, FULL),
+            pltpu.VMEM(rows.shape, LOW),
             pltpu.VMEM((tiles, capacity, tile_width), LOW),
             pltpu.VMEM((2, capacity, tile_width), LOW),
             pltpu.VMEM(w_out.shape, LOW),
@@ -1095,7 +1111,7 @@
             pltpu.VMEM((width, tile_width), FULL),
             pltpu.VMEM((experts, SLOTS, width), LOW),
             pltpu.VMEM((ff // groups, width), FULL),
-            dma((3,)),
+            dma((6,)),
             dma((groups,)),
             dma((2,)),
             dma((groups,)),
@@ -1119,19 +1135,19 @@
 
 
 def attn_back_kernel(
-    tokens_ref,
-    cot_ref,
-    hidden_ref,
-    normed2_ref,
-    mixed_ref,
+    tokens_hbm,
+    cot_hbm,
+    hidden_hbm,
+    normed2_hbm,
+    mixed_hbm,
     qkv_hbm,
     prob_hbm,
-    recv_ref,
+    recv_hbm,
     token_ref,
     gain1_ref,
     gain2_ref,
     wqkv_hbm,
-    wproj_ref,
+    wproj_hbm,
     wrouter_ref,
     onehot_ref,
     result_ref,
@@ -1145,6 +1161,13 @@
     gin_out,
     up_in,
     down_in,
+    tokens_ref,
+    cot_ref,
+    hidden_ref,
+    normed2_ref,
+    mixed_ref,
+    recv_ref,
+    wproj_ref,
     hgrad_ref,
     mgrad_ref,
     mgrad_t,
@@ -1184,7 +1207,7 @@
     small_sems,
     smallz_sems,
 ):
-    seq_len, width = tokens_ref.shape
+    seq_len, width = tokens_hbm.shape
     experts = wrouter_ref.shape[0]
     chunks = part_ref.shape[0]
     groups = group_in.shape[1]
@@ -1199,11 +1222,23 @@
         return (g, lax.bitwise_xor(me, mask))
 
     def load(index):
-        src, dst = ((qkv_hbm, qkv_ref), (prob_hbm, prob_ref), (wqkv_hbm, wqkv_ref))[index]
+        src, dst = (
+            (qkv_hbm, qkv_ref),
+            (prob_hbm, prob_ref),
+            (wqkv_hbm, wqkv_ref),
+            None,
+            (recv_hbm, recv_ref),
+            (hidden_hbm, hidden_ref),
+            (cot_hbm, cot_ref),
+            (tokens_hbm, tokens_ref),
+            (wproj_hbm, wproj_ref),
+            (normed2_hbm, normed2_ref),
+            (mixed_hbm, mixed_ref),
+        )[index]
         return pltpu.make_async_copy(src, dst, load_sems.at[index])
 
     own_result = pltpu.make_async_copy(result_ref.at[me], back_ref.at[me], load_sems.at[3])
-    for index in range(3):
+    for index in (4, 5, 6, 7, 8, 9, 10, 0, 1, 2):
         load(index).start()
     own_result.start()
     barrier = pltpu.get_barrier_semaphore()
@@ -1433,6 +1468,8 @@
     for k in range(EARLY, EARLY + 3):
         fold_source(k)
     fold_fetch(1, 0)
+    for index in range(4, 11):
+        load(index).wait()
     ggain2 = jnp.zeros((8, width), FULL)
     lg_t = []
     for row0 in range(0, seq_len, tile):
@@ -1696,9 +1733,16 @@
             sds(gin.shape, LOW),
             sds(gin.shape, LOW),
         ),
-        in_specs=[VM] * 5 + [HBM] * 2 + [VM] * 4 + [HBM] + [VM] * 3 + [HBM] * 4,
+        in_specs=[HBM] * 8 + [VM] * 3 + [HBM] * 2 + [VM] * 2 + [HBM] * 4,
         out_specs=[VM] * 4 + [HBM] * 3,
         scratch_shapes=[
+            pltpu.VMEM(tokens.shape, LOW),
+            pltpu.VMEM(cot.shape, LOW),
+            pltpu.VMEM(hidden.shape, FULL),
+            pltpu.VMEM(normed2.shape, LOW),
+            pltpu.VMEM(mixed.shape, LOW),
+            pltpu.VMEM(recv.shape, LOW),
+            pltpu.VMEM(wproj.shape, LOW),
             pltpu.VMEM((seq_len, width), FULL),
             pltpu.VMEM((seq_len, width), LOW),
             pltpu.VMEM((width, seq_len), LOW),
@@ -1729,7 +1773,7 @@
             dma((2, 2, (groups - 1) * gin.shape[1])),
             dma((2, 2)),
             dma((2,)),
-            dma((4,)),
+            dma((11,)),
             dma((2, experts)),
             dma((2, chunks, chips)),
             dma((2, chunks, chips - 1)),

time: 283 us -> 280 us (0.989)
  Pallas kernels: 278 us -> 274 us
    pallas_call x1, Pallas kernels: 97.6 us -> 94.4 us  [attn_back(): pl.pallas_call(attn_back_kernel, out_shape=(sds((seq_len, width), LOW), s...]
where the time goes in v6:
time: 280 us; the launch traced here: 276 us
  Pallas kernels  274 us (98%)
    pallas_call x1, Pallas kernels, expert_call(): pl.pallas_call(expert_kernel, out_shape=(sds((experts, SLOTS, width + 128...  99.2 us
    pallas_call x1, Pallas kernels, attn_back(): pl.pallas_call(attn_back_kernel, out_shape=(sds((seq_len, width), LOW), s...  94.4 us
    pallas_call x1, Pallas kernels, attn_dispatch(): pl.pallas_call(attn_dispatch_kernel, out_shape=(sds((seq_len, 3 * width),...  73.2 us
    pallas_call x1, Pallas kernels, outputs(): pl.pallas_call(outputs_kernel, out_shape=(sds(block.shape, LOW), sds(gtok...  7.63 us

profile of v6, /device:TPU:8, one launch (start us, length us, event | category | flops | bytes accessed | tf_op | source)
XLA Modules:
  0.0 275.9 jit_solution(4145181588499459027)
XLA Ops:
  1.3 73.2 %shard_map.222 = (bf16[512,2304]{1,0:T(8,128)(2,1)}, bf16[12,512,512]{2,1,0:T(8,128)(2,1)}, bf16[512,768]{1,0:T(8,128)(2,1)}, f32[512,768]{1,0:T(8,128)}, bf16[5...) custom-call(bf16[512,768]{1,0:T(8,128)(2,1)} %tokens_hbm.1, ...), custom_call_target="tpu_custom_call" | custom-call | tf_op jit(solution)/shard_map/pallas_call | solution.py:580
  74.5 99.2 %shard_map.223 = (bf16[8,256,896]{2,1,0:T(8,128)(2,1)}, bf16[8,256,768]{2,1,0:T(8,128)(2,1)}, bf16[4,4,192,768]{3,2,1,0:T(8,128)(2,1)}, f32[768,768]{1,0:T(8,128...) custom-call(bf16[1280,768]{1,0:T(8,128)(2,1)} %get-tuple-element.50., ...), custom_call_target="tpu_custom_call" | custom-call | flops 36238786560 | bytes 52428800 | tf_op jit(solution)/shard_map/pallas_call | solution.py:1079
  173.7 94.4 %shard_map.224 = (bf16[512,768]{1,0:T(8,128)(2,1)}, bf16[512,768]{1,0:T(8,128)(2,1)}, bf16[4,96,768]{2,1,0:T(8,128)(2,1)}, f32[16,128]{1,0:T(8,128)}, f32[192,30...) custom-call(bf16[512,768]{1,0:T(8,128)(2,1)} %tokens_hbm.1, ...), custom_call_target="tpu_custom_call" | custom-call | flops 30000001024 | bytes 31457280 | tf_op jit(solution)/shard_map/pallas_call | solution.py:1725
  268.1 7.6 %shard_map.225 = (bf16[512,768]{1,0:T(8,128)(2,1)}, bf16[512,768]{1,0:T(8,128)(2,1)}, f32[1,96]{1,0:T(1,128)}, f32[96,2304]{1,0:T(8,128)}, f32[96,768]{1,0:T(8,1...) custom-call(bf16[512,768]{1,0:T(8,128)(2,1)} %get-tuple-element.64.b, ...), custom_call_target="tpu_custom_call" | custom-call | tf_op jit(solution)/shard_map/pallas_call | solution.py:1884
